TPU v7x, 128 devices: a whole 4x4x4 slice. The times are simulated.
128 devices in a mesh: band: 4 (over z), region: 32 (over y, x, core).
Axes of the slice: x: 4, y: 4, z: 4, core: 2. Of those that a mesh axis runs over, the one named last changes fastest.
Arguments:
- grid_latent: bfloat16 [131072, 512], P(('band', 'region')), may hold values from -6 to 6
- mesh_latent: bfloat16 [8192, 512], P('region'), may hold values from -6 to 6
- encode_sender: int32 [819200], P(('band', 'region')), may hold values from 0 to 1023
- encode_receiver: int32 [819200], P(('band', 'region')), may hold values from 0 to 255
- encode_live: int32 [128, 35], P(('band', 'region')), may hold values from 1 to 2048, as said below
- encode_feature: float32 [4, 819200], P(None, ('band', 'region')), may hold values from -6 to 6
- mesh_edge: bfloat16 [253952, 512], P(('band', 'region')), may hold values from -6 to 6
- mesh_sender: int32 [253952], P(('band', 'region')), may hold values from 0 to 255
- mesh_receiver: int32 [253952], P(('band', 'region')), may hold values from 0 to 255
- mesh_live: int32 [128, 35], P(('band', 'region')), may hold values from 1 to 576, as said below
- grid_first: bfloat16 [512, 512], replicated, may hold values from -0.25 to 0.25
- grid_second: bfloat16 [512, 512], replicated, may hold values from -0.25 to 0.25
- grid_gain: float32 [512], replicated, may hold values from 0.5 to 1.5
- encode_send: bfloat16 [512, 512], replicated, may hold values from -0.25 to 0.25
- encode_receive: bfloat16 [512, 512], replicated, may hold values from -0.25 to 0.25
- encode_geometry: float32 [4, 512], replicated, may hold values from -3 to 3
- encode_output: bfloat16 [512, 512], replicated, may hold values from -0.25 to 0.25
- encode_gain: float32 [512], replicated, may hold values from 0.5 to 1.5
- node_first: bfloat16 [1024, 512], replicated, may hold values from -0.1875 to 0.1875
- node_second: bfloat16 [512, 512], replicated, may hold values from -0.25 to 0.25
- node_gain: float32 [512], replicated, may hold values from 0.5 to 1.5
- process_edge: bfloat16 [512, 512], replicated, may hold values from -0.25 to 0.25
- process_send: bfloat16 [512, 512], replicated, may hold values from -0.25 to 0.25
- process_receive: bfloat16 [512, 512], replicated, may hold values from -0.25 to 0.25
- process_output: bfloat16 [512, 512], replicated, may hold values from -0.25 to 0.25
- process_gain: float32 [512], replicated, may hold values from 0.5 to 1.5
- update_first: bfloat16 [1024, 512], replicated, may hold values from -0.1875 to 0.1875
- update_second: bfloat16 [512, 512], replicated, may hold values from -0.25 to 0.25
- update_gain: float32 [512], replicated, may hold values from 0.5 to 1.5
Outputs:
- grid_out: bfloat16 [131072, 512], P(('band', 'region'))
- mesh_out: bfloat16 [8192, 512], P('region')
- edge_out: bfloat16 [253952, 512], P(('band', 'region'))
Inputs may be any that keep to these rules, and one draw needn't show every extreme that they name: `encode_live`: live encoder edges of each block: columns 0 to 2 count slots of blocks of 2048, the others of blocks of 8; slots past the count are padding. Every draw has a device whose blocks are all full. `mesh_live`: live processor edges of each block: columns 0 to 2 count slots of blocks of 576, the others of blocks of 8; slots past the count are padding. Every draw has a device whose blocks are all full.
All inputs are finite; a program needn't handle non-finite values.
Results may differ from a plain program's by a relative error of at most 0.014.
Values may be sent and summed in bfloat16 or wider, within the bound.
No kernel may reach another device: no remote copies, remote signals or barrier semaphores. Data moves between devices by JAX's collectives and lax.ppermute only.
A program may use at most 128 MiB of HBM per device.

v0:
```python
import jax
import jax.numpy as jnp
from jax import lax
from jax.sharding import PartitionSpec as P

NEAR_G = 2048
FAR_G = 8
NEAR_M = 576
FAR_M = 8


EPSILON = 1e-05


def with_halo(x, sides, width):
    for axis, dim in sides:
        count, length = (lax.axis_size(axis), x.shape[dim])
        up = [(i, (i + 1) % count) for i in range(count)]
        down = [(j, i) for i, j in up]
        last = lax.slice_in_dim(x, length - width, length, axis=dim)
        leading = lax.slice_in_dim(x, 0, width, axis=dim)
        before = lax.ppermute(last, axis, up)
        after = lax.ppermute(leading, axis, down)
        x = jnp.concatenate([before, x, after], axis=dim)
    return x


def layer_norm(values):
    center = values - jnp.mean(values, axis=-1, keepdims=True)
    spread = jnp.mean(center * center, axis=-1, keepdims=True)
    return center * lax.rsqrt(spread + EPSILON)


def edge_message(preact, w_output, gain_row, live_mask):
    hidden = jax.nn.silu(preact).astype(jnp.bfloat16)
    message = (
        layer_norm(jnp.dot(hidden, w_output, preferred_element_type=jnp.float32)) * gain_row
    ).astype(jnp.bfloat16)
    return jnp.where(live_mask[:, None], message, jnp.zeros_like(message))


def node_update(latent, summed, w_first, w_second, gain_row):
    latent_width = latent.shape[1]
    merged = jnp.dot(latent, w_first[:latent_width], preferred_element_type=jnp.float32)
    merged = merged + jnp.dot(
        summed.astype(jnp.bfloat16), w_first[latent_width:], preferred_element_type=jnp.float32
    )
    hidden = jax.nn.silu(merged).astype(jnp.bfloat16)
    update = layer_norm(jnp.dot(hidden, w_second, preferred_element_type=jnp.float32)) * gain_row
    return (latent.astype(jnp.float32) + update).astype(jnp.bfloat16)


def receiver_sums(message, targets, node_count):
    one_hot = (jnp.arange(node_count, dtype=jnp.int32)[:, None] == targets[None, :]).astype(
        jnp.bfloat16
    )
    return jnp.dot(one_hot, message, preferred_element_type=jnp.float32)


def live_slots(live_row, near_cap, far_cap):
    near_mask = (jnp.arange(near_cap, dtype=jnp.int32)[None, :] < live_row[:3, None]).reshape(-1)
    far_mask = (jnp.arange(far_cap, dtype=jnp.int32)[None, :] < live_row[3:, None]).reshape(-1)
    return jnp.concatenate([near_mask, far_mask])


def on_device(
    grid_latent,
    mesh_latent,
    encode_sender,
    encode_receiver,
    encode_live,
    encode_feature,
    mesh_edge,
    mesh_sender,
    mesh_receiver,
    mesh_live,
    grid_first,
    grid_second,
    grid_gain,
    encode_send,
    encode_receive,
    encode_geometry,
    encode_output,
    encode_gain,
    node_first,
    node_second,
    node_gain,
    process_edge,
    process_send,
    process_receive,
    process_output,
    process_gain,
    update_first,
    update_second,
    update_gain,
):
    regions = lax.axis_size("region")
    latent_width = grid_latent.shape[1]
    grid_count = grid_latent.shape[0]
    node_count = mesh_latent.shape[0]
    near_grid = 3 * NEAR_G
    near_mesh = 3 * NEAR_M
    grid_asks = encode_sender[near_grid:].reshape(regions, FAR_G)
    mesh_asks = mesh_sender[near_mesh:].reshape(regions, FAR_M)
    asked_grid, asked_mesh = (
        lax.all_to_all(grid_asks, "region", split_axis=0, concat_axis=0, tiled=True),
        lax.all_to_all(mesh_asks, "region", split_axis=0, concat_axis=0, tiled=True),
    )
    outgoing = jnp.take(grid_latent, asked_grid.reshape(-1), axis=0).reshape(
        regions, FAR_G, latent_width
    )
    far_rows = lax.all_to_all(outgoing, "region", split_axis=0, concat_axis=0, tiled=True).reshape(
        regions * FAR_G, latent_width
    )
    grid_sectors = with_halo(grid_latent, (("region", 0),), grid_count)
    grid_hidden = jax.nn.silu(
        jnp.dot(grid_latent, grid_first, preferred_element_type=jnp.float32)
    ).astype(jnp.bfloat16)
    grid_update = (
        layer_norm(jnp.dot(grid_hidden, grid_second, preferred_element_type=jnp.float32))
        * grid_gain
    )
    grid_out = (grid_latent.astype(jnp.float32) + grid_update).astype(jnp.bfloat16)
    near_index = (
        jnp.arange(near_grid, dtype=jnp.int32) // NEAR_G * grid_count + encode_sender[:near_grid]
    )
    near_rows = jnp.take(grid_sectors, near_index, axis=0)
    sender_rows = jnp.concatenate([near_rows, far_rows], axis=0)
    receive_term = jnp.dot(mesh_latent, encode_receive, preferred_element_type=jnp.float32)
    preact = jnp.dot(sender_rows, encode_send, preferred_element_type=jnp.float32)
    preact = preact + jnp.take(receive_term, encode_receiver, axis=0)
    preact = preact + jnp.einsum(
        "ke,kh->eh", encode_feature, encode_geometry, precision=lax.Precision.HIGHEST
    )
    message = edge_message(
        preact, encode_output, encode_gain, live_slots(encode_live[0], NEAR_G, FAR_G)
    )
    partial_value = receiver_sums(message, encode_receiver, node_count)
    encode_sum = lax.psum(partial_value, "band")
    mesh_mid = node_update(mesh_latent, encode_sum, node_first, node_second, node_gain)
    outgoing_mesh = jnp.take(mesh_mid, asked_mesh.reshape(-1), axis=0).reshape(
        regions, FAR_M, latent_width
    )
    far_mesh = lax.all_to_all(
        outgoing_mesh, "region", split_axis=0, concat_axis=0, tiled=True
    ).reshape(regions * FAR_M, latent_width)
    mesh_sectors = with_halo(mesh_mid, (("region", 0),), node_count)
    near_mesh_index = (
        jnp.arange(near_mesh, dtype=jnp.int32) // NEAR_M * node_count + mesh_sender[:near_mesh]
    )
    near_mesh_rows = jnp.take(mesh_sectors, near_mesh_index, axis=0)
    mesh_rows = jnp.concatenate([near_mesh_rows, far_mesh], axis=0)
    process_term = jnp.dot(mesh_mid, process_receive, preferred_element_type=jnp.float32)
    process_pre = jnp.dot(mesh_edge, process_edge, preferred_element_type=jnp.float32)
    process_pre = process_pre + jnp.dot(mesh_rows, process_send, preferred_element_type=jnp.float32)
    process_pre = process_pre + jnp.take(process_term, mesh_receiver, axis=0)
    process_message = edge_message(
        process_pre, process_output, process_gain, live_slots(mesh_live[0], NEAR_M, FAR_M)
    )
    edge_out = (mesh_edge.astype(jnp.float32) + process_message.astype(jnp.float32)).astype(
        jnp.bfloat16
    )
    process_partial = receiver_sums(process_message, mesh_receiver, node_count)
    process_sum = lax.psum(process_partial.astype(jnp.bfloat16), "band").astype(jnp.float32)
    mesh_out = node_update(mesh_mid, process_sum, update_first, update_second, update_gain)
    return (grid_out, mesh_out, edge_out)


def solution(mesh):
    return jax.shard_map(
        on_device,
        mesh=mesh,
        in_specs=(
            P(("band", "region"), None),
            P("region", None),
            P(("band", "region")),
            P(("band", "region")),
            P(("band", "region"), None),
            P(None, ("band", "region")),
            P(("band", "region"), None),
            P(("band", "region")),
            P(("band", "region")),
            P(("band", "region"), None),
            P(),
            P(),
            P(),
            P(),
            P(),
            P(),
            P(),
            P(),
            P(),
            P(),
            P(),
            P(),
            P(),
            P(),
            P(),
            P(),
            P(),
            P(),
            P(),
        ),
        out_specs=(P(("band", "region"), None), P("region", None), P(("band", "region"), None)),
        check_vma=False,
    )
```

profile of v0, /device:TPU:0, one launch (start us, length us, event | category | flops | bytes accessed | tf_op | source)
XLA Modules:
  0.0 282.8 jit_solution(11943072679001892880)
XLA Ops:
  7.3 5.1 %collective-permute-start.1 = (bf16[1024,512]{1,0:T(8,128)(2,1)}, bf16[1024,512]{1,0:T(8,128)(2,1)}, u32[]{:S(2)}, u32[]{:S(2)}) collective-permute-start(bf16[1024,512]{1,0:T(8,128)(2,1)} %param.29), channel_id=1, source_target_pairs={{1,0},{2,1},{3,2},{4,3},{5,4},{6,5},{7,6},{8,7},{9,8},{10,9},{11,1... | collective-permute-start | bytes 3145736 | tf_op jit(solution)/shard_map/ppermute | solution.py:23
  13.7 4.1 %all-to-all-start = ((s32[32,1,8]{2,1,0:T(1,128)}), s32[32,1,8]{2,1,0:T(1,128)S(1)}, u32[]{:S(2)}, u32[]{:S(2)}) async-start(s32[32,1,8]{2,1,0:T(1,128)} %bitcast.2), calls=%async_computation | async-start | bytes 32768 | tf_op jit(solution)/shard_map/all_to_all | solution.py:106
  30.0 4.4 %fusion.55 = (f32[1024]{0:T(1024)S(1)}, f32[1024,512]{0,1:T(8,128)}) fusion(bf16[512,512]{1,0:T(8,128)(2,1)} %param.40, bf16[1024,512]{1,0:T(8,128)(2,1)} %param.29, bf16[512,512]{1,0:T(8,128)(2,1)} %param.39), kind=kOutput, calls=%fused_computation.127 | convolution fusion | flops 1076886528 | bytes 4198400 | tf_op jit(solution)/shard_map/dot_general | solution.py:120
  36.3 4.9 %fusion.69 = f32[1984,512]{1,0:T(8,128)} fusion(bf16[1984,512]{1,0:T(8,128)(2,1)} %param.35, bf16[512,512]{1,0:T(8,128)(2,1)} %param.50), kind=kOutput, calls=%fused_computation.134 | convolution fusion | flops 1040187392 | bytes 6619136 | tf_op jit(solution)/shard_map/dot_general | solution.py:154
  44.0 17.3 %gather_fusion.2 = f32[6400,512]{1,0:T(8,128)} fusion(f32[256,512]{1,0:T(8,128)S(1)} %fusion.68, s32[7168]{0:T(1024)S(1)} %pad_clamp_fusion), kind=kCustom, calls=%fused_computation.2 | custom fusion | bytes 26240000 | tf_op jit(solution)/shard_map/jit(_take)/gather | solution.py:131
  61.3 7.4 %all-to-all-start.2 = ((s32[32,1,8]{2,1,0:T(1,128)}), s32[32,1,8]{2,1,0:T(1,128)S(1)}, u32[]{:S(2)}, u32[]{:S(2)}) async-start(s32[32,1,8]{2,1,0:T(1,128)} %bitcast.9), calls=%async_computation.2 | async-start | bytes 32768 | tf_op jit(solution)/shard_map/all_to_all | solution.py:107
  71.9 4.1 %all-to-all-done.2 = s32[32,1,8]{2,1,0:T(1,128)S(1)} async-done(((s32[32,1,8]{2,1,0:T(1,128)}), s32[32,1,8]{2,1,0:T(1,128)S(1)}, u32[]{:S(2)}, u32[]{:S(2)}) %all-to-all-start.2) | async-done | bytes 1056 | tf_op jit(solution)/shard_map/all_to_all | solution.py:107
  76.0 4.1 %all-to-all-start.1 = ((bf16[32,8,512]{2,1,0:T(8,128)(2,1)}), bf16[32,8,512]{2,1,0:T(8,128)(2,1)S(1)}, u32[]{:S(2)}, u32[]{:S(2)}) async-start(bf16[32,8,512]{2,1,0:T(8,128)(2,1)} %bitcast_select_fusion.1), calls=%async_computation.1 | async-start | bytes 524288 | tf_op jit(solution)/shard_map/all_to_all | solution.py:112
  80.8 2.8 %pad_maximum_fusion = bf16[3072,512]{1,0:T(8,128)(2,1)} fusion(bf16[1024,512]{1,0:T(8,128)(2,1)} %collective-permute-done.1, bf16[1024,512]{1,0:T(8,128)(2,1)S(1)} %copy-done.1, bf16[1024,512]{1,0:T(8,128)(2,1)S(1)} %collective-permute-done), kind=kLoop, calls=%fused_computation.24 | loop fusion | flops 9437184 | bytes 6291456 | tf_op jit(solution)/shard_map/concatenate | solution.py:24
  83.7 27.9 %gather_fusion = bf16[6144,512]{1,0:T(8,128)(2,1)} fusion(bf16[3072,512]{1,0:T(8,128)(2,1)} %pad_maximum_fusion, s32[6144]{0:T(1024)S(1)} %broadcast_clamp_fusion), kind=kCustom, calls=%fused_computation | custom fusion | bytes 12607488 | tf_op jit(solution)/shard_map/jit(_take)/gather | solution.py:127
  111.6 6.8 %broadcast_select_fusion = bf16[6144,512]{1,0:T(8,128)(2,1)} fusion(bf16[6144,512]{1,0:T(8,128)(2,1)} %gather_fusion, pred[6144]{0:T(1024)(128)(4,1)S(1)} %compare_and_fusion.1), kind=kLoop, calls=%fused_computation.17 | loop fusion | flops 3145728 | bytes 12589056 | tf_op jit(solution)/shard_map/jit(_take)/select_n | solution.py:127
  118.4 11.1 %fusion.1 = f32[6400,512]{1,0:T(8,128)} fusion(bf16[512,512]{1,0:T(8,128)(2,1)S(1)} %copy-done.14, bf16[256,512]{1,0:T(8,128)(2,1)S(1)} %bitcast.43, bf16[6144,512]{1,0:T(8,128)(2,1)} %broadcast_select_fusion), kind=kOutput, calls=%fused_computation.10 | convolution fusion | flops 3368550400 | bytes 20185088 | tf_op jit(solution)/shard_map/dot_general | solution.py:130
  129.6 20.6 %multiply_convert_fusion.1 = bf16[6400,512]{1,0:T(8,128)(2,1)} fusion(f32[6400,512]{1,0:T(8,128)} %fusion.1, f32[6400,512]{1,0:T(8,128)} %gather_fusion.2, f32[4,6400]{1,0:T(4,128)S(1)} %copy-done.16, f32[4,512]{1,0:T(4,128)S(1)} %copy-done.17, pred[6400]{0:T(1024)(128)(4,1)S(1)} %compare_and_fusion), kind=kOutput, calls=%fused_computation.8 | convolution fusion | flops 183500800 | bytes 32884992 | tf_op jit(solution)/shard_map/ke,kh->eh/dot_general | solution.py:132
  150.2 6.3 %fusion.56 = (f32[6400]{0:T(1024)S(1)}, f32[6400,512]{0,1:T(8,128)S(1)}) fusion(bf16[6400,512]{1,0:T(8,128)(2,1)} %multiply_convert_fusion.1, bf16[512,512]{1,0:T(8,128)(2,1)S(1)} %copy-done), kind=kOutput, calls=%fused_computation.128 | convolution fusion | flops 3358713600 | bytes 20210688 | tf_op jit(solution)/shard_map/dot_general | solution.py:37
  157.9 2.9 %fusion.5 = f32[256,512]{1,0:T(8,128)S(1)} fusion(f32[6400,512]{0,1:T(8,128)S(1)} %get-tuple-element.19, f32[512]{0:T(512)S(1)} %copy-done.18, f32[6400]{0:T(1024)S(1)} %add_rsqrt_fusion, f32[6400]{0:T(1024)S(1)} %broadcast_multiply_fusion, pred[6400]{0:T(1024)(128)(4,1)S(1)} %pad_add_fusion, s32[6400]{0:T(1024)S(1)} %copy-done.8), kind=kOutput, calls=%fused_computation.15 | convolution fusion | flops 1695744000 | bytes 13716736 | tf_op jit(solution)/shard_map/dot_general | solution.py:57
  160.8 24.3 %all-reduce.4 = bf16[256,512]{1,0:T(8,128)(2,1)S(1)} all-reduce(f32[256,512]{1,0:T(8,128)S(1)} %fusion.5), channel_id=1, replica_groups=mesh['band'=4,'region'=32] {'band'}, use_global_device_ids=true, to_apply=%region_4.5 | all-reduce | flops 131072 | bytes 786432 | tf_op jit(solution)/shard_map/psum | solution.py:139
  187.4 5.1 %collective-permute-start.3 = (bf16[256,512]{1,0:T(8,128)(2,1)S(1)}, bf16[256,512]{1,0:T(8,128)(2,1)S(1)}, u32[]{:S(2)}, u32[]{:S(2)}) collective-permute-start(bf16[256,512]{1,0:T(8,128)(2,1)S(1)} %add_convert_fusion.3), channel_id=1, source_target_pairs={{1,0},{2,1},{3,2},{4,3},{5,4},{6,5},{7,6},{8,7},{9,8},{10,9},{11,1... | collective-permute-start | bytes 786440 | tf_op jit(solution)/shard_map/ppermute | solution.py:23
  194.4 4.6 %all-to-all-start.3 = ((bf16[32,8,512]{2,1,0:T(8,128)(2,1)}), bf16[32,8,512]{2,1,0:T(8,128)(2,1)}, u32[]{:S(2)}, u32[]{:S(2)}) async-start(bf16[32,8,512]{2,1,0:T(8,128)(2,1)} %bitcast_select_fusion), calls=%async_computation.3 | async-start | bytes 524288 | tf_op jit(solution)/shard_map/all_to_all | solution.py:144
  199.3 9.1 %gather_fusion.5 = f32[1984,512]{1,0:T(8,128)} fusion(f32[256,512]{1,0:T(8,128)S(1)} %fusion.70, s32[2048]{0:T(1024)S(1)} %pad_clamp_fusion.1), kind=kCustom, calls=%fused_computation.5 | custom fusion | bytes 8134400 | tf_op jit(solution)/shard_map/jit(_take)/gather | solution.py:156
  208.5 5.7 %gather_fusion.3 = bf16[1728,512]{1,0:T(8,128)(2,1)S(1)} fusion(bf16[768,512]{1,0:T(8,128)(2,1)S(1)} %pad_maximum_fusion.1, s32[2048]{0:T(1024)S(1)} %pad_clamp_fusion.2), kind=kCustom, calls=%fused_computation.3 | custom fusion | bytes 3545856 | tf_op jit(solution)/shard_map/jit(_take)/gather | solution.py:151
  215.8 7.6 %fusion.60 = (f32[1984]{0:T(1024)S(1)}, f32[1984,512]{1,0:T(8,128)}) fusion(bf16[512,512]{1,0:T(8,128)(2,1)} %param.53, f32[1984,512]{1,0:T(8,128)} %gather_fusion.5, f32[1984,512]{1,0:T(8,128)} %fusion.69, bf16[512,512]{1,0:T(8,128)(2,1)} %param.51, bf16[256,512]{1,0:T(8,128)(2,1)} %bitcast.13, bf16[1728,512]{1,0:T(8,128)(2,1)} %broadcast_select_fusion.1, ...), kind=kOutput, calls=%fused_computation.130 | convolution fusion | flops 2093578240 | bytes 15279808 | tf_op jit(solution)/shard_map/dot_general | solution.py:37
  223.4 3.0 %multiply_reduce_fusion.1 = f32[1984]{0:T(1024)S(1)} fusion(f32[1984,512]{1,0:T(8,128)} %get-tuple-element.23, f32[1984]{0:T(1024)S(1)} %broadcast_multiply_fusion.1), kind=kLoop, calls=%fused_computation.20 | loop fusion | flops 3045440 | bytes 4079104 | tf_op jit(solution)/shard_map/reduce_sum | solution.py:30
  226.8 2.8 %add_convert_fusion = (bf16[1984,512]{1,0:T(8,128)(2,1)}, bf16[1984,512]{1,0:T(8,128)(2,1)S(1)}) fusion(bf16[1984,512]{1,0:T(8,128)(2,1)S(1)} %copy-done.3, f32[512]{0:T(512)S(1)} %copy-done.11, f32[1984]{0:T(1024)S(1)} %add_rsqrt_fusion.1, f32[1984,512]{1,0:T(8,128)S(1)} %copy-done.2, f32[1984]{0:T(1024)S(1)} %broadcast_multiply_fusion.1, ...), kind=kLoop, calls=%fused_computation.18 | loop fusion | flops 9142272 | bytes 10177984 | tf_op jit(solution)/shard_map/convert_element_type | solution.py:160
  237.5 35.5 %all-reduce.3.cloned.1.call-done = bf16[256,512]{1,0:T(8,128)(2,1)} async-done(((bf16[256,512]{1,0:T(8,128)(2,1)}), bf16[256,512]{1,0:T(8,128)(2,1)}) %all-reduce.3.cloned.1.call-update) | async-done | bytes 262160 | tf_op jit(solution)/shard_map/psum | solution.py:164
  (120 shorter events, 40.9 us)
Async XLA Ops:
  7.2 143.0 %copy-start = (bf16[512,512]{1,0:T(8,128)(2,1)S(1)}, bf16[512,512]{1,0:T(8,128)(2,1)}, u32[]{:S(2)}) copy-start(bf16[512,512]{1,0:T(8,128)(2,1)} %param.45) | copy-start | bytes 1572868
  7.2 73.6 %collective-permute-start = (bf16[1024,512]{1,0:T(8,128)(2,1)}, bf16[1024,512]{1,0:T(8,128)(2,1)S(1)}, u32[]{:S(2)}, u32[]{:S(2)}) collective-permute-start(bf16[1024,512]{1,0:T(8,128)(2,1)} %param.29), channel_id=1, source_target_pairs={{0,1},{1,2},{2,3},{3,4},{4,5},{5,6},{6,7},{7,8},{8,9},{9,10},{10,1... | collective-permute-start | bytes 3145736 | tf_op jit(solution)/shard_map/ppermute | solution.py:22
  7.3 73.6 %collective-permute-start.1 = (bf16[1024,512]{1,0:T(8,128)(2,1)}, bf16[1024,512]{1,0:T(8,128)(2,1)}, u32[]{:S(2)}, u32[]{:S(2)}) collective-permute-start(bf16[1024,512]{1,0:T(8,128)(2,1)} %param.29), channel_id=1, source_target_pairs={{1,0},{2,1},{3,2},{4,3},{5,4},{6,5},{7,6},{8,7},{9,8},{10,9},{11,1... | collective-permute-start | bytes 3145736 | tf_op jit(solution)/shard_map/ppermute | solution.py:23
  13.7 47.6 %all-to-all-start = ((s32[32,1,8]{2,1,0:T(1,128)}), s32[32,1,8]{2,1,0:T(1,128)S(1)}, u32[]{:S(2)}, u32[]{:S(2)}) async-start(s32[32,1,8]{2,1,0:T(1,128)} %bitcast.2), calls=%async_computation | async-start | bytes 32768 | tf_op jit(solution)/shard_map/all_to_all | solution.py:106
  36.3 5.7 %copy-start.1 = (bf16[1024,512]{1,0:T(8,128)(2,1)S(1)}, bf16[1024,512]{1,0:T(8,128)(2,1)}, u32[]{:S(2)}) copy-start(bf16[1024,512]{1,0:T(8,128)(2,1)} %param.29) | copy-start | bytes 3145732
  61.3 14.7 %all-to-all-start.2 = ((s32[32,1,8]{2,1,0:T(1,128)}), s32[32,1,8]{2,1,0:T(1,128)S(1)}, u32[]{:S(2)}, u32[]{:S(2)}) async-start(s32[32,1,8]{2,1,0:T(1,128)} %bitcast.9), calls=%async_computation.2 | async-start | bytes 32768 | tf_op jit(solution)/shard_map/all_to_all | solution.py:107
  76.0 42.4 %all-to-all-start.1 = ((bf16[32,8,512]{2,1,0:T(8,128)(2,1)}), bf16[32,8,512]{2,1,0:T(8,128)(2,1)S(1)}, u32[]{:S(2)}, u32[]{:S(2)}) async-start(bf16[32,8,512]{2,1,0:T(8,128)(2,1)} %bitcast_select_fusion.1), calls=%async_computation.1 | async-start | bytes 524288 | tf_op jit(solution)/shard_map/all_to_all | solution.py:112
  111.6 6.8 %copy-start.14 = (bf16[512,512]{1,0:T(8,128)(2,1)S(1)}, bf16[512,512]{1,0:T(8,128)(2,1)}, u32[]{:S(2)}) copy-start(bf16[512,512]{1,0:T(8,128)(2,1)} %param.42) | copy-start | bytes 1572868
  118.4 11.1 %copy-start.16 = (f32[4,6400]{1,0:T(4,128)S(1)}, f32[4,6400]{1,0:T(4,128)}, u32[]{:S(2)}) copy-start(f32[4,6400]{1,0:T(4,128)} %param.34) | copy-start | bytes 307204
  118.4 11.1 %copy-start.17 = (f32[4,512]{1,0:T(4,128)S(1)}, f32[4,512]{1,0:T(4,128)}, u32[]{:S(2)}) copy-start(f32[4,512]{1,0:T(4,128)} %param.44) | copy-start | bytes 24580
  157.9 27.2 %copy-start.7 = (f32[256,512]{1,0:T(8,128)S(1)}, f32[256,512]{1,0:T(8,128)}, u32[]{:S(2)}) copy-start(f32[256,512]{1,0:T(8,128)} %fusion.29) | copy-start | bytes 1572868
  157.9 27.2 %copy-start.15 = (bf16[512,512]{1,0:T(8,128)(2,1)S(1)}, bf16[512,512]{1,0:T(8,128)(2,1)}, u32[]{:S(2)}) copy-start(bf16[512,512]{1,0:T(8,128)(2,1)} %param.48) | copy-start | bytes 1572868
  160.8 26.3 %copy-start.5 = (bf16[256,512]{1,0:T(8,128)(2,1)S(1)}, bf16[256,512]{1,0:T(8,128)(2,1)}, u32[]{:S(2)}) copy-start(bf16[256,512]{1,0:T(8,128)(2,1)} %param.30) | copy-start | bytes 786436
  160.8 26.3 %copy-start.10 = (f32[512]{0:T(512)S(1)}, f32[512]{0:T(512)}, u32[]{:S(2)}) copy-start(f32[512]{0:T(512)} %param.49) | copy-start | bytes 6148
  185.1 14.0 %copy-start.6 = (bf16[512,512]{1,0:T(8,128)(2,1)S(1)}, bf16[512,512]{1,0:T(8,128)(2,1)}, u32[]{:S(2)}) copy-start(bf16[512,512]{1,0:T(8,128)(2,1)} %param.52) | copy-start | bytes 1572868
  187.3 21.2 %collective-permute-start.2 = (bf16[256,512]{1,0:T(8,128)(2,1)S(1)}, bf16[256,512]{1,0:T(8,128)(2,1)S(1)}, u32[]{:S(2)}, u32[]{:S(2)}) collective-permute-start(bf16[256,512]{1,0:T(8,128)(2,1)S(1)} %add_convert_fusion.3), channel_id=1, source_target_pairs={{0,1},{1,2},{2,3},{3,4},{4,5},{5,6},{6,7},{7,8},{8,9},{9,10},{10,1... | collective-permute-start | bytes 786440 | tf_op jit(solution)/shard_map/ppermute | solution.py:22
  187.4 21.1 %collective-permute-start.3 = (bf16[256,512]{1,0:T(8,128)(2,1)S(1)}, bf16[256,512]{1,0:T(8,128)(2,1)S(1)}, u32[]{:S(2)}, u32[]{:S(2)}) collective-permute-start(bf16[256,512]{1,0:T(8,128)(2,1)S(1)} %add_convert_fusion.3), channel_id=1, source_target_pairs={{1,0},{2,1},{3,2},{4,3},{5,4},{6,5},{7,6},{8,7},{9,8},{10,9},{11,1... | collective-permute-start | bytes 786440 | tf_op jit(solution)/shard_map/ppermute | solution.py:23
  194.4 21.4 %all-to-all-start.3 = ((bf16[32,8,512]{2,1,0:T(8,128)(2,1)}), bf16[32,8,512]{2,1,0:T(8,128)(2,1)}, u32[]{:S(2)}, u32[]{:S(2)}) async-start(bf16[32,8,512]{2,1,0:T(8,128)(2,1)} %bitcast_select_fusion), calls=%async_computation.3 | async-start | bytes 524288 | tf_op jit(solution)/shard_map/all_to_all | solution.py:144
  199.0 73.9 %all-reduce.3.cloned.1.call-start = ((), (), s32[]{:S(2)}) async-start(), calls=%async_computation.4 | async-start | bytes 524288 | tf_op jit(solution)/shard_map/psum | solution.py:164
  215.8 10.7 %copy-start.3 = (bf16[1984,512]{1,0:T(8,128)(2,1)S(1)}, bf16[1984,512]{1,0:T(8,128)(2,1)}, u32[]{:S(2)}) copy-start(bf16[1984,512]{1,0:T(8,128)(2,1)} %param.35) | copy-start | bytes 6094852
  223.4 3.4 %copy-start.2 = (f32[1984,512]{1,0:T(8,128)S(1)}, f32[1984,512]{1,0:T(8,128)}, u32[]{:S(2)}) copy-start(f32[1984,512]{1,0:T(8,128)} %get-tuple-element.23) | copy-start | bytes 12189700
  223.4 3.4 %copy-start.11 = (f32[512]{0:T(512)S(1)}, f32[512]{0:T(512)}, u32[]{:S(2)}) copy-start(f32[512]{0:T(512)} %param.54) | copy-start | bytes 6148
  226.8 4.3 %copy-start.12 = (f32[512]{0:T(512)S(1)}, f32[512]{0:T(512)}, u32[]{:S(2)}) copy-start(f32[512]{0:T(512)} %param.41) | copy-start | bytes 6148
  233.8 41.3 %copy-start.13 = (f32[512]{0:T(512)S(1)}, f32[512]{0:T(512)}, u32[]{:S(2)}) copy-start(f32[512]{0:T(512)} %param.57) | copy-start | bytes 6148
  (4 other events, 7.2 us)
Sparse Core Ops, SparseCore 0:
  231.2 41.6 all-reduce.2
where the time goes:
time: 284 us; the launch traced here: 283 us
  local copies, waits for them, and re-layouts  73.1 us (26%)
  matrix products  68.2 us (24%)
  waiting for transfers between devices  39.6 us (14%)
  other arithmetic  32.8 us (12%)
  starting transfers between devices  30.4 us (11%)
  blocking collectives  24.3 us (9%)
  between operations  14.5 us (5%)
    psum x1, waiting for transfers between devices, on_device(): lax.psum(process_partial.astype(jnp.bfloat16), 'band').astype(jnp.float32)  35.5 us
    gather x1, local copies, waits for them, and re-layouts, on_device(): near_rows = jnp.take(grid_sectors, near_index, axis=0)  27.9 us
    psum x1, blocking collectives, on_device(): encode_sum = lax.psum(partial_value, 'band')  24.3 us
    dot_general x1, matrix products, on_device(): jnp.einsum('ke,kh->eh', encode_feature, encode_geometry, precision=lax.Pr...  20.6 us
    gather x1, local copies, waits for them, and re-layouts, on_device(): preact = preact + jnp.take(receive_term, encode_receiver, axis=0)  17.3 us
    dot_general x2, matrix products, edge_message(): jnp.dot(hidden, w_output, preferred_element_type=jnp.float32)  13.9 us
    dot_general x1, matrix products, on_device(): jnp.dot(sender_rows, encode_send, preferred_element_type=jnp.float32)  11.1 us
    ppermute x2, starting transfers between devices, with_halo(): after = lax.ppermute(leading, axis, down)  10.1 us
  transfers between devices with their start and end apart: 9, of which 2 were waited for; matrix products, arithmetic and copies ran while one was open for 39% of the time, Pallas kernels for 0%

commit v1 on v0

v1 whole, which is shorter than its diff:
```python
import functools

import jax
import jax.numpy as jnp
from jax import lax
from jax.experimental import pallas as pl
from jax.experimental.pallas import tpu as pltpu
from jax.sharding import PartitionSpec as P

NEAR_G = 2048
FAR_G = 8
NEAR_M = 576
FAR_M = 8
EPSILON = 1e-05
D = 512
NODES = 256
GRID = 1024
N_REG = 32
FAR = N_REG * FAR_G
NG = 3 * NEAR_G
NM = 3 * NEAR_M
NM_PAD = 1792
M2M = NM + FAR
BF = jnp.bfloat16
F32 = jnp.float32
VMEM = pl.BlockSpec(memory_space=pltpu.VMEM)
SMEM = pl.BlockSpec(memory_space=pltpu.SMEM)
ANY = pl.BlockSpec(memory_space=pl.ANY)


def nt(a, b):
    return lax.dot_general(a, b, (((1,), (1,)), ((), ())), preferred_element_type=F32)


def nn(a, b):
    return jnp.dot(a, b, preferred_element_type=F32)


def identity(n):
    row = lax.broadcasted_iota(jnp.int32, (n, n), 0)
    return (row == lax.broadcasted_iota(jnp.int32, (n, n), 1)).astype(F32).astype(BF)


def one_hot(rows, index):
    row = lax.broadcasted_iota(jnp.int32, (rows, index.shape[1]), 0).astype(jnp.int16)
    return jnp.where(row == index.astype(jnp.int16), jnp.ones((), BF), jnp.zeros((), BF))


def centred_t(weight):
    w_t = nt(identity(D), weight)
    return (w_t - jnp.mean(w_t, axis=0, keepdims=True)).astype(BF)


def feature_rows(feature):
    high = feature.astype(BF).astype(F32)
    zero = jnp.zeros(feature.shape, F32)
    return jnp.concatenate([high, feature - high, high, zero], axis=0).astype(BF)


def messages_t(half_pre, w_out_t, live):
    hidden = (half_pre * jnp.tanh(half_pre) + half_pre).astype(BF)
    y = nn(w_out_t, hidden)
    spread = jnp.sum(y * y, axis=0, keepdims=True) * (1 / D)
    scale = jnp.where(live, lax.rsqrt(spread + EPSILON), 0.0)
    return (y * scale).astype(BF)


def far_live(counts, width, near_cols):
    lane = lax.broadcasted_iota(jnp.int32, (1, width), 1)
    limit = jnp.zeros((1, width), jnp.int32)
    for k in range(N_REG):
        limit = jnp.where(lane // FAR_G == k, counts[0, 3 + k], limit)
    return lane % FAR_G < limit


def call(kernel, outs, in_specs, args, scratch=(), out_specs=None, flops=0, name=None, aliases=None):
    return pl.pallas_call(
        kernel,
        out_shape=outs,
        in_specs=in_specs,
        out_specs=jax.tree.map(lambda _: VMEM, outs) if out_specs is None else out_specs,
        scratch_shapes=list(scratch),
        compiler_params=pltpu.CompilerParams(vmem_limit_bytes=48 * 2**20),
        cost_estimate=pl.CostEstimate(flops=flops, bytes_accessed=2**20, transcendentals=0),
        input_output_aliases=aliases or {},
        name=name,
    )(*args)


def shape(dims, kind):
    return jax.ShapeDtypeStruct(dims, kind)


def encode_block(table, rt, gt, wt, sender, receiver, feature, live):
    hot = one_hot(NODES, receiver)
    pre = nn(table, one_hot(GRID, sender)) + nn(rt, hot) + nn(gt, feature_rows(feature))
    return nt(hot, messages_t(pre, wt, live))


def own_kernel(live, grid, mesh, sender, receiver, feature, w_send, w_recv, geo, w_out, out, wst, rt, gt, wt):
    eye = identity(D)
    wst[...] = (0.5 * nt(eye, w_send[...])).astype(BF)
    table = nt(wst[...], grid[...]).astype(BF)
    wrt = nt(eye, w_recv[...]).astype(BF)
    rt[...] = (0.5 * nt(wrt, mesh[...])).astype(BF)
    wt[...] = centred_t(w_out[...])
    half = 0.5 * geo[...]
    high = half.astype(BF).astype(F32)
    stacked = jnp.concatenate([high, high, half - high, jnp.zeros((4, D), F32)], axis=0)
    gt[...] = nt(eye, stacked.astype(BF)).astype(BF)
    part = pl.ds(NEAR_G, NEAR_G)
    lane = lax.broadcasted_iota(jnp.int32, (1, NEAR_G), 1)
    out[...] = encode_block(
        table, rt[...], gt[...], wt[...], sender[:, part], receiver[:, part], feature[:, part], lane < live[0, 1]
    )


def sides_kernel(live, before, after, sender, receiver, feature, wst, rt, gt, wt, total, out):
    lane = lax.broadcasted_iota(jnp.int32, (1, NEAR_G), 1)
    value = total[...]
    for q, rows in ((0, before), (2, after)):
        part = pl.ds(q * NEAR_G, NEAR_G)
        table = nt(wst[...], rows[...]).astype(BF)
        value = value + encode_block(
            table, rt[...], gt[...], wt[...], sender[:, part], receiver[:, part], feature[:, part], lane < live[0, q]
        )
    out[...] = value


def far_kernel(live, rows, receiver, feature, wst, rt, gt, wt, total, out):
    part = pl.ds(NG, FAR)
    hot = one_hot(NODES, receiver[:, part])
    pre = nt(wst[...], rows[...]) + nn(rt[...], hot) + nn(gt[...], feature_rows(feature[:, part]))
    message = messages_t(pre, wt[...], far_live(live, FAR, 0))
    out[...] = (total[...] + nt(hot, message)).astype(BF)


def asked_hot(asked, first, nodes):
    row = lax.broadcasted_iota(jnp.int32, (FAR, N_REG), 0)
    spread = (row // FAR_G == lax.broadcasted_iota(jnp.int32, (FAR, N_REG), 1)).astype(F32).astype(BF)
    high = (asked // 32).astype(F32).astype(BF)
    low = (asked % 32).astype(F32).astype(BF)
    value = nn(spread, high) * 32.0 + nn(spread, low)
    lane = lax.broadcasted_iota(jnp.int32, (FAR, 2 * FAR_G), 1)
    slot = lax.broadcasted_iota(jnp.int32, (FAR, 2 * FAR_G), 0) % FAR_G
    index = jnp.sum(jnp.where(lane == slot + first, value, 0.0), axis=1, keepdims=True).astype(jnp.int32)
    node = lax.broadcasted_iota(jnp.int32, (FAR, nodes), 1)
    return (node == index).astype(F32).astype(BF)


def send_kernel(asked, grid, out):
    out[...] = nn(asked_hot(asked[...], 0, GRID), grid[...]).astype(BF)


def norm(values):
    center = values - jnp.mean(values, axis=-1, keepdims=True)
    spread = jnp.mean(center * center, axis=-1, keepdims=True)
    return center * lax.rsqrt(spread + EPSILON)


def silu(values):
    half = 0.5 * values
    return (half * jnp.tanh(half) + half).astype(BF)


def mlp(latent, summed, w_first, w_second, gain):
    merged = nn(latent, w_first[:D, :]) + nn(summed, w_first[D:, :])
    update = norm(nn(silu(merged), w_second[...])) * gain[...]
    return (latent.astype(F32) + update).astype(BF)


def band_sum(p0, p1, p2, p3, edge_gain):
    total = (p0[...].astype(F32) + p2[...].astype(F32)) + (p1[...].astype(F32) + p3[...].astype(F32))
    return (total * edge_gain[...]).astype(BF)


def node_kernel(asked, mesh, p0, p1, p2, p3, edge_gain, w_first, w_second, gain, mid, rows):
    value = mlp(mesh[...], band_sum(p0, p1, p2, p3, edge_gain), w_first, w_second, gain)
    mid[...] = value
    rows[...] = nn(asked_hot(asked[...], FAR_G, NODES), value).astype(BF)


def update_kernel(mid, p0, p1, p2, p3, edge_gain, w_first, w_second, gain, out):
    out[...] = mlp(mid[...], band_sum(p0, p1, p2, p3, edge_gain), w_first, w_second, gain)


def grid_kernel(latent, w_first, w_second, gain, out):
    rows = latent[...]
    update = norm(nn(silu(nn(rows, w_first[...])), w_second[...])) * gain[...]
    out[...] = (rows.astype(F32) + update).astype(BF)


def rows_out(message, edge, gain):
    eye = identity(NODES)
    parts = [nt(eye, message[:, i : i + NODES]) for i in range(0, message.shape[1], NODES)]
    value = parts[0] if len(parts) == 1 else jnp.concatenate(parts, axis=0)
    return (edge.astype(F32) + value * gain).astype(BF)


def near_kernel(
    live, before, mid, after, edge, sender, receiver, w_edge, w_send, w_recv, w_out, gain, out, total, wet, wst, pt, wt
):
    eye = identity(D)
    wet[...] = (0.5 * nt(eye, w_edge[...])).astype(BF)
    wst[...] = (0.5 * nt(eye, w_send[...])).astype(BF)
    wrt = (0.5 * nt(eye, w_recv[...])).astype(BF)
    wt[...] = centred_t(w_out[...])
    pt[...] = nt(wrt, mid[...]).astype(BF)
    table = nt(wst[...], jnp.concatenate([before[...], mid[...], after[...]], axis=0)).astype(BF)
    lane = lax.broadcasted_iota(jnp.int32, (1, NM_PAD), 1)
    block = lane // NEAR_M
    count = jnp.where(block == 0, live[0, 0], jnp.where(block == 1, live[0, 1], live[0, 2]))
    mask = (lane - block * NEAR_M < count) & (lane < NM)
    part = pl.ds(0, NM_PAD)
    hot = one_hot(NODES, receiver[:, part])
    edges = edge[:NM_PAD, :]
    index = jnp.where(lane < NM, sender[:, part] + block * NODES, -1)
    pre = nt(wet[...], edges) + nn(table, one_hot(3 * NODES, index)) + nn(pt[...], hot)
    message = messages_t(pre, wt[...], mask)
    total[...] = nt(hot, message)
    out[:NM, :] = rows_out(message, edges, gain[...])[:NM, :]


def last_kernel(live, rows, edge, receiver, wet, wst, pt, wt, gain, total, edge_out, out, partial, held, sem):
    hot = one_hot(NODES, receiver[:, NM:M2M])
    edges = edge[NM:, :]
    pre = nt(wet[...], edges) + nt(wst[...], rows[...]) + nn(pt[...], hot)
    message = messages_t(pre, wt[...], far_live(live, FAR, 0))
    partial[...] = (total[...] + nt(hot, message)).astype(BF)
    held[...] = rows_out(message, edges, gain[...])
    copy = pltpu.make_async_copy(held, out.at[pl.ds(NM, FAR), :], sem)
    copy.start()
    copy.wait()


def band_parts(partial):
    count = lax.axis_size("band")
    moved = [
        lax.ppermute(partial, "band", [(i, (i + k) % count) for i in range(count)]) for k in range(1, count)
    ]
    return [partial] + moved


def halo(x):
    count = lax.axis_size("region")
    up = [(i, (i + 1) % count) for i in range(count)]
    down = [(j, i) for i, j in up]
    return lax.ppermute(x, "region", up), lax.ppermute(x, "region", down)


def exchange(x):
    return lax.all_to_all(x, "region", split_axis=0, concat_axis=0, tiled=True)


def on_device(
    grid_latent,
    mesh_latent,
    encode_sender,
    encode_receiver,
    encode_live,
    encode_feature,
    mesh_edge,
    mesh_sender,
    mesh_receiver,
    mesh_live,
    grid_first,
    grid_second,
    grid_gain,
    encode_send,
    encode_receive,
    encode_geometry,
    encode_output,
    encode_gain,
    node_first,
    node_second,
    node_gain,
    process_edge,
    process_send,
    process_receive,
    process_output,
    process_gain,
    update_first,
    update_second,
    update_gain,
):
    asks = jnp.concatenate(
        [encode_sender[NG:].reshape(N_REG, FAR_G), mesh_sender[NM:].reshape(N_REG, FAR_M)], axis=1
    )
    asked = exchange(asks)
    before, after = halo(grid_latent)
    sender = encode_sender.reshape(1, -1)
    receiver = encode_receiver.reshape(1, -1)
    gains = [g.reshape(1, D) for g in (grid_gain, encode_gain, node_gain, process_gain, update_gain)]

    weight = shape((D, D), BF)
    total, wst, rt, gt, wt = call(
        own_kernel,
        (shape((NODES, D), F32), weight, shape((D, NODES), BF), shape((D, 16), BF), weight),
        [SMEM] + [VMEM] * 9,
        (encode_live, grid_latent, mesh_latent, sender, receiver, encode_feature)
        + (encode_send, encode_receive, encode_geometry, encode_output),
        flops=8 * 10**9,
        name="encode_own",
    )
    outgoing = call(
        send_kernel, shape((FAR, D), BF), [VMEM] * 2, (asked, grid_latent), flops=3 * 10**8, name="encode_rows"
    )
    far_rows = exchange(outgoing.reshape(N_REG, FAR_G, D)).reshape(FAR, D)
    total = call(
        sides_kernel,
        shape((NODES, D), F32),
        [SMEM] + [VMEM] * 10,
        (encode_live, before, after, sender, receiver, encode_feature, wst, rt, gt, wt, total),
        flops=11 * 10**9,
        name="encode_sides",
    )
    partial = call(
        far_kernel,
        shape((NODES, D), BF),
        [SMEM] + [VMEM] * 8,
        (encode_live, far_rows, receiver, encode_feature, wst, rt, gt, wt, total),
        flops=10**9,
        name="encode_far",
    )
    partial, grid_rows = lax.optimization_barrier((partial, grid_latent))
    parts = band_parts(partial)
    grid_out = call(
        grid_kernel,
        shape((GRID, D), BF),
        [VMEM] * 4,
        (grid_rows, grid_first, grid_second, gains[0]),
        flops=3 * 10**9,
        name="grid_nodes",
    )
    mid, rows = call(
        node_kernel,
        (shape((NODES, D), BF), shape((FAR, D), BF)),
        [VMEM] * 10,
        (asked, mesh_latent, *parts, gains[1], node_first, node_second, gains[2]),
        flops=10**9,
        name="mesh_nodes",
    )
    far_mesh = exchange(rows.reshape(N_REG, FAR_M, D)).reshape(FAR, D)
    before_mid, after_mid = halo(mid)
    m_sender = mesh_sender.reshape(1, -1)
    m_receiver = mesh_receiver.reshape(1, -1)
    edge_near, m_total, wet, wst, pt, wt = call(
        near_kernel,
        (shape((M2M, D), BF), shape((NODES, D), F32), weight, weight, shape((D, NODES), BF), weight),
        [SMEM] + [VMEM] * 11,
        (mesh_live, before_mid, mid, after_mid, mesh_edge, m_sender, m_receiver)
        + (process_edge, process_send, process_receive, process_output, gains[3]),
        flops=6 * 10**9,
        name="process_near",
    )
    edge_out, m_partial = call(
        last_kernel,
        (shape((M2M, D), BF), shape((NODES, D), BF)),
        [SMEM] + [VMEM] * 9 + [ANY],
        (mesh_live, far_mesh, mesh_edge, m_receiver, wet, wst, pt, wt, gains[3], m_total, edge_near),
        scratch=[pltpu.VMEM((FAR, D), BF), pltpu.SemaphoreType.DMA],
        out_specs=(ANY, VMEM),
        flops=10**9,
        name="process_far",
        aliases={10: 0},
    )
    mesh_out = call(
        update_kernel,
        shape((NODES, D), BF),
        [VMEM] * 9,
        (mid, *band_parts(m_partial), gains[3], update_first, update_second, gains[4]),
        flops=10**9,
        name="mesh_update",
    )
    return (grid_out, mesh_out, edge_out)


def solution(mesh):
    edge = P(("band", "region"))
    rows = P(("band", "region"), None)
    mesh_rows = P("region", None)
    return jax.shard_map(
        on_device,
        mesh=mesh,
        in_specs=(rows, mesh_rows, edge, edge, rows, P(None, ("band", "region")), rows, edge, edge, rows) + (P(),) * 19,
        out_specs=(rows, mesh_rows, rows),
        check_vma=False,
    )
```

time: 284 us -> 142 us (0.50)
  matrix products: 68.2 us -> 0 us
  Pallas kernels: 0 us -> 43.7 us
  local copies, waits for them, and re-layouts: 73.1 us -> 38.6 us
  other arithmetic: 32.8 us -> 0.69 us
  blocking collectives: 24.3 us -> 0 us
  waiting for transfers between devices: 39.6 us -> 19.2 us
  between operations: 14.5 us -> 0.98 us
  starting transfers between devices: 30.4 us -> 37.3 us
    dot_general x14 -> x0, matrix products: 68.2 us -> none  [the longest x1 20.6 us: on_device(): jnp.einsum('ke,kh->eh', encode_feature, encode_geometry, precision=lax.Pr...]
    gather x6 -> x0, local copies, waits for them, and re-layouts: 62.3 us -> none  [the longest x1 27.9 us: on_device(): near_rows = jnp.take(grid_sectors, near_index, axis=0)]
    pallas_call x0 -> x9, Pallas kernels: none -> 43.7 us  [call(): pl.pallas_call(kernel, out_shape=outs, in_specs=in_specs, out_specs=jax.t...]
    psum x1 -> x0, waiting for transfers between devices: 35.5 us -> none  [on_device(): lax.psum(process_partial.astype(jnp.bfloat16), 'band').astype(jnp.float32)]
    unnamed x40 -> x120, local copies, waits for them, and re-layouts: 4.14 us -> 35.5 us
    psum x1 -> x0, blocking collectives: 24.3 us -> none  [on_device(): encode_sum = lax.psum(partial_value, 'band')]
    ppermute x4 -> x10, waiting for transfers between devices: 0.01 us -> 19.2 us  [the longest x6 19.1 us: band_parts(): lax.ppermute(partial, 'band', [(i, (i + k) % count) for i in range(count)])]
    ppermute x4 -> x10, starting transfers between devices: 10.3 us -> 21.7 us  [the longest x6 11.5 us: band_parts(): lax.ppermute(partial, 'band', [(i, (i + k) % count) for i in range(count)])]
  transfers between devices with their start and end apart: 9 -> 13, of which waited for: 2 -> 6; matrix products, arithmetic and copies ran while one was open for 39% -> 3% of each run, Pallas kernels for 0% -> 25%
where the time goes in v1:
time: 142 us; the launch traced here: 140 us
  Pallas kernels  43.7 us (31%)
  local copies, waits for them, and re-layouts  38.6 us (27%)
  starting transfers between devices  37.3 us (26%)
  waiting for transfers between devices  19.2 us (14%)
    pallas_call x9, Pallas kernels, call(): pl.pallas_call(kernel, out_shape=outs, in_specs=in_specs, out_specs=jax.t...  43.7 us
    unnamed x120, local copies, waits for them, and re-layouts  35.5 us
    ppermute x6, waiting for transfers between devices, band_parts(): lax.ppermute(partial, 'band', [(i, (i + k) % count) for i in range(count)])  19.1 us
    all_to_all x3, starting transfers between devices, exchange(): return lax.all_to_all(x, 'region', split_axis=0, concat_axis=0, tiled=True)  15.6 us
    ppermute x6, starting transfers between devices, band_parts(): lax.ppermute(partial, 'band', [(i, (i + k) % count) for i in range(count)])  11.5 us
    ppermute x4, starting transfers between devices, halo(): return (lax.ppermute(x, 'region', up), lax.ppermute(x, 'region', down))  10.2 us
  transfers between devices with their start and end apart: 13, of which 6 were waited for; matrix products, arithmetic and copies ran while one was open for 3% of the time, Pallas kernels for 25%

profile of v1, /device:TPU:0, one launch (start us, length us, event | category | flops | bytes accessed | tf_op | source)
XLA Modules:
  0.0 140.4 jit_solution(1858300930644350321)
XLA Ops:
  0.7 5.1 %collective-permute-start.1 = (bf16[1024,512]{1,0:T(8,128)(2,1)}, bf16[1024,512]{1,0:T(8,128)(2,1)}, u32[]{:S(2)}, u32[]{:S(2)}) collective-permute-start(bf16[1024,512]{1,0:T(8,128)(2,1)} %latent), channel_id=1, source_target_pairs={{1,0},{2,1},{3,2},{4,3},{5,4},{6,5},{7,6},{8,7},{9,8},{10,9},{11,1... | collective-permute-start | bytes 3145736 | tf_op jit(solution)/shard_map/ppermute | solution.py:248
  8.1 4.1 %all-to-all-start = ((s32[32,1,16]{2,1,0:T(1,128)}), s32[32,1,16]{2,1,0:T(1,128)S(1)}, u32[]{:S(2)}, u32[]{:S(2)}) async-start(s32[32,1,16]{2,1,0:T(1,128)} %bitcast.1), calls=%async_computation | async-start | bytes 32768 | tf_op jit(solution)/shard_map/all_to_all | solution.py:252
  13.7 1.2 copy-done.1
  21.3 7.7 %encode_own.1 = (f32[256,512]{1,0:T(8,128)S(1)}, bf16[512,512]{1,0:T(8,128)(2,1)S(1)}, bf16[512,256]{1,0:T(8,128)(2,1)S(1)}, bf16[512,16]{1,0:T(8,128)(2,1)S(1)}, bf16[512,512]{1,0:T(8,128)(2,1)S(1)}) custom-call(s32[1,35]{1,0:T(1,128)S(1)} %copy-done.46, bf16[1024,512]{1,0:T(8,128)(2,1)S(1)} %copy-done.1, bf16[256,512]{1,0:T(8,128)(2,1)S(1)} %copy-done.30, ...), custom_call_target="tpu_custom_call" | custom-call | flops 8000000000 | bytes 1048576 | tf_op jit(solution)/shard_map/encode_own/pallas_call | solution.py:77
  31.3 1.4 encode_rows.1
  32.7 7.6 %all-to-all-start.1 = ((bf16[32,8,512]{2,1,0:T(8,128)(2,1)}), bf16[32,8,512]{2,1,0:T(8,128)(2,1)S(1)}, u32[]{:S(2)}, u32[]{:S(2)}) async-start(bf16[32,8,512]{2,1,0:T(8,128)(2,1)} %bitcast.3), calls=%async_computation.1 | async-start | bytes 524288 | tf_op jit(solution)/shard_map/all_to_all | solution.py:252
  43.4 13.1 %encode_sides.1.total = f32[256,512]{1,0:T(8,128)S(1)} custom-call(s32[1,35]{1,0:T(1,128)S(1)} %copy-done.47, bf16[1024,512]{1,0:T(8,128)(2,1)S(1)} %collective-permute-done.before, bf16[1024,512]{1,0:T(8,128)(2,1)} %collective-permute-done.1.after, s32[1,6400]{1,0:T(1,128)S(1)} %reshape.74.sender, s32[1,6400]{1,0:T(1,128)S(1)} %reshape.73.receiver, ...), custom_call_target="tpu_custom_call" | custom-call | flops 11000000512 | bytes 1048576 | tf_op jit(solution)/shard_map/encode_sides/pallas_call | solution.py:77
  61.6 1.9 %encode_far.1.p0 = bf16[256,512]{1,0:T(8,128)(2,1)S(1)} custom-call(s32[1,35]{1,0:T(1,128)S(1)} %copy-done.47, bf16[256,512]{1,0:T(8,128)(2,1)S(1)} %bitcast.16, s32[1,6400]{1,0:T(1,128)S(1)} %reshape.73.receiver, f32[4,6400]{1,0:T(4,128)S(1)} %copy-done.40, bf16[512,512]{1,0:T(8,128)(2,1)S(1)} %copy-done.49, bf16[512,256]{1,0:T(8,128)(2,1)S(1)} %copy-done.57, ...), custom_call_target="tpu_custom_call" | custom-call | flops 1000000000 | bytes 1048576 | tf_op jit(solution)/shard_map/encode_far/pallas_call | solution.py:77
  63.5 2.0 %collective-permute-start.2 = (bf16[256,512]{1,0:T(8,128)(2,1)S(1)}, bf16[256,512]{1,0:T(8,128)(2,1)S(1)}, u32[]{:S(2)}, u32[]{:S(2)}) collective-permute-start(bf16[256,512]{1,0:T(8,128)(2,1)S(1)} %encode_far.1.p0), channel_id=1, source_target_pairs={{0,32},{32,64},{64,96},{96,0},{1,33},{33,65},{65,97},{97,1},{2,34}... | collective-permute-start | bytes 786440 | tf_op jit(solution)/shard_map/ppermute | solution.py:239
  65.5 3.6 %collective-permute-start.3 = (bf16[256,512]{1,0:T(8,128)(2,1)S(1)}, bf16[256,512]{1,0:T(8,128)(2,1)S(1)}, u32[]{:S(2)}, u32[]{:S(2)}) collective-permute-start(bf16[256,512]{1,0:T(8,128)(2,1)S(1)} %encode_far.1.p0), channel_id=1, source_target_pairs={{0,64},{32,96},{64,0},{96,32},{1,65},{33,97},{65,1},{97,33},{2,66}... | collective-permute-start | bytes 786440 | tf_op jit(solution)/shard_map/ppermute | solution.py:239
  70.1 4.1 %collective-permute-done.2.p1 = bf16[256,512]{1,0:T(8,128)(2,1)S(1)} collective-permute-done((bf16[256,512]{1,0:T(8,128)(2,1)S(1)}, bf16[256,512]{1,0:T(8,128)(2,1)S(1)}, u32[]{:S(2)}, u32[]{:S(2)}) %collective-permute-start.2) | collective-permute-done | bytes 262176 | tf_op jit(solution)/shard_map/ppermute | solution.py:239
  74.2 6.8 %collective-permute-done.3.p2 = bf16[256,512]{1,0:T(8,128)(2,1)S(1)} collective-permute-done((bf16[256,512]{1,0:T(8,128)(2,1)S(1)}, bf16[256,512]{1,0:T(8,128)(2,1)S(1)}, u32[]{:S(2)}, u32[]{:S(2)}) %collective-permute-start.3) | collective-permute-done | bytes 262176 | tf_op jit(solution)/shard_map/ppermute | solution.py:239
  81.1 1.9 %mesh_nodes.1 = (bf16[256,512]{1,0:T(8,128)(2,1)S(1)}, bf16[256,512]{1,0:T(8,128)(2,1)}) custom-call(s32[32,16]{1,0:T(8,128)S(1)} %bitcast.18, bf16[256,512]{1,0:T(8,128)(2,1)S(1)} %copy-done.31, bf16[256,512]{1,0:T(8,128)(2,1)S(1)} %encode_far.1.p0, bf16[256,512]{1,0:T(8,128)(2,1)S(1)} %collective-permute-done.2.p1, ...), custom_call_target="tpu_custom_call" | custom-call | flops 1000000000 | bytes 1048576 | tf_op jit(solution)/shard_map/mesh_nodes/pallas_call | solution.py:77
  83.0 5.1 %collective-permute-start.6 = (bf16[256,512]{1,0:T(8,128)(2,1)S(1)}, bf16[256,512]{1,0:T(8,128)(2,1)S(1)}, u32[]{:S(2)}, u32[]{:S(2)}) collective-permute-start(bf16[256,512]{1,0:T(8,128)(2,1)S(1)} %get-tuple-element.27.mid), channel_id=1, source_target_pairs={{1,0},{2,1},{3,2},{4,3},{5,4},{6,5},{7,6},{8,7},{9,8},{10,9},{11,1... | collective-permute-start | bytes 786440 | tf_op jit(solution)/shard_map/ppermute | solution.py:248
  88.0 3.9 %all-to-all-start.2 = ((bf16[32,8,512]{2,1,0:T(8,128)(2,1)}), bf16[32,8,512]{2,1,0:T(8,128)(2,1)S(1)}, u32[]{:S(2)}, u32[]{:S(2)}) async-start(bf16[32,8,512]{2,1,0:T(8,128)(2,1)} %bitcast.8), calls=%async_computation.2 | async-start | bytes 524288 | tf_op jit(solution)/shard_map/all_to_all | solution.py:252
  100.5 10.3 %process_near.1 = (bf16[1984,512]{1,0:T(8,128)(2,1)}, f32[256,512]{1,0:T(8,128)S(1)}, bf16[512,512]{1,0:T(8,128)(2,1)S(1)}, bf16[512,512]{1,0:T(8,128)(2,1)S(1)}...) custom-call(s32[1,35]{1,0:T(1,128)S(1)} %copy-done.15, bf16[256,512]{1,0:T(8,128)(2,1)S(1)} %copy-done.36, ...), custom_call_target="tpu_custom_call" | custom-call | flops 6000000000 | bytes 1048576 | tf_op jit(solution)/shard_map/process_near/pallas_call | solution.py:77
  119.9 2.9 %process_far.1 = (bf16[1984,512]{1,0:T(8,128)(2,1)}, bf16[256,512]{1,0:T(8,128)(2,1)S(1)}) custom-call(s32[1,35]{1,0:T(1,128)S(1)} %copy-done.15, bf16[256,512]{1,0:T(8,128)(2,1)S(1)} %bitcast.15, bf16[1984,512]{1,0:T(8,128)(2,1)S(1)} %copy-done, s32[1,1984]{1,0:T(1,128)S(1)} %bitcast.20, ...), custom_call_target="tpu_custom_call", output_to_operand_aliasing={{0}: (10, {})} | custom-call | flops 1000000000 | bytes 1048576 | tf_op jit(solution)/shard_map/process_far/pallas_call | solution.py:77
  122.9 1.3 collective-permute-start.7
  124.1 2.4 %collective-permute-start.8 = (bf16[256,512]{1,0:T(8,128)(2,1)S(1)}, bf16[256,512]{1,0:T(8,128)(2,1)S(1)}, u32[]{:S(2)}, u32[]{:S(2)}) collective-permute-start(bf16[256,512]{1,0:T(8,128)(2,1)S(1)} %get-tuple-element.35.p0), channel_id=1, source_target_pairs={{0,64},{32,96},{64,0},{96,32},{1,65},{33,97},{65,1},{97,33},{2,66}... | collective-permute-start | bytes 786440 | tf_op jit(solution)/shard_map/ppermute | solution.py:239
  126.5 1.2 collective-permute-start.9
  127.8 2.8 %grid_nodes.1 = bf16[1024,512]{1,0:T(8,128)(2,1)} custom-call(bf16[1024,512]{1,0:T(8,128)(2,1)S(1)} %copy-done.2, bf16[512,512]{1,0:T(8,128)(2,1)S(1)} %copy-done.27, bf16[512,512]{1,0:T(8,128)(2,1)S(1)} %copy-done.28, f32[1,512]{1,0:T(1,128)S(1)} %bitcast.27), custom_call_target="tpu_custom_call" | custom-call | flops 3000000000 | bytes 1048576 | tf_op jit(solution)/shard_map/grid_nodes/pallas_call | solution.py:77
  130.6 2.3 %collective-permute-done.7.p1 = bf16[256,512]{1,0:T(8,128)(2,1)S(1)} collective-permute-done((bf16[256,512]{1,0:T(8,128)(2,1)S(1)}, bf16[256,512]{1,0:T(8,128)(2,1)S(1)}, u32[]{:S(2)}, u32[]{:S(2)}) %collective-permute-start.7) | collective-permute-done | bytes 262176 | tf_op jit(solution)/shard_map/ppermute | solution.py:239
  132.9 5.6 %collective-permute-done.8.p2 = bf16[256,512]{1,0:T(8,128)(2,1)S(1)} collective-permute-done((bf16[256,512]{1,0:T(8,128)(2,1)S(1)}, bf16[256,512]{1,0:T(8,128)(2,1)S(1)}, u32[]{:S(2)}, u32[]{:S(2)}) %collective-permute-start.8) | collective-permute-done | bytes 262176 | tf_op jit(solution)/shard_map/ppermute | solution.py:239
  138.8 1.6 %mesh_update.1 = bf16[256,512]{1,0:T(8,128)(2,1)} custom-call(bf16[256,512]{1,0:T(8,128)(2,1)S(1)} %copy-done.34, bf16[256,512]{1,0:T(8,128)(2,1)S(1)} %get-tuple-element.35.p0, bf16[256,512]{1,0:T(8,128)(2,1)S(1)} %collective-permute-done.7.p1, bf16[256,512]{1,0:T(8,128)(2,1)S(1)} %collective-permute-done.8.p2, ...), custom_call_target="tpu_custom_call" | custom-call | flops 1000000000 | bytes 1048576 | tf_op jit(solution)/shard_map/mesh_update/pallas_call | solution.py:77
  (138 shorter events, 39.6 us)
Async XLA Ops:
  0.6 39.7 %collective-permute-start = (bf16[1024,512]{1,0:T(8,128)(2,1)}, bf16[1024,512]{1,0:T(8,128)(2,1)S(1)}, u32[]{:S(2)}, u32[]{:S(2)}) collective-permute-start(bf16[1024,512]{1,0:T(8,128)(2,1)} %latent), channel_id=1, source_target_pairs={{0,1},{1,2},{2,3},{3,4},{4,5},{5,6},{6,7},{7,8},{8,9},{9,10},{10,1... | collective-permute-start | bytes 3145736 | tf_op jit(solution)/shard_map/ppermute | solution.py:248
  0.7 39.6 %collective-permute-start.1 = (bf16[1024,512]{1,0:T(8,128)(2,1)}, bf16[1024,512]{1,0:T(8,128)(2,1)}, u32[]{:S(2)}, u32[]{:S(2)}) collective-permute-start(bf16[1024,512]{1,0:T(8,128)(2,1)} %latent), channel_id=1, source_target_pairs={{1,0},{2,1},{3,2},{4,3},{5,4},{6,5},{7,6},{8,7},{9,8},{10,9},{11,1... | collective-permute-start | bytes 3145736 | tf_op jit(solution)/shard_map/ppermute | solution.py:248
  8.1 23.2 %all-to-all-start = ((s32[32,1,16]{2,1,0:T(1,128)}), s32[32,1,16]{2,1,0:T(1,128)S(1)}, u32[]{:S(2)}, u32[]{:S(2)}) async-start(s32[32,1,16]{2,1,0:T(1,128)} %bitcast.1), calls=%async_computation | async-start | bytes 32768 | tf_op jit(solution)/shard_map/all_to_all | solution.py:252
  21.3 19.0 %copy-start.40 = (f32[4,6400]{1,0:T(4,128)S(1)}, f32[4,6400]{1,0:T(4,128)}, u32[]{:S(2)}) copy-start(f32[4,6400]{1,0:T(4,128)} %feature.5) | copy-start | bytes 307204
  21.3 19.1 %copy-start.47 = (s32[1,35]{1,0:T(1,128)S(1)}, s32[1,35]{1,0:T(1,128)}, u32[]{:S(2)}) copy-start(s32[1,35]{1,0:T(1,128)} %live.7) | copy-start | bytes 424
  32.7 24.6 %all-to-all-start.1 = ((bf16[32,8,512]{2,1,0:T(8,128)(2,1)}), bf16[32,8,512]{2,1,0:T(8,128)(2,1)S(1)}, u32[]{:S(2)}, u32[]{:S(2)}) async-start(bf16[32,8,512]{2,1,0:T(8,128)(2,1)} %bitcast.3), calls=%async_computation.1 | async-start | bytes 524288 | tf_op jit(solution)/shard_map/all_to_all | solution.py:252
  57.3 23.7 %copy-start.17 = (bf16[1024,512]{1,0:T(8,128)(2,1)S(1)}, bf16[1024,512]{1,0:T(8,128)(2,1)}, u32[]{:S(2)}) copy-start(bf16[1024,512]{1,0:T(8,128)(2,1)} %w_first.4) | copy-start | bytes 3145732
  57.3 23.7 %copy-start.22 = (bf16[512,512]{1,0:T(8,128)(2,1)S(1)}, bf16[512,512]{1,0:T(8,128)(2,1)}, u32[]{:S(2)}) copy-start(bf16[512,512]{1,0:T(8,128)(2,1)} %w_second.4) | copy-start | bytes 1572868
  57.3 23.7 %copy-start.31 = (bf16[256,512]{1,0:T(8,128)(2,1)S(1)}, bf16[256,512]{1,0:T(8,128)(2,1)}, u32[]{:S(2)}) copy-start(bf16[256,512]{1,0:T(8,128)(2,1)} %mesh.3) | copy-start | bytes 786436
  57.3 23.7 %copy-start.42 = (f32[512]{0:T(512)S(1)}, f32[512]{0:T(512)}, u32[]{:S(2)}) copy-start(f32[512]{0:T(512)} %param.46) | copy-start | bytes 6148
  57.3 23.7 %copy-start.43 = (f32[512]{0:T(512)S(1)}, f32[512]{0:T(512)}, u32[]{:S(2)}) copy-start(f32[512]{0:T(512)} %param.49) | copy-start | bytes 6148
  63.5 10.7 %collective-permute-start.2 = (bf16[256,512]{1,0:T(8,128)(2,1)S(1)}, bf16[256,512]{1,0:T(8,128)(2,1)S(1)}, u32[]{:S(2)}, u32[]{:S(2)}) collective-permute-start(bf16[256,512]{1,0:T(8,128)(2,1)S(1)} %encode_far.1.p0), channel_id=1, source_target_pairs={{0,32},{32,64},{64,96},{96,0},{1,33},{33,65},{65,97},{97,1},{2,34}... | collective-permute-start | bytes 786440 | tf_op jit(solution)/shard_map/ppermute | solution.py:239
  65.5 15.5 %collective-permute-start.3 = (bf16[256,512]{1,0:T(8,128)(2,1)S(1)}, bf16[256,512]{1,0:T(8,128)(2,1)S(1)}, u32[]{:S(2)}, u32[]{:S(2)}) collective-permute-start(bf16[256,512]{1,0:T(8,128)(2,1)S(1)} %encode_far.1.p0), channel_id=1, source_target_pairs={{0,64},{32,96},{64,0},{96,32},{1,65},{33,97},{65,1},{97,33},{2,66}... | collective-permute-start | bytes 786440 | tf_op jit(solution)/shard_map/ppermute | solution.py:239
  69.1 11.9 %collective-permute-start.4 = (bf16[256,512]{1,0:T(8,128)(2,1)S(1)}, bf16[256,512]{1,0:T(8,128)(2,1)S(1)}, u32[]{:S(2)}, u32[]{:S(2)}) collective-permute-start(bf16[256,512]{1,0:T(8,128)(2,1)S(1)} %encode_far.1.p0), channel_id=1, source_target_pairs={{0,96},{32,0},{64,32},{96,64},{1,97},{33,1},{65,33},{97,65},{2,98}... | collective-permute-start | bytes 786440 | tf_op jit(solution)/shard_map/ppermute | solution.py:239
  81.0 12.5 %copy-start.13 = (s32[1984]{0:T(1024)S(1)}, s32[1984]{0:T(1024)}, u32[]{:S(2)}) copy-start(s32[1984]{0:T(1024)} %param.37) | copy-start | bytes 23812
  81.0 12.5 %copy-start.14 = (f32[512]{0:T(512)S(1)}, f32[512]{0:T(512)}, u32[]{:S(2)}) copy-start(f32[512]{0:T(512)} %param.54) | copy-start | bytes 6148
  81.0 12.5 %copy-start.15 = (s32[1,35]{1,0:T(1,128)S(1)}, s32[1,35]{1,0:T(1,128)}, u32[]{:S(2)}) copy-start(s32[1,35]{1,0:T(1,128)} %live.9) | copy-start | bytes 424
  83.0 9.1 %collective-permute-start.5 = (bf16[256,512]{1,0:T(8,128)(2,1)S(1)}, bf16[256,512]{1,0:T(8,128)(2,1)S(1)}, u32[]{:S(2)}, u32[]{:S(2)}) collective-permute-start(bf16[256,512]{1,0:T(8,128)(2,1)S(1)} %get-tuple-element.27.mid), channel_id=1, source_target_pairs={{0,1},{1,2},{2,3},{3,4},{4,5},{5,6},{6,7},{7,8},{8,9},{9,10},{10,1... | collective-permute-start | bytes 786440 | tf_op jit(solution)/shard_map/ppermute | solution.py:248
  83.0 9.8 %collective-permute-start.6 = (bf16[256,512]{1,0:T(8,128)(2,1)S(1)}, bf16[256,512]{1,0:T(8,128)(2,1)S(1)}, u32[]{:S(2)}, u32[]{:S(2)}) collective-permute-start(bf16[256,512]{1,0:T(8,128)(2,1)S(1)} %get-tuple-element.27.mid), channel_id=1, source_target_pairs={{1,0},{2,1},{3,2},{4,3},{5,4},{6,5},{7,6},{8,7},{9,8},{10,9},{11,1... | collective-permute-start | bytes 786440 | tf_op jit(solution)/shard_map/ppermute | solution.py:248
  88.0 26.8 %all-to-all-start.2 = ((bf16[32,8,512]{2,1,0:T(8,128)(2,1)}), bf16[32,8,512]{2,1,0:T(8,128)(2,1)S(1)}, u32[]{:S(2)}, u32[]{:S(2)}) async-start(bf16[32,8,512]{2,1,0:T(8,128)(2,1)} %bitcast.8), calls=%async_computation.2 | async-start | bytes 524288 | tf_op jit(solution)/shard_map/all_to_all | solution.py:252
  100.5 14.3 %copy-start = (bf16[1984,512]{1,0:T(8,128)(2,1)S(1)}, bf16[1984,512]{1,0:T(8,128)(2,1)}, u32[]{:S(2)}) copy-start(bf16[1984,512]{1,0:T(8,128)(2,1)} %edge.3) | copy-start | bytes 6094852
  122.9 10.1 %collective-permute-start.7 = (bf16[256,512]{1,0:T(8,128)(2,1)S(1)}, bf16[256,512]{1,0:T(8,128)(2,1)S(1)}, u32[]{:S(2)}, u32[]{:S(2)}) collective-permute-start(bf16[256,512]{1,0:T(8,128)(2,1)S(1)} %get-tuple-element.35.p0), channel_id=1, source_target_pairs={{0,32},{32,64},{64,96},{96,0},{1,33},{33,65},{65,97},{97,1},{2,34}... | collective-permute-start | bytes 786440 | tf_op jit(solution)/shard_map/ppermute | solution.py:239
  124.1 14.4 %collective-permute-start.8 = (bf16[256,512]{1,0:T(8,128)(2,1)S(1)}, bf16[256,512]{1,0:T(8,128)(2,1)S(1)}, u32[]{:S(2)}, u32[]{:S(2)}) collective-permute-start(bf16[256,512]{1,0:T(8,128)(2,1)S(1)} %get-tuple-element.35.p0), channel_id=1, source_target_pairs={{0,64},{32,96},{64,0},{96,32},{1,65},{33,97},{65,1},{97,33},{2,66}... | collective-permute-start | bytes 786440 | tf_op jit(solution)/shard_map/ppermute | solution.py:239
  126.5 12.2 %collective-permute-start.9 = (bf16[256,512]{1,0:T(8,128)(2,1)S(1)}, bf16[256,512]{1,0:T(8,128)(2,1)S(1)}, u32[]{:S(2)}, u32[]{:S(2)}) collective-permute-start(bf16[256,512]{1,0:T(8,128)(2,1)S(1)} %get-tuple-element.35.p0), channel_id=1, source_target_pairs={{0,96},{32,0},{64,32},{96,64},{1,97},{33,1},{65,33},{97,65},{2,98}... | collective-permute-start | bytes 786440 | tf_op jit(solution)/shard_map/ppermute | solution.py:239
  (49 other events, 145.0 us)

commit v2 on v1

--- a/solution.py
+++ b/solution.py
@@ -26,6 +26,8 @@
 VMEM = pl.BlockSpec(memory_space=pltpu.VMEM)
 SMEM = pl.BlockSpec(memory_space=pltpu.SMEM)
 ANY = pl.BlockSpec(memory_space=pl.ANY)
+HBM = pl.BlockSpec(memory_space=pltpu.HBM)
+HALF = NEAR_G // 2
 
 
 def nt(a, b):
@@ -73,14 +75,44 @@
     return lane % FAR_G < limit
 
 
-def call(kernel, outs, in_specs, args, scratch=(), out_specs=None, flops=0, name=None, aliases=None):
+class Late:
+    def __init__(self, held, copy):
+        self.held, self.copy = held, copy
+        self.shape = held.shape
+
+    def __getitem__(self, index):
+        if self.copy is not None:
+            self.copy.wait()
+            self.copy = None
+        return self.held[index]
+
+
+def call(kernel, outs, specs, args, scratch=(), out_specs=None, flops=0, name=None, aliases=None, grant=24):
+    late = [i for i, spec in enumerate(specs) if spec in "HA"]
+    place = {"S": SMEM, "V": VMEM, "H": HBM, "A": ANY, "R": ANY}
+    n_in, n_out = len(args), len(jax.tree.leaves(outs))
+
+    def body(*refs):
+        ins, rest = list(refs[:n_in]), refs[n_in:]
+        held, sems = rest[n_out : n_out + len(late)], rest[n_out + len(late)]
+        copies = [pltpu.make_async_copy(ins[i], held[j], sems.at[j]) for j, i in enumerate(late)]
+        for j, i in enumerate(late):
+            copies[j].start()
+            ins[i] = Late(held[j], copies[j])
+        kernel(*ins, *rest[:n_out], *rest[n_out + len(late) + 1 :])
+        for i in late:
+            if ins[i].copy is not None:
+                ins[i].copy.wait()
+
     return pl.pallas_call(
-        kernel,
+        body,
         out_shape=outs,
-        in_specs=in_specs,
+        in_specs=[place[spec] for spec in specs],
         out_specs=jax.tree.map(lambda _: VMEM, outs) if out_specs is None else out_specs,
-        scratch_shapes=list(scratch),
-        compiler_params=pltpu.CompilerParams(vmem_limit_bytes=48 * 2**20),
+        scratch_shapes=[pltpu.VMEM(args[i].shape, args[i].dtype) for i in late]
+        + [pltpu.SemaphoreType.DMA((len(late),))]
+        + list(scratch),
+        compiler_params=pltpu.CompilerParams(vmem_limit_bytes=grant * 2**20),
         cost_estimate=pl.CostEstimate(flops=flops, bytes_accessed=2**20, transcendentals=0),
         input_output_aliases=aliases or {},
         name=name,
@@ -91,46 +123,45 @@
     return jax.ShapeDtypeStruct(dims, kind)
 
 
-def encode_block(table, rt, gt, wt, sender, receiver, feature, live):
-    hot = one_hot(NODES, receiver)
-    pre = nn(table, one_hot(GRID, sender)) + nn(rt, hot) + nn(gt, feature_rows(feature))
-    return nt(hot, messages_t(pre, wt, live))
-
-
-def own_kernel(live, grid, mesh, sender, receiver, feature, w_send, w_recv, geo, w_out, out, wst, rt, gt, wt):
+def encode_block(q, table, rt, gt, wt, sender, receiver, feature, limit):
+    value = None
+    for i in range(0, NEAR_G, HALF):
+        part = slice(q * NEAR_G + i, q * NEAR_G + i + HALF)
+        hot = one_hot(NODES, receiver[part].reshape(1, HALF))
+        pre = nn(table, one_hot(GRID, sender[part].reshape(1, HALF))) + nn(rt, hot)
+        pre = pre + nn(gt, feature_rows(feature[:, part]))
+        live = lax.broadcasted_iota(jnp.int32, (1, HALF), 1) + i < limit
+        term = nt(hot, messages_t(pre, wt, live))
+        value = term if value is None else value + term
+    return value
+
+
+def own_kernel(live, w_send, grid, w_recv, mesh, geo, w_out, sender, receiver, feature, out, wst, rt, gt, wt):
     eye = identity(D)
     wst[...] = (0.5 * nt(eye, w_send[...])).astype(BF)
     table = nt(wst[...], grid[...]).astype(BF)
     wrt = nt(eye, w_recv[...]).astype(BF)
     rt[...] = (0.5 * nt(wrt, mesh[...])).astype(BF)
-    wt[...] = centred_t(w_out[...])
     half = 0.5 * geo[...]
     high = half.astype(BF).astype(F32)
     stacked = jnp.concatenate([high, high, half - high, jnp.zeros((4, D), F32)], axis=0)
     gt[...] = nt(eye, stacked.astype(BF)).astype(BF)
-    part = pl.ds(NEAR_G, NEAR_G)
-    lane = lax.broadcasted_iota(jnp.int32, (1, NEAR_G), 1)
-    out[...] = encode_block(
-        table, rt[...], gt[...], wt[...], sender[:, part], receiver[:, part], feature[:, part], lane < live[0, 1]
-    )
-
-
-def sides_kernel(live, before, after, sender, receiver, feature, wst, rt, gt, wt, total, out):
-    lane = lax.broadcasted_iota(jnp.int32, (1, NEAR_G), 1)
-    value = total[...]
+    wt[...] = centred_t(w_out[...])
+    out[...] = encode_block(1, table, rt[...], gt[...], wt[...], sender, receiver, feature, live[0, 1])
+
+
+def sides_kernel(live, before, wst, sender, receiver, feature, rt, gt, wt, after, total, out):
+    value = 0.0
     for q, rows in ((0, before), (2, after)):
-        part = pl.ds(q * NEAR_G, NEAR_G)
         table = nt(wst[...], rows[...]).astype(BF)
-        value = value + encode_block(
-            table, rt[...], gt[...], wt[...], sender[:, part], receiver[:, part], feature[:, part], lane < live[0, q]
-        )
-    out[...] = value
-
-
-def far_kernel(live, rows, receiver, feature, wst, rt, gt, wt, total, out):
-    part = pl.ds(NG, FAR)
-    hot = one_hot(NODES, receiver[:, part])
-    pre = nt(wst[...], rows[...]) + nn(rt[...], hot) + nn(gt[...], feature_rows(feature[:, part]))
+        value = value + encode_block(q, table, rt[...], gt[...], wt[...], sender, receiver, feature, live[0, q])
+    out[...] = total[...] + value
+
+
+def far_kernel(live, receiver, feature, rt, gt, wst, rows, wt, total, out):
+    part = slice(NG, NG + FAR)
+    hot = one_hot(NODES, receiver[part].reshape(1, FAR))
+    pre = nn(rt[...], hot) + nn(gt[...], feature_rows(feature[:, part])) + nt(wst[...], rows[...])
     message = messages_t(pre, wt[...], far_live(live, FAR, 0))
     out[...] = (total[...] + nt(hot, message)).astype(BF)
 
@@ -197,39 +228,39 @@
     return (edge.astype(F32) + value * gain).astype(BF)
 
 
-def near_kernel(
-    live, before, mid, after, edge, sender, receiver, w_edge, w_send, w_recv, w_out, gain, out, total, wet, wst, pt, wt
-):
+def prepare_kernel(w_edge, edge, w_send, w_recv, w_out, near, far, wst, wrt, wt):
     eye = identity(D)
-    wet[...] = (0.5 * nt(eye, w_edge[...])).astype(BF)
+    wet = (0.5 * nt(eye, w_edge[...])).astype(BF)
+    near[...] = nt(wet, edge[:NM_PAD, :]).astype(BF)
+    far[...] = nt(wet, edge[NM:, :]).astype(BF)
     wst[...] = (0.5 * nt(eye, w_send[...])).astype(BF)
-    wrt = (0.5 * nt(eye, w_recv[...])).astype(BF)
+    wrt[...] = (0.5 * nt(eye, w_recv[...])).astype(BF)
     wt[...] = centred_t(w_out[...])
-    pt[...] = nt(wrt, mid[...]).astype(BF)
+
+
+def near_kernel(live, wst, wrt, before, mid, after, sender, receiver, edge_pre, wt, edge, gain, out, total, pt):
+    pt[...] = nt(wrt[...], mid[...]).astype(BF)
     table = nt(wst[...], jnp.concatenate([before[...], mid[...], after[...]], axis=0)).astype(BF)
     lane = lax.broadcasted_iota(jnp.int32, (1, NM_PAD), 1)
     block = lane // NEAR_M
     count = jnp.where(block == 0, live[0, 0], jnp.where(block == 1, live[0, 1], live[0, 2]))
     mask = (lane - block * NEAR_M < count) & (lane < NM)
-    part = pl.ds(0, NM_PAD)
-    hot = one_hot(NODES, receiver[:, part])
-    edges = edge[:NM_PAD, :]
-    index = jnp.where(lane < NM, sender[:, part] + block * NODES, -1)
-    pre = nt(wet[...], edges) + nn(table, one_hot(3 * NODES, index)) + nn(pt[...], hot)
+    hot = one_hot(NODES, receiver[:NM_PAD].reshape(1, NM_PAD))
+    index = jnp.where(lane < NM, sender[:NM_PAD].reshape(1, NM_PAD) + block * NODES, -1)
+    pre = edge_pre[...].astype(F32) + nn(table, one_hot(3 * NODES, index)) + nn(pt[...], hot)
     message = messages_t(pre, wt[...], mask)
     total[...] = nt(hot, message)
-    out[:NM, :] = rows_out(message, edges, gain[...])[:NM, :]
-
-
-def last_kernel(live, rows, edge, receiver, wet, wst, pt, wt, gain, total, edge_out, out, partial, held, sem):
-    hot = one_hot(NODES, receiver[:, NM:M2M])
-    edges = edge[NM:, :]
-    pre = nt(wet[...], edges) + nt(wst[...], rows[...]) + nn(pt[...], hot)
+    out[:NM, :] = rows_out(message, edge[:NM_PAD, :], gain[...])[:NM, :]
+
+
+def last_kernel(live, receiver, pt, edge_pre, wst, rows, wt, total, edge, gain, edge_out, out, partial, held, sem):
+    hot = one_hot(NODES, receiver[NM:].reshape(1, FAR))
+    pre = edge_pre[...].astype(F32) + nn(pt[...], hot) + nt(wst[...], rows[...])
     message = messages_t(pre, wt[...], far_live(live, FAR, 0))
-    partial[...] = (total[...] + nt(hot, message)).astype(BF)
-    held[...] = rows_out(message, edges, gain[...])
+    held[...] = rows_out(message, edge[NM:, :], gain[...])
     copy = pltpu.make_async_copy(held, out.at[pl.ds(NM, FAR), :], sem)
     copy.start()
+    partial[...] = (total[...] + nt(hot, message)).astype(BF)
     copy.wait()
 
 
@@ -288,87 +319,93 @@
     )
     asked = exchange(asks)
     before, after = halo(grid_latent)
-    sender = encode_sender.reshape(1, -1)
-    receiver = encode_receiver.reshape(1, -1)
     gains = [g.reshape(1, D) for g in (grid_gain, encode_gain, node_gain, process_gain, update_gain)]
 
     weight = shape((D, D), BF)
     total, wst, rt, gt, wt = call(
         own_kernel,
         (shape((NODES, D), F32), weight, shape((D, NODES), BF), shape((D, 16), BF), weight),
-        [SMEM] + [VMEM] * 9,
-        (encode_live, grid_latent, mesh_latent, sender, receiver, encode_feature)
-        + (encode_send, encode_receive, encode_geometry, encode_output),
+        "SHHHHHHHHH",
+        (encode_live, encode_send, grid_latent, encode_receive, mesh_latent, encode_geometry, encode_output)
+        + (encode_sender, encode_receiver, encode_feature),
         flops=8 * 10**9,
         name="encode_own",
     )
     outgoing = call(
-        send_kernel, shape((FAR, D), BF), [VMEM] * 2, (asked, grid_latent), flops=3 * 10**8, name="encode_rows"
+        send_kernel, shape((FAR, D), BF), "VH", (asked, grid_latent), flops=3 * 10**8, name="encode_rows"
     )
     far_rows = exchange(outgoing.reshape(N_REG, FAR_G, D)).reshape(FAR, D)
     total = call(
         sides_kernel,
         shape((NODES, D), F32),
-        [SMEM] + [VMEM] * 10,
-        (encode_live, before, after, sender, receiver, encode_feature, wst, rt, gt, wt, total),
+        "SAAHHHAAAAA",
+        (encode_live, before, wst, encode_sender, encode_receiver, encode_feature, rt, gt, wt, after, total),
         flops=11 * 10**9,
         name="encode_sides",
     )
     partial = call(
         far_kernel,
         shape((NODES, D), BF),
-        [SMEM] + [VMEM] * 8,
-        (encode_live, far_rows, receiver, encode_feature, wst, rt, gt, wt, total),
+        "SHHAAAAAA",
+        (encode_live, encode_receiver, encode_feature, rt, gt, wst, far_rows, wt, total),
         flops=10**9,
         name="encode_far",
     )
-    partial, grid_rows = lax.optimization_barrier((partial, grid_latent))
+    partial, later_edge = lax.optimization_barrier((partial, mesh_edge))
     parts = band_parts(partial)
-    grid_out = call(
-        grid_kernel,
-        shape((GRID, D), BF),
-        [VMEM] * 4,
-        (grid_rows, grid_first, grid_second, gains[0]),
+    near_pre, far_pre, p_wst, p_wrt, p_wt = call(
+        prepare_kernel,
+        (shape((D, NM_PAD), BF), shape((D, FAR), BF), weight, weight, weight),
+        "HHHHH",
+        (process_edge, later_edge, process_send, process_receive, process_output),
         flops=3 * 10**9,
-        name="grid_nodes",
+        name="process_prepare",
     )
     mid, rows = call(
         node_kernel,
         (shape((NODES, D), BF), shape((FAR, D), BF)),
-        [VMEM] * 10,
+        "VHAAAAHHHH",
         (asked, mesh_latent, *parts, gains[1], node_first, node_second, gains[2]),
         flops=10**9,
         name="mesh_nodes",
     )
     far_mesh = exchange(rows.reshape(N_REG, FAR_M, D)).reshape(FAR, D)
     before_mid, after_mid = halo(mid)
-    m_sender = mesh_sender.reshape(1, -1)
-    m_receiver = mesh_receiver.reshape(1, -1)
-    edge_near, m_total, wet, wst, pt, wt = call(
+    edge_near, m_total, pt = call(
         near_kernel,
-        (shape((M2M, D), BF), shape((NODES, D), F32), weight, weight, shape((D, NODES), BF), weight),
-        [SMEM] + [VMEM] * 11,
-        (mesh_live, before_mid, mid, after_mid, mesh_edge, m_sender, m_receiver)
-        + (process_edge, process_send, process_receive, process_output, gains[3]),
-        flops=6 * 10**9,
+        (shape((M2M, D), BF), shape((NODES, D), F32), shape((D, NODES), BF)),
+        "SAAAAAHHAAHH",
+        (mesh_live, p_wst, p_wrt, before_mid, mid, after_mid, mesh_sender, mesh_receiver, near_pre, p_wt)
+        + (mesh_edge, gains[3]),
+        flops=4 * 10**9,
         name="process_near",
     )
     edge_out, m_partial = call(
         last_kernel,
         (shape((M2M, D), BF), shape((NODES, D), BF)),
-        [SMEM] + [VMEM] * 9 + [ANY],
-        (mesh_live, far_mesh, mesh_edge, m_receiver, wet, wst, pt, wt, gains[3], m_total, edge_near),
+        "SHAAAAAAHHR",
+        (mesh_live, mesh_receiver, pt, far_pre, p_wst, far_mesh, p_wt, m_total, mesh_edge, gains[3], edge_near),
         scratch=[pltpu.VMEM((FAR, D), BF), pltpu.SemaphoreType.DMA],
         out_specs=(ANY, VMEM),
         flops=10**9,
         name="process_far",
         aliases={10: 0},
     )
+    m_partial, grid_rows = lax.optimization_barrier((m_partial, grid_latent))
+    m_parts = band_parts(m_partial)
+    grid_out = call(
+        grid_kernel,
+        shape((GRID, D), BF),
+        "HHHH",
+        (grid_rows, grid_first, grid_second, gains[0]),
+        flops=3 * 10**9,
+        name="grid_nodes",
+    )
     mesh_out = call(
         update_kernel,
         shape((NODES, D), BF),
-        [VMEM] * 9,
-        (mid, *band_parts(m_partial), gains[3], update_first, update_second, gains[4]),
+        "AAAAAHHHH",
+        (mid, *m_parts, gains[3], update_first, update_second, gains[4]),
         flops=10**9,
         name="mesh_update",
     )

time: 142 us -> 151 us (1.063)
  Pallas kernels: 43.7 us -> 52.9 us
  waiting for transfers between devices: 19.2 us -> 23.6 us
  local copies, waits for them, and re-layouts: 38.6 us -> 34.6 us
    pallas_call x9 -> x10, Pallas kernels: 43.7 us -> 52.9 us  [call(): pl.pallas_call(body, out_shape=outs, in_specs=[place[spec] for spec in sp...]
    ppermute x6, waiting for transfers between devices: 19.1 us -> 23.6 us  [band_parts(): lax.ppermute(partial, 'band', [(i, (i + k) % count) for i in range(count)])]
    ppermute x6, starting transfers between devices: 11.5 us -> 7.74 us  [band_parts(): lax.ppermute(partial, 'band', [(i, (i + k) % count) for i in range(count)])]
    all_to_all x3, starting transfers between devices: 15.6 us -> 18.4 us  [exchange(): return lax.all_to_all(x, 'region', split_axis=0, concat_axis=0, tiled=True)]
    unnamed x120 -> x122, local copies, waits for them, and re-layouts: 35.5 us -> 33 us
    reshape x2 -> x0, local copies, waits for them, and re-layouts: 1.54 us -> none  [the longest x1 0.77 us: on_device(): sender = encode_sender.reshape(1, -1)]
  transfers between devices with their start and end apart: 13 -> 13, of which waited for: 6 -> 5; matrix products, arithmetic and copies ran while one was open for 3% -> 2% of each run, Pallas kernels for 25% -> 28%
where the time goes in v2:
time: 151 us; the launch traced here: 149 us
  Pallas kernels  52.9 us (35%)
  starting transfers between devices  35.9 us (24%)
  local copies, waits for them, and re-layouts  34.6 us (23%)
  waiting for transfers between devices  23.6 us (16%)
    pallas_call x10, Pallas kernels, call(): pl.pallas_call(body, out_shape=outs, in_specs=[place[spec] for spec in sp...  52.9 us
    unnamed x122, local copies, waits for them, and re-layouts  33 us
    ppermute x6, waiting for transfers between devices, band_parts(): lax.ppermute(partial, 'band', [(i, (i + k) % count) for i in range(count)])  23.6 us
    all_to_all x3, starting transfers between devices, exchange(): return lax.all_to_all(x, 'region', split_axis=0, concat_axis=0, tiled=True)  18.4 us
    ppermute x4, starting transfers between devices, halo(): return (lax.ppermute(x, 'region', up), lax.ppermute(x, 'region', down))  9.8 us
    ppermute x6, starting transfers between devices, band_parts(): lax.ppermute(partial, 'band', [(i, (i + k) % count) for i in range(count)])  7.74 us
  transfers between devices with their start and end apart: 13, of which 5 were waited for; matrix products, arithmetic and copies ran while one was open for 2% of the time, Pallas kernels for 28%

profile of v2, /device:TPU:0, one launch (start us, length us, event | category | flops | bytes accessed | tf_op | source)
XLA Modules:
  0.0 148.9 jit_solution(12300577841192432485)
XLA Ops:
  0.7 5.1 %collective-permute-start.1 = (bf16[1024,512]{1,0:T(8,128)(2,1)}, bf16[1024,512]{1,0:T(8,128)(2,1)}, u32[]{:S(2)}, u32[]{:S(2)}) collective-permute-start(bf16[1024,512]{1,0:T(8,128)(2,1)} %refs_0_.12), channel_id=1, source_target_pairs={{1,0},{2,1},{3,2},{4,3},{5,4},{6,5},{7,6},{8,7},{9,8},{10,9},{11,1... | collective-permute-start | bytes 3145736 | tf_op jit(solution)/shard_map/ppermute | solution.py:279
  8.1 4.1 %all-to-all-start = ((s32[32,1,16]{2,1,0:T(1,128)}), s32[32,1,16]{2,1,0:T(1,128)S(1)}, u32[]{:S(2)}, u32[]{:S(2)}) async-start(s32[32,1,16]{2,1,0:T(1,128)} %bitcast.1), calls=%async_computation | async-start | bytes 32768 | tf_op jit(solution)/shard_map/all_to_all | solution.py:283
  21.2 9.6 %encode_own.1 = (f32[256,512]{1,0:T(8,128)S(1)}, bf16[512,512]{1,0:T(8,128)(2,1)S(1)}, bf16[512,256]{1,0:T(8,128)(2,1)S(1)}, bf16[512,16]{1,0:T(8,128)(2,1)S(1)}, bf16[512,512]{1,0:T(8,128)(2,1)S(1)}) custom-call(s32[1,35]{1,0:T(1,128)S(1)} %copy-done.46, bf16[512,512]{1,0:T(8,128)(2,1)S(1)} %copy-done.24, bf16[1024,512]{1,0:T(8,128)(2,1)S(1)} %copy-done.1, ...), custom_call_target="tpu_custom_call" | custom-call | flops 8000000000 | bytes 1048576 | tf_op jit(solution)/shard_map/encode_own/pallas_call | solution.py:107
  32.4 1.6 %encode_rows.1 = bf16[256,512]{1,0:T(8,128)(2,1)} custom-call(s32[32,16]{1,0:T(8,128)S(1)} %bitcast.16, bf16[1024,512]{1,0:T(8,128)(2,1)S(1)} %copy-done.2), custom_call_target="tpu_custom_call" | custom-call | flops 300000000 | bytes 1048576 | tf_op jit(solution)/shard_map/encode_rows/pallas_call | solution.py:107
  34.0 7.6 %all-to-all-start.1 = ((bf16[32,8,512]{2,1,0:T(8,128)(2,1)}), bf16[32,8,512]{2,1,0:T(8,128)(2,1)S(1)}, u32[]{:S(2)}, u32[]{:S(2)}) async-start(bf16[32,8,512]{2,1,0:T(8,128)(2,1)} %bitcast.3), calls=%async_computation.1 | async-start | bytes 524288 | tf_op jit(solution)/shard_map/all_to_all | solution.py:283
  43.7 13.3 %encode_sides.1.refs_8_ = f32[256,512]{1,0:T(8,128)S(1)} custom-call(s32[1,35]{1,0:T(1,128)S(1)} %copy-done.47, bf16[1024,512]{1,0:T(8,128)(2,1)S(1)} %collective-permute-done.refs_1_, bf16[512,512]{1,0:T(8,128)(2,1)S(1)} %get-tuple-element.26.refs_2_.refs_5_, s32[6400]{0:T(1024)S(1)} %copy-done.21, s32[6400]{0:T(1024)S(1)} %copy-done.40, ...), custom_call_target="tpu_custom_call" | custom-call | flops 11000000512 | bytes 1048576 | tf_op jit(solution)/shard_map/encode_sides/pallas_call | solution.py:107
  61.0 2.6 %encode_far.1.refs_2_ = bf16[256,512]{1,0:T(8,128)(2,1)S(1)} custom-call(s32[1,35]{1,0:T(1,128)S(1)} %copy-done.47, s32[6400]{0:T(1024)S(1)} %copy-done.40, f32[4,6400]{1,0:T(4,128)S(1)} %copy-done.38, bf16[512,256]{1,0:T(8,128)(2,1)S(1)} %copy-done.54, bf16[512,16]{1,0:T(8,128)(2,1)S(1)} %get-tuple-element.25.refs_7_.refs_4_, ...), custom_call_target="tpu_custom_call" | custom-call | flops 1000000000 | bytes 1048576 | tf_op jit(solution)/shard_map/encode_far/pallas_call | solution.py:107
  63.7 4.1 %collective-permute-start.4 = (bf16[256,512]{1,0:T(8,128)(2,1)S(1)}, bf16[256,512]{1,0:T(8,128)(2,1)S(1)}, u32[]{:S(2)}, u32[]{:S(2)}) collective-permute-start(bf16[256,512]{1,0:T(8,128)(2,1)S(1)} %encode_far.1.refs_2_), channel_id=1, source_target_pairs={{0,96},{32,0},{64,32},{96,64},{1,97},{33,1},{65,33},{97,65},{2,98}... | collective-permute-start | bytes 786440 | tf_op jit(solution)/shard_map/ppermute | solution.py:270
  67.8 1.3 collective-permute-start.2
  69.1 10.2 %collective-permute-done.4.refs_5_ = bf16[256,512]{1,0:T(8,128)(2,1)S(1)} collective-permute-done((bf16[256,512]{1,0:T(8,128)(2,1)S(1)}, bf16[256,512]{1,0:T(8,128)(2,1)S(1)}, u32[]{:S(2)}, u32[]{:S(2)}) %collective-permute-start.4) | collective-permute-done | bytes 262176 | tf_op jit(solution)/shard_map/ppermute | solution.py:270
  79.2 3.4 %collective-permute-done.2.refs_3_ = bf16[256,512]{1,0:T(8,128)(2,1)S(1)} collective-permute-done((bf16[256,512]{1,0:T(8,128)(2,1)S(1)}, bf16[256,512]{1,0:T(8,128)(2,1)S(1)}, u32[]{:S(2)}, u32[]{:S(2)}) %collective-permute-start.2) | collective-permute-done | bytes 262176 | tf_op jit(solution)/shard_map/ppermute | solution.py:270
  82.7 2.5 %mesh_nodes.1 = (bf16[256,512]{1,0:T(8,128)(2,1)}, bf16[256,512]{1,0:T(8,128)(2,1)S(1)}) custom-call(s32[32,16]{1,0:T(8,128)S(1)} %bitcast.17, bf16[256,512]{1,0:T(8,128)(2,1)S(1)} %copy-done.36, bf16[256,512]{1,0:T(8,128)(2,1)S(1)} %encode_far.1.refs_2_, bf16[256,512]{1,0:T(8,128)(2,1)S(1)} %collective-permute-done.2.refs_3_, ...), custom_call_target="tpu_custom_call" | custom-call | flops 1000000000 | bytes 1048576 | tf_op jit(solution)/shard_map/mesh_nodes/pallas_call | solution.py:107
  85.9 4.7 %collective-permute-start.6 = (bf16[256,512]{1,0:T(8,128)(2,1)}, bf16[256,512]{1,0:T(8,128)(2,1)}, u32[]{:S(2)}, u32[]{:S(2)}) collective-permute-start(bf16[256,512]{1,0:T(8,128)(2,1)} %get-tuple-element.33.refs_4_.refs_0_), channel_id=1, source_target_pairs={{1,0},{2,1},{3,2},{4,3},{5,4},{6,5},{7,6},{8,7},{9,8},{10,9},{11,1... | collective-permute-start | bytes 786440 | tf_op jit(solution)/shard_map/ppermute | solution.py:279
  90.6 3.9 %process_prepare.1 = (bf16[512,1792]{1,0:T(8,128)(2,1)S(1)}, bf16[512,256]{1,0:T(8,128)(2,1)S(1)}, bf16[512,512]{1,0:T(8,128)(2,1)S(1)}, bf16[512,512]{1,0:T(8,128)(2,1)S(1)}, bf16[512,512]{1,0:T(8,128)(2,1)S(1)}) custom-call(bf16[512,512]{1,0:T(8,128)(2,1)S(1)} %copy-done.28, bf16[1984,512]{1,0:T(8,128)(2,1)S(1)} %copy-done, ...), custom_call_target="tpu_custom_call" | custom-call | flops 3000000000 | bytes 1048576 | tf_op jit(solution)/shard_map/process_prepare/pallas_call | solution.py:107
  98.9 6.7 %all-to-all-start.2 = ((bf16[32,8,512]{2,1,0:T(8,128)(2,1)}), bf16[32,8,512]{2,1,0:T(8,128)(2,1)S(1)}, u32[]{:S(2)}, u32[]{:S(2)}) async-start(bf16[32,8,512]{2,1,0:T(8,128)(2,1)} %bitcast.14), calls=%async_computation.2 | async-start | bytes 524288 | tf_op jit(solution)/shard_map/all_to_all | solution.py:283
  107.8 1.5 %copy-done.56 = bf16[512,1792]{1,0:T(8,128)(2,1)S(1)} copy-done((bf16[512,1792]{1,0:T(8,128)(2,1)S(1)}, bf16[512,1792]{1,0:T(8,128)(2,1)}, u32[]{:S(2)}) %copy-start.56) | copy-done | bytes 1835032
  110.3 9.5 %process_near.1 = (bf16[1984,512]{1,0:T(8,128)(2,1)}, f32[256,512]{1,0:T(8,128)S(1)}, bf16[512,256]{1,0:T(8,128)(2,1)S(1)}) custom-call(s32[1,35]{1,0:T(1,128)S(1)} %copy-done.18, bf16[512,512]{1,0:T(8,128)(2,1)S(1)} %copy-done.4, bf16[512,512]{1,0:T(8,128)(2,1)S(1)} %copy-done.58, bf16[256,512]{1,0:T(8,128)(2,1)} %collective-permute-done.5.refs_3_, ...), custom_call_target="tpu_custom_call" | custom-call | flops 4000000000 | bytes 1048576 | tf_op jit(solution)/shard_map/process_near/pallas_call | solution.py:107
  126.4 3.5 %process_far.1 = (bf16[1984,512]{1,0:T(8,128)(2,1)}, bf16[256,512]{1,0:T(8,128)(2,1)S(1)}) custom-call(s32[1,35]{1,0:T(1,128)S(1)} %copy-done.18, s32[1984]{0:T(1024)S(1)} %copy-done.16, bf16[512,256]{1,0:T(8,128)(2,1)S(1)} %copy-done.14, bf16[512,256]{1,0:T(8,128)(2,1)S(1)} %copy-done.12, ...), custom_call_target="tpu_custom_call", output_to_operand_aliasing={{0}: (10, {})} | custom-call | flops 1000000000 | bytes 1048576 | tf_op jit(solution)/shard_map/process_far/pallas_call | solution.py:107
  130.9 1.3 collective-permute-start.7
  132.3 3.4 %grid_nodes.1 = bf16[1024,512]{1,0:T(8,128)(2,1)} custom-call(bf16[1024,512]{1,0:T(8,128)(2,1)S(1)} %copy-done.2, bf16[512,512]{1,0:T(8,128)(2,1)S(1)} %copy-done.32, bf16[512,512]{1,0:T(8,128)(2,1)S(1)} %copy-done.33, f32[1,512]{1,0:T(1,128)S(1)} %bitcast.23), custom_call_target="tpu_custom_call" | custom-call | flops 3000000000 | bytes 1048576 | tf_op jit(solution)/shard_map/grid_nodes/pallas_call | solution.py:107
  135.7 3.4 %collective-permute-done.9.refs_4_ = bf16[256,512]{1,0:T(8,128)(2,1)S(1)} collective-permute-done((bf16[256,512]{1,0:T(8,128)(2,1)S(1)}, bf16[256,512]{1,0:T(8,128)(2,1)S(1)}, u32[]{:S(2)}, u32[]{:S(2)}) %collective-permute-start.9) | collective-permute-done | bytes 262176 | tf_op jit(solution)/shard_map/ppermute | solution.py:270
  139.1 1.8 %collective-permute-done.8.refs_3_ = bf16[256,512]{1,0:T(8,128)(2,1)S(1)} collective-permute-done((bf16[256,512]{1,0:T(8,128)(2,1)S(1)}, bf16[256,512]{1,0:T(8,128)(2,1)S(1)}, u32[]{:S(2)}, u32[]{:S(2)}) %collective-permute-start.8) | collective-permute-done | bytes 262176 | tf_op jit(solution)/shard_map/ppermute | solution.py:270
  140.9 4.8 %collective-permute-done.7.refs_2_ = bf16[256,512]{1,0:T(8,128)(2,1)S(1)} collective-permute-done((bf16[256,512]{1,0:T(8,128)(2,1)S(1)}, bf16[256,512]{1,0:T(8,128)(2,1)S(1)}, u32[]{:S(2)}, u32[]{:S(2)}) %collective-permute-start.7) | collective-permute-done | bytes 262176 | tf_op jit(solution)/shard_map/ppermute | solution.py:270
  145.7 3.1 %mesh_update.1 = bf16[256,512]{1,0:T(8,128)(2,1)} custom-call(bf16[256,512]{1,0:T(8,128)(2,1)} %get-tuple-element.33.refs_4_.refs_0_, bf16[256,512]{1,0:T(8,128)(2,1)S(1)} %get-tuple-element.43.refs_1_, bf16[256,512]{1,0:T(8,128)(2,1)S(1)} %collective-permute-done.7.refs_2_, bf16[256,512]{1,0:T(8,128)(2,1)S(1)} %collective-permute-done.8.refs_3_, ...), custom_call_target="tpu_custom_call" | custom-call | flops 1000000000 | bytes 1048576 | tf_op jit(solution)/shard_map/mesh_update/pallas_call | solution.py:107
  (139 shorter events, 34.9 us)
Async XLA Ops:
  0.6 40.9 %collective-permute-start = (bf16[1024,512]{1,0:T(8,128)(2,1)}, bf16[1024,512]{1,0:T(8,128)(2,1)S(1)}, u32[]{:S(2)}, u32[]{:S(2)}) collective-permute-start(bf16[1024,512]{1,0:T(8,128)(2,1)} %refs_0_.12), channel_id=1, source_target_pairs={{0,1},{1,2},{2,3},{3,4},{4,5},{5,6},{6,7},{7,8},{8,9},{9,10},{10,1... | collective-permute-start | bytes 3145736 | tf_op jit(solution)/shard_map/ppermute | solution.py:279
  0.7 40.8 %collective-permute-start.1 = (bf16[1024,512]{1,0:T(8,128)(2,1)}, bf16[1024,512]{1,0:T(8,128)(2,1)}, u32[]{:S(2)}, u32[]{:S(2)}) collective-permute-start(bf16[1024,512]{1,0:T(8,128)(2,1)} %refs_0_.12), channel_id=1, source_target_pairs={{1,0},{2,1},{3,2},{4,3},{5,4},{6,5},{7,6},{8,7},{9,8},{10,9},{11,1... | collective-permute-start | bytes 3145736 | tf_op jit(solution)/shard_map/ppermute | solution.py:279
  8.1 24.3 %all-to-all-start = ((s32[32,1,16]{2,1,0:T(1,128)}), s32[32,1,16]{2,1,0:T(1,128)S(1)}, u32[]{:S(2)}, u32[]{:S(2)}) async-start(s32[32,1,16]{2,1,0:T(1,128)} %bitcast.1), calls=%async_computation | async-start | bytes 32768 | tf_op jit(solution)/shard_map/all_to_all | solution.py:283
  21.2 20.4 %copy-start.47 = (s32[1,35]{1,0:T(1,128)S(1)}, s32[1,35]{1,0:T(1,128)}, u32[]{:S(2)}) copy-start(s32[1,35]{1,0:T(1,128)} %refs_0_.8) | copy-start | bytes 424
  34.0 23.8 %all-to-all-start.1 = ((bf16[32,8,512]{2,1,0:T(8,128)(2,1)}), bf16[32,8,512]{2,1,0:T(8,128)(2,1)S(1)}, u32[]{:S(2)}, u32[]{:S(2)}) async-start(bf16[32,8,512]{2,1,0:T(8,128)(2,1)} %bitcast.3), calls=%async_computation.1 | async-start | bytes 524288 | tf_op jit(solution)/shard_map/all_to_all | solution.py:283
  57.8 24.9 %copy-start.36 = (bf16[256,512]{1,0:T(8,128)(2,1)S(1)}, bf16[256,512]{1,0:T(8,128)(2,1)}, u32[]{:S(2)}) copy-start(bf16[256,512]{1,0:T(8,128)(2,1)} %refs_1_.10) | copy-start | bytes 786436
  57.8 24.9 %copy-start.42 = (f32[512]{0:T(512)S(1)}, f32[512]{0:T(512)}, u32[]{:S(2)}) copy-start(f32[512]{0:T(512)} %param.46) | copy-start | bytes 6148
  57.8 24.9 %copy-start.43 = (f32[512]{0:T(512)S(1)}, f32[512]{0:T(512)}, u32[]{:S(2)}) copy-start(f32[512]{0:T(512)} %param.49) | copy-start | bytes 6148
  57.8 24.9 %copy-start.22 = (bf16[1024,512]{1,0:T(8,128)(2,1)S(1)}, bf16[1024,512]{1,0:T(8,128)(2,1)}, u32[]{:S(2)}) copy-start(bf16[1024,512]{1,0:T(8,128)(2,1)} %refs_7_.5) | copy-start | bytes 3145732
  57.8 24.9 %copy-start.27 = (bf16[512,512]{1,0:T(8,128)(2,1)S(1)}, bf16[512,512]{1,0:T(8,128)(2,1)}, u32[]{:S(2)}) copy-start(bf16[512,512]{1,0:T(8,128)(2,1)} %refs_8_.4) | copy-start | bytes 1572868
  61.0 29.6 %copy-start.31 = (bf16[512,512]{1,0:T(8,128)(2,1)S(1)}, bf16[512,512]{1,0:T(8,128)(2,1)}, u32[]{:S(2)}) copy-start(bf16[512,512]{1,0:T(8,128)(2,1)} %refs_4_.5) | copy-start | bytes 1572868
  63.6 26.9 %copy-start = (bf16[1984,512]{1,0:T(8,128)(2,1)S(1)}, bf16[1984,512]{1,0:T(8,128)(2,1)}, u32[]{:S(2)}) copy-start(bf16[1984,512]{1,0:T(8,128)(2,1)} %refs_8_.5) | copy-start | bytes 6094852
  63.7 26.9 %copy-start.28 = (bf16[512,512]{1,0:T(8,128)(2,1)S(1)}, bf16[512,512]{1,0:T(8,128)(2,1)}, u32[]{:S(2)}) copy-start(bf16[512,512]{1,0:T(8,128)(2,1)} %refs_0_.9) | copy-start | bytes 1572868
  63.7 26.9 %copy-start.29 = (bf16[512,512]{1,0:T(8,128)(2,1)S(1)}, bf16[512,512]{1,0:T(8,128)(2,1)}, u32[]{:S(2)}) copy-start(bf16[512,512]{1,0:T(8,128)(2,1)} %refs_2_.6) | copy-start | bytes 1572868
  63.7 26.9 %copy-start.30 = (bf16[512,512]{1,0:T(8,128)(2,1)S(1)}, bf16[512,512]{1,0:T(8,128)(2,1)}, u32[]{:S(2)}) copy-start(bf16[512,512]{1,0:T(8,128)(2,1)} %refs_3_.5) | copy-start | bytes 1572868
  63.7 15.5 %collective-permute-start.4 = (bf16[256,512]{1,0:T(8,128)(2,1)S(1)}, bf16[256,512]{1,0:T(8,128)(2,1)S(1)}, u32[]{:S(2)}, u32[]{:S(2)}) collective-permute-start(bf16[256,512]{1,0:T(8,128)(2,1)S(1)} %encode_far.1.refs_2_), channel_id=1, source_target_pairs={{0,96},{32,0},{64,32},{96,64},{1,97},{33,1},{65,33},{97,65},{2,98}... | collective-permute-start | bytes 786440 | tf_op jit(solution)/shard_map/ppermute | solution.py:270
  67.8 11.4 %collective-permute-start.3 = (bf16[256,512]{1,0:T(8,128)(2,1)S(1)}, bf16[256,512]{1,0:T(8,128)(2,1)S(1)}, u32[]{:S(2)}, u32[]{:S(2)}) collective-permute-start(bf16[256,512]{1,0:T(8,128)(2,1)S(1)} %encode_far.1.refs_2_), channel_id=1, source_target_pairs={{0,64},{32,96},{64,0},{96,32},{1,65},{33,97},{65,1},{97,33},{2,66}... | collective-permute-start | bytes 786440 | tf_op jit(solution)/shard_map/ppermute | solution.py:270
  67.8 14.9 %collective-permute-start.2 = (bf16[256,512]{1,0:T(8,128)(2,1)S(1)}, bf16[256,512]{1,0:T(8,128)(2,1)S(1)}, u32[]{:S(2)}, u32[]{:S(2)}) collective-permute-start(bf16[256,512]{1,0:T(8,128)(2,1)S(1)} %encode_far.1.refs_2_), channel_id=1, source_target_pairs={{0,32},{32,64},{64,96},{96,0},{1,33},{33,65},{65,97},{97,1},{2,34}... | collective-permute-start | bytes 786440 | tf_op jit(solution)/shard_map/ppermute | solution.py:270
  85.9 19.8 %collective-permute-start.6 = (bf16[256,512]{1,0:T(8,128)(2,1)}, bf16[256,512]{1,0:T(8,128)(2,1)}, u32[]{:S(2)}, u32[]{:S(2)}) collective-permute-start(bf16[256,512]{1,0:T(8,128)(2,1)} %get-tuple-element.33.refs_4_.refs_0_), channel_id=1, source_target_pairs={{1,0},{2,1},{3,2},{4,3},{5,4},{6,5},{7,6},{8,7},{9,8},{10,9},{11,1... | collective-permute-start | bytes 786440 | tf_op jit(solution)/shard_map/ppermute | solution.py:279
  90.5 15.1 %collective-permute-start.5 = (bf16[256,512]{1,0:T(8,128)(2,1)}, bf16[256,512]{1,0:T(8,128)(2,1)}, u32[]{:S(2)}, u32[]{:S(2)}) collective-permute-start(bf16[256,512]{1,0:T(8,128)(2,1)} %get-tuple-element.33.refs_4_.refs_0_), channel_id=1, source_target_pairs={{0,1},{1,2},{2,3},{3,4},{4,5},{5,6},{6,7},{7,8},{8,9},{9,10},{10,1... | collective-permute-start | bytes 786440 | tf_op jit(solution)/shard_map/ppermute | solution.py:279
  98.9 22.4 %all-to-all-start.2 = ((bf16[32,8,512]{2,1,0:T(8,128)(2,1)}), bf16[32,8,512]{2,1,0:T(8,128)(2,1)S(1)}, u32[]{:S(2)}, u32[]{:S(2)}) async-start(bf16[32,8,512]{2,1,0:T(8,128)(2,1)} %bitcast.14), calls=%async_computation.2 | async-start | bytes 524288 | tf_op jit(solution)/shard_map/all_to_all | solution.py:283
  129.9 9.2 %collective-permute-start.9 = (bf16[256,512]{1,0:T(8,128)(2,1)S(1)}, bf16[256,512]{1,0:T(8,128)(2,1)S(1)}, u32[]{:S(2)}, u32[]{:S(2)}) collective-permute-start(bf16[256,512]{1,0:T(8,128)(2,1)S(1)} %get-tuple-element.43.refs_1_), channel_id=1, source_target_pairs={{0,96},{32,0},{64,32},{96,64},{1,97},{33,1},{65,33},{97,65},{2,98}... | collective-permute-start | bytes 786440 | tf_op jit(solution)/shard_map/ppermute | solution.py:270
  130.2 10.7 %collective-permute-start.8 = (bf16[256,512]{1,0:T(8,128)(2,1)S(1)}, bf16[256,512]{1,0:T(8,128)(2,1)S(1)}, u32[]{:S(2)}, u32[]{:S(2)}) collective-permute-start(bf16[256,512]{1,0:T(8,128)(2,1)S(1)} %get-tuple-element.43.refs_1_), channel_id=1, source_target_pairs={{0,64},{32,96},{64,0},{96,32},{1,65},{33,97},{65,1},{97,33},{2,66}... | collective-permute-start | bytes 786440 | tf_op jit(solution)/shard_map/ppermute | solution.py:270
  130.9 14.7 %collective-permute-start.7 = (bf16[256,512]{1,0:T(8,128)(2,1)S(1)}, bf16[256,512]{1,0:T(8,128)(2,1)S(1)}, u32[]{:S(2)}, u32[]{:S(2)}) collective-permute-start(bf16[256,512]{1,0:T(8,128)(2,1)S(1)} %get-tuple-element.43.refs_1_), channel_id=1, source_target_pairs={{0,32},{32,64},{64,96},{96,0},{1,33},{33,65},{65,97},{97,1},{2,34}... | collective-permute-start | bytes 786440 | tf_op jit(solution)/shard_map/ppermute | solution.py:270
  (50 other events, 251.5 us)

commit v3 on v2

--- a/solution.py
+++ b/solution.py
@@ -19,7 +19,7 @@
 FAR = N_REG * FAR_G
 NG = 3 * NEAR_G
 NM = 3 * NEAR_M
-NM_PAD = 1792
+NM_PAD = 640
 M2M = NM + FAR
 BF = jnp.bfloat16
 F32 = jnp.float32
@@ -88,39 +88,59 @@
 
 
 def call(kernel, outs, specs, args, scratch=(), out_specs=None, flops=0, name=None, aliases=None, grant=24):
-    late = [i for i, spec in enumerate(specs) if spec in "HA"]
-    place = {"S": SMEM, "V": VMEM, "H": HBM, "A": ANY, "R": ANY}
-    n_in, n_out = len(args), len(jax.tree.leaves(outs))
+    outs = jax.tree.leaves(outs)
+    scratch_in = [i for i, spec in enumerate(specs) if spec in "SHF"]
+    keep = [i for i, spec in enumerate(specs) if spec == "K"]
+    late = scratch_in + keep
+    n_in, n_out, n_keep = len(args), len(outs), len(keep)
+    place = {"S": HBM, "H": HBM, "K": HBM, "F": HBM, "V": VMEM, "R": ANY}
+    pin = {"S": pltpu.HBM, "H": pltpu.HBM, "K": pltpu.HBM, "F": pltpu.HBM, "V": pltpu.VMEM, "R": pl.ANY}
 
     def body(*refs):
         ins, rest = list(refs[:n_in]), refs[n_in:]
-        held, sems = rest[n_out : n_out + len(late)], rest[n_out + len(late)]
-        copies = [pltpu.make_async_copy(ins[i], held[j], sems.at[j]) for j, i in enumerate(late)]
-        for j, i in enumerate(late):
-            copies[j].start()
-            ins[i] = Late(held[j], copies[j])
-        kernel(*ins, *rest[:n_out], *rest[n_out + len(late) + 1 :])
+        targets = list(rest[n_out + n_keep : n_out + n_keep + len(scratch_in)]) + list(rest[n_out : n_out + n_keep])
+        rest_scratch = rest[n_out + n_keep + len(scratch_in) :]
+        if late:
+            sems, rest_scratch = rest_scratch[0], rest_scratch[1:]
+        order = sorted(range(len(late)), key=lambda j: late[j])
+        for j in order:
+            source = ins[late[j]].at[pl.ds(NM, FAR), :] if specs[late[j]] == "F" else ins[late[j]]
+            copy = pltpu.make_async_copy(source, targets[j], sems.at[j])
+            copy.start()
+            ins[late[j]] = Late(targets[j], copy)
+        kernel(*ins, *rest[:n_out], *rest_scratch)
         for i in late:
             if ins[i].copy is not None:
                 ins[i].copy.wait()
 
-    return pl.pallas_call(
+    out_shape = outs + [pltpu.VMEM(args[i].shape, args[i].dtype) for i in keep]
+    result = pl.pallas_call(
         body,
-        out_shape=outs,
+        out_shape=out_shape,
         in_specs=[place[spec] for spec in specs],
-        out_specs=jax.tree.map(lambda _: VMEM, outs) if out_specs is None else out_specs,
-        scratch_shapes=[pltpu.VMEM(args[i].shape, args[i].dtype) for i in late]
-        + [pltpu.SemaphoreType.DMA((len(late),))]
+        out_specs=(list(out_specs) if out_specs else [VMEM] * n_out) + [VMEM] * n_keep,
+        scratch_shapes=[
+            pltpu.VMEM((FAR, D), BF)
+            if specs[i] == "F"
+            else (pltpu.SMEM if specs[i] == "S" else pltpu.VMEM)(args[i].shape, args[i].dtype)
+            for i in scratch_in
+        ]
+        + ([pltpu.SemaphoreType.DMA((len(late),))] if late else [])
         + list(scratch),
         compiler_params=pltpu.CompilerParams(vmem_limit_bytes=grant * 2**20),
         cost_estimate=pl.CostEstimate(flops=flops, bytes_accessed=2**20, transcendentals=0),
         input_output_aliases=aliases or {},
         name=name,
-    )(*args)
+    )(*[arg if spec == "R" else pltpu.with_memory_space_constraint(arg, pin[spec]) for arg, spec in zip(args, specs)])
+    return result if len(result) > 1 else result[0]
 
 
 def shape(dims, kind):
     return jax.ShapeDtypeStruct(dims, kind)
+
+
+def kept(dims, kind):
+    return pltpu.VMEM(dims, kind)
 
 
 def encode_block(q, table, rt, gt, wt, sender, receiver, feature, limit):
@@ -136,10 +156,22 @@
     return value
 
 
-def own_kernel(live, w_send, grid, w_recv, mesh, geo, w_out, sender, receiver, feature, out, wst, rt, gt, wt):
+def slots_to_rows(row, first):
+    lane = lax.broadcasted_iota(jnp.int32, (N_REG, FAR), 1)
+    mine = lane // FAR_G == lax.broadcasted_iota(jnp.int32, (N_REG, FAR), 0)
+    lane = lax.broadcasted_iota(jnp.int32, (2 * FAR_G, FAR), 1)
+    pick = (lane % FAR_G + first == lax.broadcasted_iota(jnp.int32, (2 * FAR_G, FAR), 0)).astype(F32).astype(BF)
+    high = jnp.where(mine, row // 32, 0).astype(F32).astype(BF)
+    low = jnp.where(mine, row % 32, 0).astype(F32).astype(BF)
+    return nt(high, pick) * 32.0 + nt(low, pick)
+
+
+def start_kernel(sender, m_sender, w_send, w_recv, mesh, geo, w_out, grid, receiver, feature, *rest):
+    asks, wst, rt, gt, wt = rest[:5]
+    far = slots_to_rows(sender[NG:].reshape(1, FAR), 0) + slots_to_rows(m_sender[NM:].reshape(1, FAR), FAR_G)
+    asks[...] = far.astype(jnp.int32)
     eye = identity(D)
     wst[...] = (0.5 * nt(eye, w_send[...])).astype(BF)
-    table = nt(wst[...], grid[...]).astype(BF)
     wrt = nt(eye, w_recv[...]).astype(BF)
     rt[...] = (0.5 * nt(wrt, mesh[...])).astype(BF)
     half = 0.5 * geo[...]
@@ -147,6 +179,10 @@
     stacked = jnp.concatenate([high, high, half - high, jnp.zeros((4, D), F32)], axis=0)
     gt[...] = nt(eye, stacked.astype(BF)).astype(BF)
     wt[...] = centred_t(w_out[...])
+
+
+def own_kernel(live, grid, wst, sender, receiver, feature, rt, gt, wt, out):
+    table = nt(wst[...], grid[...]).astype(BF)
     out[...] = encode_block(1, table, rt[...], gt[...], wt[...], sender, receiver, feature, live[0, 1])
 
 
@@ -205,63 +241,87 @@
     return (total * edge_gain[...]).astype(BF)
 
 
-def node_kernel(asked, mesh, p0, p1, p2, p3, edge_gain, w_first, w_second, gain, mid, rows):
+def node_kernel(asked, mesh, p0, p1, p2, p3, edge_gain, w_first, w_second, gain, wrt, mid, rows, pt):
     value = mlp(mesh[...], band_sum(p0, p1, p2, p3, edge_gain), w_first, w_second, gain)
     mid[...] = value
     rows[...] = nn(asked_hot(asked[...], FAR_G, NODES), value).astype(BF)
+    pt[...] = nt(wrt[...], value).astype(BF)
 
 
 def update_kernel(mid, p0, p1, p2, p3, edge_gain, w_first, w_second, gain, out):
     out[...] = mlp(mid[...], band_sum(p0, p1, p2, p3, edge_gain), w_first, w_second, gain)
 
 
-def grid_kernel(latent, w_first, w_second, gain, out):
+def grid_kernel(latent, w_first, w_second, gain, *rest):
+    out = rest[-1]
     rows = latent[...]
     update = norm(nn(silu(nn(rows, w_first[...])), w_second[...])) * gain[...]
     out[...] = (rows.astype(F32) + update).astype(BF)
 
 
-def rows_out(message, edge, gain):
+def rows_out(message, edge, gain, size):
+    width = message.shape[1]
     eye = identity(NODES)
-    parts = [nt(eye, message[:, i : i + NODES]) for i in range(0, message.shape[1], NODES)]
+    parts = []
+    for i in range(0, width, NODES):
+        n = min(NODES, width - i)
+        parts.append(nt(eye[:n, :n], message[:, i : i + n]))
     value = parts[0] if len(parts) == 1 else jnp.concatenate(parts, axis=0)
-    return (edge.astype(F32) + value * gain).astype(BF)
-
-
-def prepare_kernel(w_edge, edge, w_send, w_recv, w_out, near, far, wst, wrt, wt):
+    return (edge.astype(F32) + value[:size, :] * gain).astype(BF)
+
+
+def prepare_kernel(w_edge, edge, w_send, w_recv, w_out, *rest):
+    near, far, wst, wrt, wt, held, sem = rest[7:]
     eye = identity(D)
     wet = (0.5 * nt(eye, w_edge[...])).astype(BF)
-    near[...] = nt(wet, edge[:NM_PAD, :]).astype(BF)
+    for q in range(3):
+        held[q] = nt(wet, edge[q * NEAR_M : q * NEAR_M + NM_PAD, :]).astype(BF)
+    copy = pltpu.make_async_copy(held, near, sem)
+    copy.start()
     far[...] = nt(wet, edge[NM:, :]).astype(BF)
     wst[...] = (0.5 * nt(eye, w_send[...])).astype(BF)
     wrt[...] = (0.5 * nt(eye, w_recv[...])).astype(BF)
     wt[...] = centred_t(w_out[...])
-
-
-def near_kernel(live, wst, wrt, before, mid, after, sender, receiver, edge_pre, wt, edge, gain, out, total, pt):
-    pt[...] = nt(wrt[...], mid[...]).astype(BF)
-    table = nt(wst[...], jnp.concatenate([before[...], mid[...], after[...]], axis=0)).astype(BF)
+    copy.wait()
+
+
+def near_kernel(live, wst, mid, before, after, sender, receiver, pt, edge_pre, wt, total, sent, held, sem):
     lane = lax.broadcasted_iota(jnp.int32, (1, NM_PAD), 1)
-    block = lane // NEAR_M
-    count = jnp.where(block == 0, live[0, 0], jnp.where(block == 1, live[0, 1], live[0, 2]))
-    mask = (lane - block * NEAR_M < count) & (lane < NM)
-    hot = one_hot(NODES, receiver[:NM_PAD].reshape(1, NM_PAD))
-    index = jnp.where(lane < NM, sender[:NM_PAD].reshape(1, NM_PAD) + block * NODES, -1)
-    pre = edge_pre[...].astype(F32) + nn(table, one_hot(3 * NODES, index)) + nn(pt[...], hot)
-    message = messages_t(pre, wt[...], mask)
-    total[...] = nt(hot, message)
-    out[:NM, :] = rows_out(message, edge[:NM_PAD, :], gain[...])[:NM, :]
-
-
-def last_kernel(live, receiver, pt, edge_pre, wst, rows, wt, total, edge, gain, edge_out, out, partial, held, sem):
+    value = 0.0
+    for q, rows in ((1, mid), (0, before), (2, after)):
+        part = slice(q * NEAR_M, q * NEAR_M + NM_PAD)
+        table = nt(wst[...], rows[...]).astype(BF)
+        hot = one_hot(NODES, receiver[part].reshape(1, NM_PAD))
+        pre = nn(table, one_hot(NODES, sender[part].reshape(1, NM_PAD))) + nn(pt[...], hot) + edge_pre[q].astype(F32)
+        message = messages_t(pre, wt[...], (lane < live[0, q]) & (lane < NEAR_M))
+        held[q] = message
+        value = value + nt(hot, message)
+    copy = pltpu.make_async_copy(held, sent, sem)
+    copy.start()
+    total[...] = value
+    copy.wait()
+
+
+def last_kernel(live, receiver, pt, edge_pre, wst, rows, wt, total, partial, sent):
     hot = one_hot(NODES, receiver[NM:].reshape(1, FAR))
     pre = edge_pre[...].astype(F32) + nn(pt[...], hot) + nt(wst[...], rows[...])
     message = messages_t(pre, wt[...], far_live(live, FAR, 0))
-    held[...] = rows_out(message, edge[NM:, :], gain[...])
-    copy = pltpu.make_async_copy(held, out.at[pl.ds(NM, FAR), :], sem)
-    copy.start()
+    sent[...] = message
     partial[...] = (total[...] + nt(hot, message)).astype(BF)
-    copy.wait()
+
+
+def edge_kernel(far, near, edge, gain, out, held, sem):
+    copies = []
+    for q in range(4):
+        size = NEAR_M if q < 3 else FAR
+        part = slice(q * NEAR_M, q * NEAR_M + size)
+        message = near[q] if q < 3 else far[...]
+        held[part, :] = rows_out(message, edge[part, :], gain[...], size)
+        rows = pl.ds(q * NEAR_M, size)
+        copies.append(pltpu.make_async_copy(held.at[rows, :], out.at[rows, :], sem.at[q]))
+        copies[-1].start()
+    for copy in copies:
+        copy.wait()
 
 
 def band_parts(partial):
@@ -314,98 +374,114 @@
     update_second,
     update_gain,
 ):
-    asks = jnp.concatenate(
-        [encode_sender[NG:].reshape(N_REG, FAR_G), mesh_sender[NM:].reshape(N_REG, FAR_M)], axis=1
+    gains = [g.reshape(1, D) for g in (grid_gain, encode_gain, node_gain, process_gain, update_gain)]
+    before, after = halo(grid_latent)
+    weight = kept((D, D), BF)
+    asks, wst, rt, gt, wt, sender, kept_grid, receiver, feature = call(
+        start_kernel,
+        (kept((N_REG, 2 * FAR_G), jnp.int32), weight, kept((D, NODES), BF), kept((D, 16), BF), weight),
+        "KHHHHHHKKK",
+        (encode_sender, mesh_sender, encode_send, encode_receive, mesh_latent, encode_geometry, encode_output)
+        + (grid_latent, encode_receiver, encode_feature),
+        flops=2 * 10**9,
+        name="encode_start",
     )
     asked = exchange(asks)
-    before, after = halo(grid_latent)
-    gains = [g.reshape(1, D) for g in (grid_gain, encode_gain, node_gain, process_gain, update_gain)]
-
-    weight = shape((D, D), BF)
-    total, wst, rt, gt, wt = call(
+    total = call(
         own_kernel,
-        (shape((NODES, D), F32), weight, shape((D, NODES), BF), shape((D, 16), BF), weight),
-        "SHHHHHHHHH",
-        (encode_live, encode_send, grid_latent, encode_receive, mesh_latent, encode_geometry, encode_output)
-        + (encode_sender, encode_receiver, encode_feature),
-        flops=8 * 10**9,
+        [kept((NODES, D), F32)],
+        "SVVVVVVVV",
+        (encode_live, kept_grid, wst, sender, receiver, feature, rt, gt, wt),
+        flops=6 * 10**9,
         name="encode_own",
     )
     outgoing = call(
-        send_kernel, shape((FAR, D), BF), "VH", (asked, grid_latent), flops=3 * 10**8, name="encode_rows"
+        send_kernel, [shape((FAR, D), BF)], "VV", (asked, kept_grid), flops=3 * 10**8, name="encode_rows"
     )
     far_rows = exchange(outgoing.reshape(N_REG, FAR_G, D)).reshape(FAR, D)
     total = call(
         sides_kernel,
-        shape((NODES, D), F32),
-        "SAAHHHAAAAA",
-        (encode_live, before, wst, encode_sender, encode_receiver, encode_feature, rt, gt, wt, after, total),
+        [kept((NODES, D), F32)],
+        "SHVVVVVVVHV",
+        (encode_live, before, wst, sender, receiver, feature, rt, gt, wt, after, total),
         flops=11 * 10**9,
         name="encode_sides",
     )
     partial = call(
         far_kernel,
-        shape((NODES, D), BF),
-        "SHHAAAAAA",
-        (encode_live, encode_receiver, encode_feature, rt, gt, wst, far_rows, wt, total),
+        [kept((NODES, D), BF)],
+        "SVVVVVVVV",
+        (encode_live, receiver, feature, rt, gt, wst, far_rows, wt, total),
         flops=10**9,
         name="encode_far",
     )
     partial, later_edge = lax.optimization_barrier((partial, mesh_edge))
     parts = band_parts(partial)
-    near_pre, far_pre, p_wst, p_wrt, p_wt = call(
+    prepared = call(
         prepare_kernel,
-        (shape((D, NM_PAD), BF), shape((D, FAR), BF), weight, weight, weight),
-        "HHHHH",
-        (process_edge, later_edge, process_send, process_receive, process_output),
+        (pltpu.HBM((3, D, NM_PAD), BF), kept((D, FAR), BF), weight, weight, weight),
+        "HHHHHKKKKKKK",
+        (process_edge, later_edge, process_send, process_receive, process_output)
+        + (node_first, node_second, mesh_latent, gains[1], gains[2], mesh_sender, mesh_receiver),
+        scratch=[pltpu.VMEM((3, D, NM_PAD), BF), pltpu.SemaphoreType.DMA],
+        out_specs=(HBM, VMEM, VMEM, VMEM, VMEM),
         flops=3 * 10**9,
         name="process_prepare",
     )
-    mid, rows = call(
+    near_pre, far_pre, p_wst, p_wrt, p_wt, n_first, n_second, n_mesh, n_eg, n_gain, m_sender, m_receiver = prepared
+    mid, rows, pt = call(
         node_kernel,
-        (shape((NODES, D), BF), shape((FAR, D), BF)),
-        "VHAAAAHHHH",
-        (asked, mesh_latent, *parts, gains[1], node_first, node_second, gains[2]),
+        (kept((NODES, D), BF), shape((FAR, D), BF), kept((D, NODES), BF)),
+        "VVVVVVVVVVV",
+        (asked, n_mesh, *parts, n_eg, n_first, n_second, n_gain, p_wrt),
         flops=10**9,
         name="mesh_nodes",
     )
     far_mesh = exchange(rows.reshape(N_REG, FAR_M, D)).reshape(FAR, D)
     before_mid, after_mid = halo(mid)
-    edge_near, m_total, pt = call(
+    m_total, near_sent = call(
         near_kernel,
-        (shape((M2M, D), BF), shape((NODES, D), F32), shape((D, NODES), BF)),
-        "SAAAAAHHAAHH",
-        (mesh_live, p_wst, p_wrt, before_mid, mid, after_mid, mesh_sender, mesh_receiver, near_pre, p_wt)
-        + (mesh_edge, gains[3]),
+        (kept((NODES, D), F32), pltpu.HBM((3, D, NM_PAD), BF)),
+        "SVVVVVVVHV",
+        (mesh_live, p_wst, mid, before_mid, after_mid, m_sender, m_receiver, pt, near_pre, p_wt),
+        scratch=[pltpu.VMEM((3, D, NM_PAD), BF), pltpu.SemaphoreType.DMA],
+        out_specs=(VMEM, HBM),
         flops=4 * 10**9,
         name="process_near",
     )
-    edge_out, m_partial = call(
+    m_partial, far_sent = call(
         last_kernel,
-        (shape((M2M, D), BF), shape((NODES, D), BF)),
-        "SHAAAAAAHHR",
-        (mesh_live, mesh_receiver, pt, far_pre, p_wst, far_mesh, p_wt, m_total, mesh_edge, gains[3], edge_near),
-        scratch=[pltpu.VMEM((FAR, D), BF), pltpu.SemaphoreType.DMA],
-        out_specs=(ANY, VMEM),
+        (kept((NODES, D), BF), kept((D, FAR), BF)),
+        "SVVVVVVV",
+        (mesh_live, m_receiver, pt, far_pre, p_wst, far_mesh, p_wt, m_total),
         flops=10**9,
         name="process_far",
-        aliases={10: 0},
     )
     m_partial, grid_rows = lax.optimization_barrier((m_partial, grid_latent))
     m_parts = band_parts(m_partial)
-    grid_out = call(
+    edge_out, m_gain = call(
+        edge_kernel,
+        [pltpu.HBM((M2M, D), BF)],
+        "VHHK",
+        (far_sent, near_sent, mesh_edge, gains[3]),
+        scratch=[pltpu.VMEM((M2M, D), BF), pltpu.SemaphoreType.DMA((4,))],
+        out_specs=[HBM],
+        flops=3 * 10**9,
+        name="process_rows",
+    )
+    grid_out, u_first, u_second, u_gain = call(
         grid_kernel,
-        shape((GRID, D), BF),
-        "HHHH",
-        (grid_rows, grid_first, grid_second, gains[0]),
+        [shape((GRID, D), BF)],
+        "HHHHKKK",
+        (grid_rows, grid_first, grid_second, gains[0], update_first, update_second, gains[4]),
         flops=3 * 10**9,
         name="grid_nodes",
     )
     mesh_out = call(
         update_kernel,
-        shape((NODES, D), BF),
-        "AAAAAHHHH",
-        (mid, *m_parts, gains[3], update_first, update_second, gains[4]),
+        [shape((NODES, D), BF)],
+        "VVVVVVVVV",
+        (mid, *m_parts, m_gain, u_first, u_second, u_gain),
         flops=10**9,
         name="mesh_update",
     )

time: 151 us -> 107 us (0.71)
  local copies, waits for them, and re-layouts: 34.6 us -> 1.04 us
  waiting for transfers between devices: 23.6 us -> 16.4 us
    unnamed x122 -> x4, local copies, waits for them, and re-layouts: 33 us -> 1.04 us
    ppermute x6, waiting for transfers between devices: 23.6 us -> 13.3 us  [band_parts(): lax.ppermute(partial, 'band', [(i, (i + k) % count) for i in range(count)])]
    ppermute x4, waiting for transfers between devices: 0.01 us -> 2.37 us  [halo(): return (lax.ppermute(x, 'region', up), lax.ppermute(x, 'region', down))]
    pallas_call x10 -> x12, Pallas kernels: 52.9 us -> 52.3 us  [call(): pl.pallas_call(body, out_shape=out_shape, in_specs=[place[spec] for spec...]
  transfers between devices with their start and end apart: 13 -> 13, of which waited for: 5 -> 6; matrix products, arithmetic and copies ran while one was open for 2% -> 0% of each run, Pallas kernels for 28% -> 43%
where the time goes in v3:
time: 107 us; the launch traced here: 106 us
  Pallas kernels  52.3 us (49%)
  starting transfers between devices  35 us (33%)
  waiting for transfers between devices  16.4 us (15%)
    pallas_call x12, Pallas kernels, call(): pl.pallas_call(body, out_shape=out_shape, in_specs=[place[spec] for spec...  52.3 us
    all_to_all x3, starting transfers between devices, exchange(): return lax.all_to_all(x, 'region', split_axis=0, concat_axis=0, tiled=True)  17.7 us
    ppermute x6, waiting for transfers between devices, band_parts(): lax.ppermute(partial, 'band', [(i, (i + k) % count) for i in range(count)])  13.3 us
    ppermute x4, starting transfers between devices, halo(): return (lax.ppermute(x, 'region', up), lax.ppermute(x, 'region', down))  9.52 us
    ppermute x6, starting transfers between devices, band_parts(): lax.ppermute(partial, 'band', [(i, (i + k) % count) for i in range(count)])  7.74 us
    ppermute x4, waiting for transfers between devices, halo(): return (lax.ppermute(x, 'region', up), lax.ppermute(x, 'region', down))  2.37 us
  transfers between devices with their start and end apart: 13, of which 6 were waited for; matrix products, arithmetic and copies ran while one was open for 0% of the time, Pallas kernels for 43%

profile of v3, /device:TPU:0, one launch (start us, length us, event | category | flops | bytes accessed | tf_op | source)
XLA Modules:
  0.0 105.5 jit_solution(8205803877691007182)
XLA Ops:
  0.7 5.0 %collective-permute-start.1 = (bf16[1024,512]{1,0:T(8,128)(2,1)}, bf16[1024,512]{1,0:T(8,128)(2,1)}, u32[]{:S(2)}, u32[]{:S(2)}) collective-permute-start(bf16[1024,512]{1,0:T(8,128)(2,1)} %refs_0_.14), channel_id=1, source_target_pairs={{1,0},{2,1},{3,2},{4,3},{5,4},{6,5},{7,6},{8,7},{9,8},{10,9},{11,1... | collective-permute-start | bytes 3145736 | tf_op jit(solution)/shard_map/ppermute | solution.py:339
  5.8 4.2 %encode_start.1 = (s32[32,16]{1,0:T(8,128)}, bf16[512,512]{1,0:T(8,128)(2,1)S(1)}, bf16[512,256]{1,0:T(8,128)(2,1)S(1)}, bf16[512,16]{1,0:T(8,128)(2,1)S(1)}, bf...) custom-call(s32[6400]{0:T(1024)} %refs_0_.7, ...), custom_call_target="tpu_custom_call" | custom-call | flops 2000000000 | bytes 1048576 | tf_op jit(solution)/shard_map/encode_start/pallas_call | solution.py:117
  10.0 4.1 %all-to-all-start = ((s32[32,1,16]{2,1,0:T(1,128)}), s32[32,1,16]{2,1,0:T(1,128)S(1)}, u32[]{:S(2)}, u32[]{:S(2)}) async-start(s32[32,1,16]{2,1,0:T(1,128)} %bitcast.1), calls=%async_computation | async-start | bytes 32768 | tf_op jit(solution)/shard_map/all_to_all | solution.py:343
  14.1 6.6 %encode_own.1.refs_10_ = f32[256,512]{1,0:T(8,128)S(1)} custom-call(s32[1,35]{1,0:T(1,128)} %refs_0_.10, bf16[1024,512]{1,0:T(8,128)(2,1)S(1)} %get-tuple-element.47.refs_1_, bf16[512,512]{1,0:T(8,128)(2,1)S(1)} %get-tuple-element.45.refs_2_.refs_5_, s32[6400]{0:T(1024)S(1)} %get-tuple-element.49.refs_3_, s32[6400]{0:T(1024)S(1)} %get-tuple-element.41.refs_4_.refs_1_, ...), custom_call_target="tpu_custom_call" | custom-call | flops 6000000000 | bytes 1048576 | tf_op jit(solution)/shard_map/encode_own/pallas_call | solution.py:117
  21.3 1.4 %encode_rows.1 = bf16[256,512]{1,0:T(8,128)(2,1)} custom-call(s32[32,16]{1,0:T(8,128)S(1)} %bitcast.15, bf16[1024,512]{1,0:T(8,128)(2,1)S(1)} %get-tuple-element.47.refs_1_), custom_call_target="tpu_custom_call" | custom-call | flops 300000000 | bytes 1048576 | tf_op jit(solution)/shard_map/encode_rows/pallas_call | solution.py:117
  22.7 6.9 %all-to-all-start.1 = ((bf16[32,8,512]{2,1,0:T(8,128)(2,1)}), bf16[32,8,512]{2,1,0:T(8,128)(2,1)S(1)}, u32[]{:S(2)}, u32[]{:S(2)}) async-start(bf16[32,8,512]{2,1,0:T(8,128)(2,1)} %bitcast.3), calls=%async_computation.1 | async-start | bytes 524288 | tf_op jit(solution)/shard_map/all_to_all | solution.py:343
  30.7 13.1 %encode_sides.1.refs_8_ = f32[256,512]{1,0:T(8,128)S(1)} custom-call(s32[1,35]{1,0:T(1,128)} %refs_0_.10, bf16[1024,512]{1,0:T(8,128)(2,1)} %collective-permute-done.refs_1_, bf16[512,512]{1,0:T(8,128)(2,1)S(1)} %get-tuple-element.45.refs_2_.refs_5_, s32[6400]{0:T(1024)S(1)} %get-tuple-element.49.refs_3_, s32[6400]{0:T(1024)S(1)} %get-tuple-element.41.refs_4_.refs_1_, ...), custom_call_target="tpu_custom_call" | custom-call | flops 11000000512 | bytes 1048576 | tf_op jit(solution)/shard_map/encode_sides/pallas_call | solution.py:117
  43.9 1.9 %encode_far.1.refs_2_ = bf16[256,512]{1,0:T(8,128)(2,1)S(1)} custom-call(s32[1,35]{1,0:T(1,128)} %refs_0_.10, s32[6400]{0:T(1024)S(1)} %get-tuple-element.41.refs_4_.refs_1_, f32[4,6400]{1,0:T(4,128)S(1)} %get-tuple-element.42.refs_5_.refs_2_, bf16[512,256]{1,0:T(8,128)(2,1)S(1)} %get-tuple-element.43.refs_6_.refs_3_, ...), custom_call_target="tpu_custom_call" | custom-call | flops 1000000000 | bytes 1048576 | tf_op jit(solution)/shard_map/encode_far/pallas_call | solution.py:117
  45.8 4.1 %collective-permute-start.4 = (bf16[256,512]{1,0:T(8,128)(2,1)S(1)}, bf16[256,512]{1,0:T(8,128)(2,1)S(1)}, u32[]{:S(2)}, u32[]{:S(2)}) collective-permute-start(bf16[256,512]{1,0:T(8,128)(2,1)S(1)} %encode_far.1.refs_2_), channel_id=1, source_target_pairs={{0,96},{32,0},{64,32},{96,64},{1,97},{33,1},{65,33},{97,65},{2,98}... | collective-permute-start | bytes 786440 | tf_op jit(solution)/shard_map/ppermute | solution.py:330
  49.9 1.3 %collective-permute-start.2 = (bf16[256,512]{1,0:T(8,128)(2,1)S(1)}, bf16[256,512]{1,0:T(8,128)(2,1)S(1)}, u32[]{:S(2)}, u32[]{:S(2)}) collective-permute-start(bf16[256,512]{1,0:T(8,128)(2,1)S(1)} %encode_far.1.refs_2_), channel_id=1, source_target_pairs={{0,32},{32,64},{64,96},{96,0},{1,33},{33,65},{65,97},{97,1},{2,34}... | collective-permute-start | bytes 786440 | tf_op jit(solution)/shard_map/ppermute | solution.py:330
  51.2 5.0 %process_prepare.1 = (bf16[3,512,640]{2,1,0:T(8,128)(2,1)}, bf16[512,256]{1,0:T(8,128)(2,1)S(1)}, bf16[512,512]{1,0:T(8,128)(2,1)S(1)}, bf16[512,512]{1,0:T(8,12...) custom-call(bf16[512,512]{1,0:T(8,128)(2,1)} %refs_0_.11, ...), custom_call_target="tpu_custom_call" | custom-call | flops 3000000000 | bytes 1048576 | tf_op jit(solution)/shard_map/process_prepare/pallas_call | solution.py:117
  56.2 5.2 %collective-permute-done.4.refs_5_ = bf16[256,512]{1,0:T(8,128)(2,1)S(1)} collective-permute-done((bf16[256,512]{1,0:T(8,128)(2,1)S(1)}, bf16[256,512]{1,0:T(8,128)(2,1)S(1)}, u32[]{:S(2)}, u32[]{:S(2)}) %collective-permute-start.4) | collective-permute-done | bytes 262176 | tf_op jit(solution)/shard_map/ppermute | solution.py:330
  61.4 3.4 %collective-permute-done.2.refs_3_ = bf16[256,512]{1,0:T(8,128)(2,1)S(1)} collective-permute-done((bf16[256,512]{1,0:T(8,128)(2,1)S(1)}, bf16[256,512]{1,0:T(8,128)(2,1)S(1)}, u32[]{:S(2)}, u32[]{:S(2)}) %collective-permute-start.2) | collective-permute-done | bytes 262176 | tf_op jit(solution)/shard_map/ppermute | solution.py:330
  64.8 1.8 %mesh_nodes.1 = (bf16[256,512]{1,0:T(8,128)(2,1)S(1)}, bf16[256,512]{1,0:T(8,128)(2,1)}, bf16[512,256]{1,0:T(8,128)(2,1)S(1)}) custom-call(s32[32,16]{1,0:T(8,128)S(1)} %bitcast.16, bf16[256,512]{1,0:T(8,128)(2,1)S(1)} %get-tuple-element.52.refs_1_, bf16[256,512]{1,0:T(8,128)(2,1)S(1)} %encode_far.1.refs_2_, ...), custom_call_target="tpu_custom_call" | custom-call | flops 1000000000 | bytes 1048576 | tf_op jit(solution)/shard_map/mesh_nodes/pallas_call | solution.py:117
  66.6 4.4 %collective-permute-start.6 = (bf16[256,512]{1,0:T(8,128)(2,1)S(1)}, bf16[256,512]{1,0:T(8,128)(2,1)S(1)}, u32[]{:S(2)}, u32[]{:S(2)}) collective-permute-start(bf16[256,512]{1,0:T(8,128)(2,1)S(1)} %get-tuple-element.64.refs_2_.refs_0_), channel_id=1, source_target_pairs={{1,0},{2,1},{3,2},{4,3},{5,4},{6,5},{7,6},{8,7},{9,8},{10,9},{11,1... | collective-permute-start | bytes 786440 | tf_op jit(solution)/shard_map/ppermute | solution.py:339
  71.0 6.7 %all-to-all-start.2 = ((bf16[32,8,512]{2,1,0:T(8,128)(2,1)}), bf16[32,8,512]{2,1,0:T(8,128)(2,1)S(1)}, u32[]{:S(2)}, u32[]{:S(2)}) async-start(bf16[32,8,512]{2,1,0:T(8,128)(2,1)} %bitcast.7), calls=%async_computation.2 | async-start | bytes 524288 | tf_op jit(solution)/shard_map/all_to_all | solution.py:343
  77.7 2.4 %collective-permute-done.5.refs_3_ = bf16[256,512]{1,0:T(8,128)(2,1)S(1)} collective-permute-done((bf16[256,512]{1,0:T(8,128)(2,1)S(1)}, bf16[256,512]{1,0:T(8,128)(2,1)S(1)}, u32[]{:S(2)}, u32[]{:S(2)}) %collective-permute-start.5) | collective-permute-done | bytes 262176 | tf_op jit(solution)/shard_map/ppermute | solution.py:339
  80.1 6.6 %process_near.1 = (f32[256,512]{1,0:T(8,128)S(1)}, bf16[3,512,640]{2,1,0:T(8,128)(2,1)}) custom-call(s32[1,35]{1,0:T(1,128)} %refs_0_.13, bf16[512,512]{1,0:T(8,128)(2,1)S(1)} %get-tuple-element.61.refs_1_.refs_4_, bf16[256,512]{1,0:T(8,128)(2,1)S(1)} %get-tuple-element.64.refs_2_.refs_0_, bf16[256,512]{1,0:T(8,128)(2,1)S(1)} %collective-permute-done.5.refs_3_, ...), custom_call_target="tpu_custom_call" | custom-call | flops 4000000000 | bytes 1048576 | tf_op jit(solution)/shard_map/process_near/pallas_call | solution.py:117
  86.7 1.5 %process_far.1 = (bf16[256,512]{1,0:T(8,128)(2,1)S(1)}, bf16[512,256]{1,0:T(8,128)(2,1)S(1)}) custom-call(s32[1,35]{1,0:T(1,128)} %refs_0_.13, s32[1984]{0:T(1024)S(1)} %get-tuple-element.51.refs_6_.refs_1_, bf16[512,256]{1,0:T(8,128)(2,1)S(1)} %get-tuple-element.59.refs_7_.refs_2_, bf16[512,256]{1,0:T(8,128)(2,1)S(1)} %get-tuple-element.60.refs_3_, ...), custom_call_target="tpu_custom_call" | custom-call | flops 1000000000 | bytes 1048576 | tf_op jit(solution)/shard_map/process_far/pallas_call | solution.py:117
  89.3 1.3 %collective-permute-start.7 = (bf16[256,512]{1,0:T(8,128)(2,1)S(1)}, bf16[256,512]{1,0:T(8,128)(2,1)S(1)}, u32[]{:S(2)}, u32[]{:S(2)}) collective-permute-start(bf16[256,512]{1,0:T(8,128)(2,1)S(1)} %get-tuple-element.71.refs_1_), channel_id=1, source_target_pairs={{0,32},{32,64},{64,96},{96,0},{1,33},{33,65},{65,97},{97,1},{2,34}... | collective-permute-start | bytes 786440 | tf_op jit(solution)/shard_map/ppermute | solution.py:330
  90.6 4.0 %process_rows.1 = (bf16[1984,512]{1,0:T(8,128)(2,1)}, f32[1,512]{1,0:T(1,128)S(1)}) custom-call(bf16[512,256]{1,0:T(8,128)(2,1)S(1)} %get-tuple-element.72.refs_0_, bf16[3,512,640]{2,1,0:T(8,128)(2,1)} %get-tuple-element.73.refs_1_, bf16[1984,512]{1,0:T(8,128)(2,1)} %refs_2_.7, f32[1,512]{1,0:T(1,128)} %bitcast.19), custom_call_target="tpu_custom_call" | custom-call | flops 3000000000 | bytes 1048576 | tf_op jit(solution)/shard_map/process_rows/pallas_call | solution.py:117
  94.6 4.5 %grid_nodes.1 = (bf16[1024,512]{1,0:T(8,128)(2,1)}, bf16[1024,512]{1,0:T(8,128)(2,1)S(1)}, bf16[512,512]{1,0:T(8,128)(2,1)S(1)}, f32[1,512]{1,0:T(1,128)S(1)}) custom-call(bf16[1024,512]{1,0:T(8,128)(2,1)} %refs_0_.14, bf16[512,512]{1,0:T(8,128)(2,1)} %refs_1_.4, bf16[512,512]{1,0:T(8,128)(2,1)} %refs_2_.6, f32[1,512]{1,0:T(1,128)} %bitcast.20, ...), custom_call_target="tpu_custom_call" | custom-call | flops 3000000000 | bytes 1048576 | tf_op jit(solution)/shard_map/grid_nodes/pallas_call | solution.py:117
  99.2 4.6 %collective-permute-done.7.refs_2_ = bf16[256,512]{1,0:T(8,128)(2,1)S(1)} collective-permute-done((bf16[256,512]{1,0:T(8,128)(2,1)S(1)}, bf16[256,512]{1,0:T(8,128)(2,1)S(1)}, u32[]{:S(2)}, u32[]{:S(2)}) %collective-permute-start.7) | collective-permute-done | bytes 262176 | tf_op jit(solution)/shard_map/ppermute | solution.py:330
  103.9 1.6 %mesh_update.1 = bf16[256,512]{1,0:T(8,128)(2,1)} custom-call(bf16[256,512]{1,0:T(8,128)(2,1)S(1)} %get-tuple-element.64.refs_2_.refs_0_, bf16[256,512]{1,0:T(8,128)(2,1)S(1)} %get-tuple-element.71.refs_1_, bf16[256,512]{1,0:T(8,128)(2,1)S(1)} %collective-permute-done.7.refs_2_, bf16[256,512]{1,0:T(8,128)(2,1)S(1)} %collective-permute-done.8.refs_3_, ...), custom_call_target="tpu_custom_call" | custom-call | flops 1000000000 | bytes 1048576 | tf_op jit(solution)/shard_map/mesh_update/pallas_call | solution.py:117
  (18 shorter events, 3.0 us)
Async XLA Ops:
  0.6 29.0 %collective-permute-start = (bf16[1024,512]{1,0:T(8,128)(2,1)}, bf16[1024,512]{1,0:T(8,128)(2,1)}, u32[]{:S(2)}, u32[]{:S(2)}) collective-permute-start(bf16[1024,512]{1,0:T(8,128)(2,1)} %refs_0_.14), channel_id=1, source_target_pairs={{0,1},{1,2},{2,3},{3,4},{4,5},{5,6},{6,7},{7,8},{8,9},{9,10},{10,1... | collective-permute-start | bytes 3145736 | tf_op jit(solution)/shard_map/ppermute | solution.py:339
  0.7 28.9 %collective-permute-start.1 = (bf16[1024,512]{1,0:T(8,128)(2,1)}, bf16[1024,512]{1,0:T(8,128)(2,1)}, u32[]{:S(2)}, u32[]{:S(2)}) collective-permute-start(bf16[1024,512]{1,0:T(8,128)(2,1)} %refs_0_.14), channel_id=1, source_target_pairs={{1,0},{2,1},{3,2},{4,3},{5,4},{6,5},{7,6},{8,7},{9,8},{10,9},{11,1... | collective-permute-start | bytes 3145736 | tf_op jit(solution)/shard_map/ppermute | solution.py:339
  10.0 11.4 %all-to-all-start = ((s32[32,1,16]{2,1,0:T(1,128)}), s32[32,1,16]{2,1,0:T(1,128)S(1)}, u32[]{:S(2)}, u32[]{:S(2)}) async-start(s32[32,1,16]{2,1,0:T(1,128)} %bitcast.1), calls=%async_computation | async-start | bytes 32768 | tf_op jit(solution)/shard_map/all_to_all | solution.py:343
  20.6 9.0 %copy-start = (f32[256,512]{1,0:T(8,128)}, f32[256,512]{1,0:T(8,128)S(1)}, u32[]{:S(2)}) copy-start(f32[256,512]{1,0:T(8,128)S(1)} %encode_own.1.refs_10_) | copy-start | bytes 1572868
  22.7 21.1 %all-to-all-start.1 = ((bf16[32,8,512]{2,1,0:T(8,128)(2,1)}), bf16[32,8,512]{2,1,0:T(8,128)(2,1)S(1)}, u32[]{:S(2)}, u32[]{:S(2)}) async-start(bf16[32,8,512]{2,1,0:T(8,128)(2,1)} %bitcast.3), calls=%async_computation.1 | async-start | bytes 524288 | tf_op jit(solution)/shard_map/all_to_all | solution.py:343
  29.6 1.0 copy-start.1
  45.8 15.5 %collective-permute-start.4 = (bf16[256,512]{1,0:T(8,128)(2,1)S(1)}, bf16[256,512]{1,0:T(8,128)(2,1)S(1)}, u32[]{:S(2)}, u32[]{:S(2)}) collective-permute-start(bf16[256,512]{1,0:T(8,128)(2,1)S(1)} %encode_far.1.refs_2_), channel_id=1, source_target_pairs={{0,96},{32,0},{64,32},{96,64},{1,97},{33,1},{65,33},{97,65},{2,98}... | collective-permute-start | bytes 786440 | tf_op jit(solution)/shard_map/ppermute | solution.py:330
  49.9 11.4 %collective-permute-start.3 = (bf16[256,512]{1,0:T(8,128)(2,1)S(1)}, bf16[256,512]{1,0:T(8,128)(2,1)S(1)}, u32[]{:S(2)}, u32[]{:S(2)}) collective-permute-start(bf16[256,512]{1,0:T(8,128)(2,1)S(1)} %encode_far.1.refs_2_), channel_id=1, source_target_pairs={{0,64},{32,96},{64,0},{96,32},{1,65},{33,97},{65,1},{97,33},{2,66}... | collective-permute-start | bytes 786440 | tf_op jit(solution)/shard_map/ppermute | solution.py:330
  49.9 14.9 %collective-permute-start.2 = (bf16[256,512]{1,0:T(8,128)(2,1)S(1)}, bf16[256,512]{1,0:T(8,128)(2,1)S(1)}, u32[]{:S(2)}, u32[]{:S(2)}) collective-permute-start(bf16[256,512]{1,0:T(8,128)(2,1)S(1)} %encode_far.1.refs_2_), channel_id=1, source_target_pairs={{0,32},{32,64},{64,96},{96,0},{1,33},{33,65},{65,97},{97,1},{2,34}... | collective-permute-start | bytes 786440 | tf_op jit(solution)/shard_map/ppermute | solution.py:330
  66.6 11.1 %collective-permute-start.6 = (bf16[256,512]{1,0:T(8,128)(2,1)S(1)}, bf16[256,512]{1,0:T(8,128)(2,1)S(1)}, u32[]{:S(2)}, u32[]{:S(2)}) collective-permute-start(bf16[256,512]{1,0:T(8,128)(2,1)S(1)} %get-tuple-element.64.refs_2_.refs_0_), channel_id=1, source_target_pairs={{1,0},{2,1},{3,2},{4,3},{5,4},{6,5},{7,6},{8,7},{9,8},{10,9},{11,1... | collective-permute-start | bytes 786440 | tf_op jit(solution)/shard_map/ppermute | solution.py:339
  71.0 9.1 %collective-permute-start.5 = (bf16[256,512]{1,0:T(8,128)(2,1)S(1)}, bf16[256,512]{1,0:T(8,128)(2,1)S(1)}, u32[]{:S(2)}, u32[]{:S(2)}) collective-permute-start(bf16[256,512]{1,0:T(8,128)(2,1)S(1)} %get-tuple-element.64.refs_2_.refs_0_), channel_id=1, source_target_pairs={{0,1},{1,2},{2,3},{3,4},{4,5},{5,6},{6,7},{7,8},{8,9},{9,10},{10,1... | collective-permute-start | bytes 786440 | tf_op jit(solution)/shard_map/ppermute | solution.py:339
  71.0 15.7 %all-to-all-start.2 = ((bf16[32,8,512]{2,1,0:T(8,128)(2,1)}), bf16[32,8,512]{2,1,0:T(8,128)(2,1)S(1)}, u32[]{:S(2)}, u32[]{:S(2)}) async-start(bf16[32,8,512]{2,1,0:T(8,128)(2,1)} %bitcast.7), calls=%async_computation.2 | async-start | bytes 524288 | tf_op jit(solution)/shard_map/all_to_all | solution.py:343
  88.2 10.9 %collective-permute-start.9 = (bf16[256,512]{1,0:T(8,128)(2,1)S(1)}, bf16[256,512]{1,0:T(8,128)(2,1)S(1)}, u32[]{:S(2)}, u32[]{:S(2)}) collective-permute-start(bf16[256,512]{1,0:T(8,128)(2,1)S(1)} %get-tuple-element.71.refs_1_), channel_id=1, source_target_pairs={{0,96},{32,0},{64,32},{96,64},{1,97},{33,1},{65,33},{97,65},{2,98}... | collective-permute-start | bytes 786440 | tf_op jit(solution)/shard_map/ppermute | solution.py:330
  88.5 10.7 %collective-permute-start.8 = (bf16[256,512]{1,0:T(8,128)(2,1)S(1)}, bf16[256,512]{1,0:T(8,128)(2,1)S(1)}, u32[]{:S(2)}, u32[]{:S(2)}) collective-permute-start(bf16[256,512]{1,0:T(8,128)(2,1)S(1)} %get-tuple-element.71.refs_1_), channel_id=1, source_target_pairs={{0,64},{32,96},{64,0},{96,32},{1,65},{33,97},{65,1},{97,33},{2,66}... | collective-permute-start | bytes 786440 | tf_op jit(solution)/shard_map/ppermute | solution.py:330
  89.3 14.6 %collective-permute-start.7 = (bf16[256,512]{1,0:T(8,128)(2,1)S(1)}, bf16[256,512]{1,0:T(8,128)(2,1)S(1)}, u32[]{:S(2)}, u32[]{:S(2)}) collective-permute-start(bf16[256,512]{1,0:T(8,128)(2,1)S(1)} %get-tuple-element.71.refs_1_), channel_id=1, source_target_pairs={{0,32},{32,64},{64,96},{96,0},{1,33},{33,65},{65,97},{97,1},{2,34}... | collective-permute-start | bytes 786440 | tf_op jit(solution)/shard_map/ppermute | solution.py:330

commit v4 on v3

--- a/solution.py
+++ b/solution.py
@@ -59,15 +59,17 @@
     return jnp.concatenate([high, feature - high, high, zero], axis=0).astype(BF)
 
 
-def messages_t(half_pre, w_out_t, live):
+def messages_t(half_pre, w_out_t, live=None):
     hidden = (half_pre * jnp.tanh(half_pre) + half_pre).astype(BF)
     y = nn(w_out_t, hidden)
     spread = jnp.sum(y * y, axis=0, keepdims=True) * (1 / D)
-    scale = jnp.where(live, lax.rsqrt(spread + EPSILON), 0.0)
+    scale = lax.rsqrt(spread + EPSILON)
+    if live is not None:
+        scale = jnp.where(live, scale, 0.0)
     return (y * scale).astype(BF)
 
 
-def far_live(counts, width, near_cols):
+def far_live(counts, width):
     lane = lax.broadcasted_iota(jnp.int32, (1, width), 1)
     limit = jnp.zeros((1, width), jnp.int32)
     for k in range(N_REG):
@@ -143,15 +145,14 @@
     return pltpu.VMEM(dims, kind)
 
 
-def encode_block(q, table, rt, gt, wt, sender, receiver, feature, limit):
+def encode_block(q, halves, table, rt, gt, wt, sender, receiver, feature):
     value = None
-    for i in range(0, NEAR_G, HALF):
+    for i in halves:
         part = slice(q * NEAR_G + i, q * NEAR_G + i + HALF)
-        hot = one_hot(NODES, receiver[part].reshape(1, HALF))
+        hot = one_hot(NODES, receiver[:, part])
         pre = nn(table, one_hot(GRID, sender[part].reshape(1, HALF))) + nn(rt, hot)
         pre = pre + nn(gt, feature_rows(feature[:, part]))
-        live = lax.broadcasted_iota(jnp.int32, (1, HALF), 1) + i < limit
-        term = nt(hot, messages_t(pre, wt, live))
+        term = nt(hot, messages_t(pre, wt))
         value = term if value is None else value + term
     return value
 
@@ -166,14 +167,22 @@
     return nt(high, pick) * 32.0 + nt(low, pick)
 
 
-def start_kernel(sender, m_sender, w_send, w_recv, mesh, geo, w_out, grid, receiver, feature, *rest):
-    asks, wst, rt, gt, wt = rest[:5]
+def asks_kernel(sender, m_sender, asks, *_):
     far = slots_to_rows(sender[NG:].reshape(1, FAR), 0) + slots_to_rows(m_sender[NM:].reshape(1, FAR), FAR_G)
     asks[...] = far.astype(jnp.int32)
+
+
+def weights_kernel(w_send, live, w_recv, mesh, receiver, geo, w_out, *rest):
+    wst, rt, gt, wt, targets = rest[2:]
     eye = identity(D)
     wst[...] = (0.5 * nt(eye, w_send[...])).astype(BF)
     wrt = nt(eye, w_recv[...]).astype(BF)
     rt[...] = (0.5 * nt(wrt, mesh[...])).astype(BF)
+    lane = lax.broadcasted_iota(jnp.int32, (1, NEAR_G), 1)
+    for q in range(3):
+        part = slice(q * NEAR_G, (q + 1) * NEAR_G)
+        targets[:, part] = jnp.where(lane < live[0, q], receiver[part].reshape(1, NEAR_G), -1)
+    targets[:, NG:] = jnp.where(far_live(live, FAR), receiver[NG:].reshape(1, FAR), -1)
     half = 0.5 * geo[...]
     high = half.astype(BF).astype(F32)
     stacked = jnp.concatenate([high, high, half - high, jnp.zeros((4, D), F32)], axis=0)
@@ -181,25 +190,31 @@
     wt[...] = centred_t(w_out[...])
 
 
-def own_kernel(live, grid, wst, sender, receiver, feature, rt, gt, wt, out):
+def first_edges_kernel(grid, wst, sender, receiver, feature, rt, gt, wt, out):
     table = nt(wst[...], grid[...]).astype(BF)
-    out[...] = encode_block(1, table, rt[...], gt[...], wt[...], sender, receiver, feature, live[0, 1])
-
-
-def sides_kernel(live, before, wst, sender, receiver, feature, rt, gt, wt, after, total, out):
-    value = 0.0
-    for q, rows in ((0, before), (2, after)):
+    out[...] = encode_block(1, (0,), table, rt[...], gt[...], wt[...], sender, receiver, feature).astype(BF)
+
+
+def near_edges_kernel(grid, wst, sender, receiver, feature, rt, gt, wt, begun, before, after, out):
+    value = begun[...].astype(F32)
+    for q, rows in ((1, grid), (0, before), (2, after)):
         table = nt(wst[...], rows[...]).astype(BF)
-        value = value + encode_block(q, table, rt[...], gt[...], wt[...], sender, receiver, feature, live[0, q])
-    out[...] = total[...] + value
-
-
-def far_kernel(live, receiver, feature, rt, gt, wst, rows, wt, total, out):
+        halves = (HALF,) if q == 1 else (0, HALF)
+        value = value + encode_block(q, halves, table, rt[...], gt[...], wt[...], sender, receiver, feature)
+    out[...] = value
+
+
+def far_kernel(receiver, feature, rt, gt, wst, rows, wt, total, *rest):
     part = slice(NG, NG + FAR)
-    hot = one_hot(NODES, receiver[part].reshape(1, FAR))
+    hot = one_hot(NODES, receiver[:, part])
     pre = nn(rt[...], hot) + nn(gt[...], feature_rows(feature[:, part])) + nt(wst[...], rows[...])
-    message = messages_t(pre, wt[...], far_live(live, FAR, 0))
-    out[...] = (total[...] + nt(hot, message)).astype(BF)
+    split(total[...] + nt(hot, messages_t(pre, wt[...])), *rest[-2:])
+
+
+def split(value, low, high):
+    value = value.astype(BF)
+    low[...] = value[: NODES // 2, :]
+    high[...] = value[NODES // 2 :, :]
 
 
 def asked_hot(asked, first, nodes):
@@ -236,27 +251,41 @@
     return (latent.astype(F32) + update).astype(BF)
 
 
-def band_sum(p0, p1, p2, p3, edge_gain):
-    total = (p0[...].astype(F32) + p2[...].astype(F32)) + (p1[...].astype(F32) + p3[...].astype(F32))
-    return (total * edge_gain[...]).astype(BF)
+def plus(a, b):
+    return a[...].astype(F32) + b[...].astype(F32)
+
+
+def add_kernel(a, b, out):
+    out[...] = plus(a, b).astype(BF)
+
+
+def band_total(low, low_in, high, high_in, edge_gain):
+    return (jnp.concatenate([plus(low, low_in), plus(high, high_in)], axis=0) * edge_gain[...]).astype(BF)
 
 
 def node_kernel(asked, mesh, p0, p1, p2, p3, edge_gain, w_first, w_second, gain, wrt, mid, rows, pt):
-    value = mlp(mesh[...], band_sum(p0, p1, p2, p3, edge_gain), w_first, w_second, gain)
+    value = mlp(mesh[...], band_total(p0, p1, p2, p3, edge_gain), w_first, w_second, gain)
     mid[...] = value
     rows[...] = nn(asked_hot(asked[...], FAR_G, NODES), value).astype(BF)
     pt[...] = nt(wrt[...], value).astype(BF)
 
 
 def update_kernel(mid, p0, p1, p2, p3, edge_gain, w_first, w_second, gain, out):
-    out[...] = mlp(mid[...], band_sum(p0, p1, p2, p3, edge_gain), w_first, w_second, gain)
-
-
-def grid_kernel(latent, w_first, w_second, gain, *rest):
-    out = rest[-1]
-    rows = latent[...]
-    update = norm(nn(silu(nn(rows, w_first[...])), w_second[...])) * gain[...]
-    out[...] = (rows.astype(F32) + update).astype(BF)
+    out[...] = mlp(mid[...], band_total(p0, p1, p2, p3, edge_gain), w_first, w_second, gain)
+
+
+def grid_kernel(latent, w_first, w_second, gain, out, held, sems):
+    copies = []
+    for i in range(4):
+        part = slice(i * NODES, (i + 1) * NODES)
+        rows = latent[part, :]
+        update = norm(nn(silu(nn(rows, w_first[...])), w_second[...])) * gain[...]
+        held[part, :] = (rows.astype(F32) + update).astype(BF)
+        where = pl.ds(i * NODES, NODES)
+        copies.append(pltpu.make_async_copy(held.at[where, :], out.at[where, :], sems.at[i]))
+        copies[-1].start()
+    for copy in copies:
+        copy.wait()
 
 
 def rows_out(message, edge, gain, size):
@@ -270,52 +299,64 @@
     return (edge.astype(F32) + value[:size, :] * gain).astype(BF)
 
 
-def prepare_kernel(w_edge, edge, w_send, w_recv, w_out, *rest):
-    near, far, wst, wrt, wt, held, sem = rest[7:]
-    eye = identity(D)
-    wet = (0.5 * nt(eye, w_edge[...])).astype(BF)
+def edge_terms_kernel(w_edge, edge, *rest):
+    near, far, held, sem = rest[-4:]
+    wet = (0.5 * nt(identity(D), w_edge[...])).astype(BF)
     for q in range(3):
-        held[q] = nt(wet, edge[q * NEAR_M : q * NEAR_M + NM_PAD, :]).astype(BF)
+        held[:, q * NM_PAD : (q + 1) * NM_PAD] = nt(wet, edge[q * NEAR_M : q * NEAR_M + NM_PAD, :]).astype(BF)
     copy = pltpu.make_async_copy(held, near, sem)
     copy.start()
     far[...] = nt(wet, edge[NM:, :]).astype(BF)
+    copy.wait()
+
+
+def prepare_kernel(w_send, live, sender, receiver, w_recv, w_out, wst, wrt, wt, near, far):
+    eye = identity(D)
     wst[...] = (0.5 * nt(eye, w_send[...])).astype(BF)
     wrt[...] = (0.5 * nt(eye, w_recv[...])).astype(BF)
     wt[...] = centred_t(w_out[...])
-    copy.wait()
-
-
-def near_kernel(live, wst, mid, before, after, sender, receiver, pt, edge_pre, wt, total, sent, held, sem):
     lane = lax.broadcasted_iota(jnp.int32, (1, NM_PAD), 1)
-    value = 0.0
-    for q, rows in ((1, mid), (0, before), (2, after)):
-        part = slice(q * NEAR_M, q * NEAR_M + NM_PAD)
-        table = nt(wst[...], rows[...]).astype(BF)
-        hot = one_hot(NODES, receiver[part].reshape(1, NM_PAD))
-        pre = nn(table, one_hot(NODES, sender[part].reshape(1, NM_PAD))) + nn(pt[...], hot) + edge_pre[q].astype(F32)
-        message = messages_t(pre, wt[...], (lane < live[0, q]) & (lane < NEAR_M))
-        held[q] = message
-        value = value + nt(hot, message)
+    for q in range(3):
+        part, put = slice(q * NEAR_M, q * NEAR_M + NM_PAD), slice(q * NM_PAD, (q + 1) * NM_PAD)
+        here = (lane < live[0, q]) & (lane < NEAR_M)
+        near[0:1, put] = jnp.where(here, receiver[part].reshape(1, NM_PAD), -1)
+        near[1:2, put] = sender[part].reshape(1, NM_PAD)
+    far[...] = jnp.where(far_live(live, FAR), receiver[NM:].reshape(1, FAR), -1)
+
+
+def near_kernel(edge_pre, wst, mid, before, after, index, pt, wt, total, sent, held, sem):
+    table = nt(wst[...], jnp.concatenate([before[...], mid[...], after[...]], axis=0)).astype(BF)
+    target = index[0:1, :]
+    hot = one_hot(NODES, target)
+    gathered = [
+        nn(table[:, q * NODES : (q + 1) * NODES], one_hot(NODES, index[1:2, q * NM_PAD : (q + 1) * NM_PAD]))
+        for q in range(3)
+    ]
+    pre = nn(pt[...], hot) + jnp.concatenate(gathered, axis=1) + edge_pre[...].astype(F32)
+    message = messages_t(pre, wt[...], target >= 0)
+    held[...] = message
     copy = pltpu.make_async_copy(held, sent, sem)
     copy.start()
-    total[...] = value
+    total[...] = nt(hot, message)
     copy.wait()
 
 
-def last_kernel(live, receiver, pt, edge_pre, wst, rows, wt, total, partial, sent):
-    hot = one_hot(NODES, receiver[NM:].reshape(1, FAR))
+def last_kernel(target, pt, edge_pre, wst, rows, wt, total, *rest):
+    low, high, sent = rest[-3:]
+    hot = one_hot(NODES, target[...])
     pre = edge_pre[...].astype(F32) + nn(pt[...], hot) + nt(wst[...], rows[...])
-    message = messages_t(pre, wt[...], far_live(live, FAR, 0))
+    message = messages_t(pre, wt[...], target[...] >= 0)
     sent[...] = message
-    partial[...] = (total[...] + nt(hot, message)).astype(BF)
-
-
-def edge_kernel(far, near, edge, gain, out, held, sem):
+    split(total[...] + nt(hot, message), low, high)
+
+
+def edge_kernel(far, edge, near, gain, *rest):
+    out, held, sem = rest[-3:]
     copies = []
-    for q in range(4):
+    for q in (3, 0, 1, 2):
         size = NEAR_M if q < 3 else FAR
         part = slice(q * NEAR_M, q * NEAR_M + size)
-        message = near[q] if q < 3 else far[...]
+        message = near[:, q * NM_PAD : (q + 1) * NM_PAD] if q < 3 else far[...]
         held[part, :] = rows_out(message, edge[part, :], gain[...], size)
         rows = pl.ds(q * NEAR_M, size)
         copies.append(pltpu.make_async_copy(held.at[rows, :], out.at[rows, :], sem.at[q]))
@@ -324,12 +365,21 @@
         copy.wait()
 
 
-def band_parts(partial):
-    count = lax.axis_size("band")
-    moved = [
-        lax.ppermute(partial, "band", [(i, (i + k) % count) for i in range(count)]) for k in range(1, count)
-    ]
-    return [partial] + moved
+def swap(x, bit):
+    return lax.ppermute(x, "band", [(i, i ^ bit) for i in range(4)])
+
+
+def band_stages(low, high, first_args, first, second_args, second):
+    low, high, first_args = lax.optimization_barrier((low, high, first_args))
+    low_in, high_in = swap(low, 1), swap(high, 3)
+    first_out = first(first_args)
+    low_in, high_in, first_out = lax.optimization_barrier((low_in, high_in, first_out))
+    half = kept((NODES // 2, D), BF)
+    low = call(add_kernel, [half], "VV", (low, low_in), name="band_add_low")
+    low_in = swap(low, 3)
+    high = call(add_kernel, [half], "VV", (high, high_in), name="band_add_high")
+    high_in = swap(high, 1)
+    return (low, low_in, high, high_in), first_out, second(second_args)
 
 
 def halo(x):
@@ -377,58 +427,89 @@
     gains = [g.reshape(1, D) for g in (grid_gain, encode_gain, node_gain, process_gain, update_gain)]
     before, after = halo(grid_latent)
     weight = kept((D, D), BF)
-    asks, wst, rt, gt, wt, sender, kept_grid, receiver, feature = call(
-        start_kernel,
-        (kept((N_REG, 2 * FAR_G), jnp.int32), weight, kept((D, NODES), BF), kept((D, 16), BF), weight),
-        "KHHHHHHKKK",
-        (encode_sender, mesh_sender, encode_send, encode_receive, mesh_latent, encode_geometry, encode_output)
-        + (grid_latent, encode_receiver, encode_feature),
-        flops=2 * 10**9,
-        name="encode_start",
+    asks, sender = call(
+        asks_kernel,
+        [kept((N_REG, 2 * FAR_G), jnp.int32)],
+        "KH",
+        (encode_sender, mesh_sender),
+        name="far_asks",
     )
     asked = exchange(asks)
+    asks_sent, w_send = lax.optimization_barrier((asks, encode_send))
+    wst, rt, gt, wt, receiver, grid, feature = call(
+        weights_kernel,
+        (weight, kept((D, NODES), BF), kept((D, 16), BF), weight, kept((1, NG + FAR), jnp.int32)),
+        "HSHHHHHKK",
+        (w_send, encode_live, encode_receive, mesh_latent, encode_receiver, encode_geometry, encode_output)
+        + (grid_latent, encode_feature),
+        flops=3 * 10**9,
+        name="encode_weights",
+    )
+    begun = call(
+        first_edges_kernel,
+        [kept((NODES, D), BF)],
+        "VVVVVVVV",
+        (grid, wst, sender, receiver, feature, rt, gt, wt),
+        flops=3 * 10**9,
+        name="encode_begin",
+    )
+    asked, wst, begun = lax.optimization_barrier((asked, wst, begun))
+    outgoing = call(send_kernel, [shape((FAR, D), BF)], "VV", (asked, grid), flops=3 * 10**8, name="encode_rows")
+    far_rows = exchange(outgoing.reshape(N_REG, FAR_G, D)).reshape(FAR, D)
+    outgoing, wst = lax.optimization_barrier((outgoing, wst))
     total = call(
-        own_kernel,
+        near_edges_kernel,
         [kept((NODES, D), F32)],
-        "SVVVVVVVV",
-        (encode_live, kept_grid, wst, sender, receiver, feature, rt, gt, wt),
-        flops=6 * 10**9,
-        name="encode_own",
-    )
-    outgoing = call(
-        send_kernel, [shape((FAR, D), BF)], "VV", (asked, kept_grid), flops=3 * 10**8, name="encode_rows"
-    )
-    far_rows = exchange(outgoing.reshape(N_REG, FAR_G, D)).reshape(FAR, D)
-    total = call(
-        sides_kernel,
-        [kept((NODES, D), F32)],
-        "SHVVVVVVVHV",
-        (encode_live, before, wst, sender, receiver, feature, rt, gt, wt, after, total),
-        flops=11 * 10**9,
-        name="encode_sides",
-    )
-    partial = call(
+        "VVVVVVVVVHH",
+        (grid, wst, sender, receiver, feature, rt, gt, wt, begun, before, after),
+        flops=15 * 10**9,
+        name="encode_near",
+    )
+    half = kept((NODES // 2, D), BF)
+    low, high, e_weight, e_rows = call(
         far_kernel,
-        [kept((NODES, D), BF)],
-        "SVVVVVVVV",
-        (encode_live, receiver, feature, rt, gt, wst, far_rows, wt, total),
+        (half, half),
+        "VVVVVVVVKK",
+        (receiver, feature, rt, gt, wst, far_rows, wt, total, process_edge, mesh_edge),
         flops=10**9,
         name="encode_far",
     )
-    partial, later_edge = lax.optimization_barrier((partial, mesh_edge))
-    parts = band_parts(partial)
-    prepared = call(
-        prepare_kernel,
-        (pltpu.HBM((3, D, NM_PAD), BF), kept((D, FAR), BF), weight, weight, weight),
-        "HHHHHKKKKKKK",
-        (process_edge, later_edge, process_send, process_receive, process_output)
-        + (node_first, node_second, mesh_latent, gains[1], gains[2], mesh_sender, mesh_receiver),
-        scratch=[pltpu.VMEM((3, D, NM_PAD), BF), pltpu.SemaphoreType.DMA],
-        out_specs=(HBM, VMEM, VMEM, VMEM, VMEM),
-        flops=3 * 10**9,
-        name="process_prepare",
-    )
-    near_pre, far_pre, p_wst, p_wrt, p_wt, n_first, n_second, n_mesh, n_eg, n_gain, m_sender, m_receiver = prepared
+
+    def edge_terms(args):
+        return call(
+            edge_terms_kernel,
+            (pltpu.HBM((D, 3 * NM_PAD), BF), kept((D, FAR), BF)),
+            "VVKKKKKKKKKK",
+            args,
+            scratch=[pltpu.VMEM((D, 3 * NM_PAD), BF), pltpu.SemaphoreType.DMA],
+            out_specs=(HBM, VMEM),
+            flops=2 * 10**9,
+            name="process_terms",
+        )
+
+    def prepare(args):
+        return call(
+            prepare_kernel,
+            (weight, weight, weight, kept((8, 3 * NM_PAD), jnp.int32), kept((1, FAR), jnp.int32)),
+            "VSVVVV",
+            args,
+            flops=2 * 10**9,
+            name="process_prepare",
+        )
+
+    (low, low_in, high, high_in), terms, _ = band_stages(
+        low,
+        high,
+        (e_weight, e_rows, process_send, mesh_sender, mesh_receiver, process_receive, process_output)
+        + (node_first, node_second, mesh_latent, gains[1], gains[2]),
+        edge_terms,
+        (),
+        lambda args: (),
+    )
+    near_pre, far_pre, p_send, p_from, p_to, p_recv, p_out, n_first, n_second, n_mesh, n_eg, n_gain = terms
+    low, high, p_send = lax.optimization_barrier((low, high, p_send))
+    p_wst, p_wrt, p_wt, near_index, far_index = prepare((p_send, mesh_live, p_from, p_to, p_recv, p_out))
+    parts = (low, low_in, high, high_in)
     mid, rows, pt = call(
         node_kernel,
         (kept((NODES, D), BF), shape((FAR, D), BF), kept((D, NODES), BF)),
@@ -441,47 +522,63 @@
     before_mid, after_mid = halo(mid)
     m_total, near_sent = call(
         near_kernel,
-        (kept((NODES, D), F32), pltpu.HBM((3, D, NM_PAD), BF)),
-        "SVVVVVVVHV",
-        (mesh_live, p_wst, mid, before_mid, after_mid, m_sender, m_receiver, pt, near_pre, p_wt),
-        scratch=[pltpu.VMEM((3, D, NM_PAD), BF), pltpu.SemaphoreType.DMA],
+        (kept((NODES, D), F32), pltpu.HBM((D, 3 * NM_PAD), BF)),
+        "HVVVVVVV",
+        (near_pre, p_wst, mid, before_mid, after_mid, near_index, pt, p_wt),
+        scratch=[pltpu.VMEM((D, 3 * NM_PAD), BF), pltpu.SemaphoreType.DMA],
         out_specs=(VMEM, HBM),
         flops=4 * 10**9,
         name="process_near",
     )
-    m_partial, far_sent = call(
+    low, high, far_sent, r_edge = call(
         last_kernel,
-        (kept((NODES, D), BF), kept((D, FAR), BF)),
-        "SVVVVVVV",
-        (mesh_live, m_receiver, pt, far_pre, p_wst, far_mesh, p_wt, m_total),
+        (half, half, kept((D, FAR), BF)),
+        "VVVVVVVK",
+        (far_index, pt, far_pre, p_wst, far_mesh, p_wt, m_total, mesh_edge),
         flops=10**9,
         name="process_far",
     )
-    m_partial, grid_rows = lax.optimization_barrier((m_partial, grid_latent))
-    m_parts = band_parts(m_partial)
-    edge_out, m_gain = call(
-        edge_kernel,
-        [pltpu.HBM((M2M, D), BF)],
-        "VHHK",
-        (far_sent, near_sent, mesh_edge, gains[3]),
-        scratch=[pltpu.VMEM((M2M, D), BF), pltpu.SemaphoreType.DMA((4,))],
+
+    def edge_rows(args):
+        return call(
+            edge_kernel,
+            [pltpu.HBM((M2M, D), BF)],
+            "VVHKKKKKKKK",
+            args,
+            scratch=[pltpu.VMEM((M2M, D), BF), pltpu.SemaphoreType.DMA((4,))],
+            out_specs=[HBM],
+            flops=3 * 10**9,
+            name="process_rows",
+        )
+
+    (low, low_in, high, high_in), from_rows, _ = band_stages(
+        low,
+        high,
+        (far_sent, r_edge, near_sent, gains[3], grid_latent, grid_first, grid_second, gains[0])
+        + (update_first, update_second, gains[4]),
+        edge_rows,
+        (),
+        lambda args: (),
+    )
+    edge_out, m_gain, g_rows, g_first, g_second, g_gain, u_first, u_second, u_gain = from_rows
+    low, high, g_rows = lax.optimization_barrier((low, high, g_rows))
+    grid_out = call(
+        grid_kernel,
+        [pltpu.HBM((GRID, D), BF)],
+        "VVVV",
+        (g_rows, g_first, g_second, g_gain),
+        scratch=[pltpu.VMEM((GRID, D), BF), pltpu.SemaphoreType.DMA((4,))],
         out_specs=[HBM],
         flops=3 * 10**9,
-        name="process_rows",
-    )
-    grid_out, u_first, u_second, u_gain = call(
-        grid_kernel,
-        [shape((GRID, D), BF)],
-        "HHHHKKK",
-        (grid_rows, grid_first, grid_second, gains[0], update_first, update_second, gains[4]),
-        flops=3 * 10**9,
         name="grid_nodes",
     )
+    grid_out, u_gain = lax.optimization_barrier((grid_out, u_gain))
+    parts = (low, low_in, high, high_in)
     mesh_out = call(
         update_kernel,
         [shape((NODES, D), BF)],
         "VVVVVVVVV",
-        (mid, *m_parts, m_gain, u_first, u_second, u_gain),
+        (mid, *parts, m_gain, u_first, u_second, u_gain),
         flops=10**9,
         name="mesh_update",
     )

time: 107 us -> 98.8 us (0.923)
  waiting for transfers between devices: 16.4 us -> 8.6 us
  starting transfers between devices: 35 us -> 38 us
  Pallas kernels: 52.3 us -> 49.9 us
    ppermute x6 -> x8, waiting for transfers between devices: 13.3 us -> 4.39 us  [swap(): return lax.ppermute(x, 'band', [(i, i ^ bit) for i in range(4)])]
    ppermute x6 -> x8, starting transfers between devices: 7.74 us -> 13.6 us  [swap(): return lax.ppermute(x, 'band', [(i, i ^ bit) for i in range(4)])]
    all_to_all x3, starting transfers between devices: 17.7 us -> 14.2 us  [exchange(): return lax.all_to_all(x, 'region', split_axis=0, concat_axis=0, tiled=True)]
    all_to_all x3, waiting for transfers between devices: 0.7 us -> 4.03 us  [exchange(): return lax.all_to_all(x, 'region', split_axis=0, concat_axis=0, tiled=True)]
    pallas_call x12 -> x18, Pallas kernels: 52.3 us -> 49.9 us  [call(): pl.pallas_call(body, out_shape=out_shape, in_specs=[place[spec] for spec...]
    ppermute x4, waiting for transfers between devices: 2.37 us -> 0.18 us  [halo(): return (lax.ppermute(x, 'region', up), lax.ppermute(x, 'region', down))]
  transfers between devices with their start and end apart: 13 -> 15, of which waited for: 6 -> 8; matrix products, arithmetic and copies ran while one was open for 0% -> 0% of each run, Pallas kernels for 43% -> 43%
where the time goes in v4:
time: 98.8 us; the launch traced here: 98.2 us
  Pallas kernels  49.9 us (51%)
  starting transfers between devices  38 us (38%)
  waiting for transfers between devices  8.6 us (9%)
    pallas_call x18, Pallas kernels, call(): pl.pallas_call(body, out_shape=out_shape, in_specs=[place[spec] for spec...  49.9 us
    all_to_all x3, starting transfers between devices, exchange(): return lax.all_to_all(x, 'region', split_axis=0, concat_axis=0, tiled=True)  14.2 us
    ppermute x8, starting transfers between devices, swap(): return lax.ppermute(x, 'band', [(i, i ^ bit) for i in range(4)])  13.6 us
    ppermute x4, starting transfers between devices, halo(): return (lax.ppermute(x, 'region', up), lax.ppermute(x, 'region', down))  10.2 us
    ppermute x8, waiting for transfers between devices, swap(): return lax.ppermute(x, 'band', [(i, i ^ bit) for i in range(4)])  4.39 us
    all_to_all x3, waiting for transfers between devices, exchange(): return lax.all_to_all(x, 'region', split_axis=0, concat_axis=0, tiled=True)  4.03 us
  transfers between devices with their start and end apart: 15, of which 8 were waited for; matrix products, arithmetic and copies ran while one was open for 0% of the time, Pallas kernels for 43%

profile of v4, /device:TPU:0, one launch (start us, length us, event | category | flops | bytes accessed | tf_op | source)
XLA Modules:
  0.0 98.2 jit_solution(3832063178048107863)
XLA Ops:
  0.7 5.0 %collective-permute-start.1 = (bf16[1024,512]{1,0:T(8,128)(2,1)}, bf16[1024,512]{1,0:T(8,128)(2,1)}, u32[]{:S(2)}, u32[]{:S(2)}) collective-permute-start(bf16[1024,512]{1,0:T(8,128)(2,1)} %refs_4_.3), channel_id=1, source_target_pairs={{1,0},{2,1},{3,2},{4,3},{5,4},{6,5},{7,6},{8,7},{9,8},{10,9},{11,1... | collective-permute-start | bytes 3145736 | tf_op jit(solution)/shard_map/ppermute | solution.py:389
  5.8 1.7 %far_asks.1 = (s32[32,16]{1,0:T(8,128)}, s32[6400]{0:T(1024)S(1)}) custom-call(s32[6400]{0:T(1024)} %refs_0_.1, s32[1984]{0:T(1024)} %refs_3_.2), custom_call_target="tpu_custom_call" | custom-call | bytes 1048576 | tf_op jit(solution)/shard_map/far_asks/pallas_call | solution.py:119
  7.5 4.1 %all-to-all-start = ((s32[32,1,16]{2,1,0:T(1,128)}), s32[32,1,16]{2,1,0:T(1,128)S(1)}, u32[]{:S(2)}, u32[]{:S(2)}) async-start(s32[32,1,16]{2,1,0:T(1,128)} %bitcast.1), calls=%async_computation | async-start | bytes 32768 | tf_op jit(solution)/shard_map/all_to_all | solution.py:393
  11.6 3.6 %encode_weights.1 = (bf16[512,512]{1,0:T(8,128)(2,1)S(1)}, bf16[512,256]{1,0:T(8,128)(2,1)S(1)}, bf16[512,16]{1,0:T(8,128)(2,1)S(1)}, bf16[512,512]{1,0:T(8,128)...) custom-call(bf16[512,512]{1,0:T(8,128)(2,1)} %refs_0_.2, s32[1,35]{1,0:T(1,128)} %refs_1_.4, ...), custom_call_target="tpu_custom_call" | custom-call | flops 3000000000 | bytes 1048576 | tf_op jit(solution)/shard_map/encode_weights/pallas_call | solution.py:119
  15.2 3.4 %encode_begin.1.refs_8_ = bf16[256,512]{1,0:T(8,128)(2,1)S(1)} custom-call(bf16[1024,512]{1,0:T(8,128)(2,1)S(1)} %get-tuple-element.123.refs_0_.refs_1_, bf16[512,512]{1,0:T(8,128)(2,1)S(1)} %get-tuple-element.128.refs_1_.refs_4_, s32[6400]{0:T(1024)S(1)} %get-tuple-element.124.refs_2_, s32[1,6400]{1,0:T(1,128)S(1)} %get-tuple-element.118.refs_3_.refs_0_, ...), custom_call_target="tpu_custom_call" | custom-call | flops 3000000000 | bytes 1048576 | tf_op jit(solution)/shard_map/encode_begin/pallas_call | solution.py:119
  21.5 6.2 %all-to-all-start.1 = ((bf16[32,8,512]{2,1,0:T(8,128)(2,1)}), bf16[32,8,512]{2,1,0:T(8,128)(2,1)S(1)}, u32[]{:S(2)}, u32[]{:S(2)}) async-start(bf16[32,8,512]{2,1,0:T(8,128)(2,1)} %bitcast.3), calls=%async_computation.1 | async-start | bytes 524288 | tf_op jit(solution)/shard_map/all_to_all | solution.py:393
  28.7 15.1 %encode_near.1.refs_7_ = f32[256,512]{1,0:T(8,128)S(1)} custom-call(bf16[1024,512]{1,0:T(8,128)(2,1)S(1)} %get-tuple-element.123.refs_0_.refs_1_, bf16[512,512]{1,0:T(8,128)(2,1)S(1)} %get-tuple-element.128.refs_1_.refs_4_, s32[6400]{0:T(1024)S(1)} %get-tuple-element.124.refs_2_, s32[1,6400]{1,0:T(1,128)S(1)} %get-tuple-element.118.refs_3_.refs_0_, ...), custom_call_target="tpu_custom_call" | custom-call | flops 15000000512 | bytes 1048576 | tf_op jit(solution)/shard_map/encode_near/pallas_call | solution.py:119
  43.8 2.1 %encode_far.1 = (bf16[128,512]{1,0:T(8,128)(2,1)S(1)}, bf16[128,512]{1,0:T(8,128)(2,1)S(1)}, bf16[512,512]{1,0:T(8,128)(2,1)S(1)}, bf16[1984,512]{1,0:T(8,128)(2,1)S(1)}) custom-call(s32[1,6400]{1,0:T(1,128)S(1)} %get-tuple-element.118.refs_3_.refs_0_, f32[4,6400]{1,0:T(4,128)S(1)} %get-tuple-element.119.refs_4_.refs_1_, ...), custom_call_target="tpu_custom_call" | custom-call | flops 1000000000 | bytes 1048576 | tf_op jit(solution)/shard_map/encode_far/pallas_call | solution.py:119
  46.0 2.1 %collective-permute-start.2 = (bf16[128,512]{1,0:T(8,128)(2,1)S(1)}, bf16[128,512]{1,0:T(8,128)(2,1)S(1)}, u32[]{:S(2)}, u32[]{:S(2)}) collective-permute-start(bf16[128,512]{1,0:T(8,128)(2,1)S(1)} %get-tuple-element.134.refs_0_), channel_id=1, source_target_pairs={{0,32},{32,0},{64,96},{96,64},{1,33},{33,1},{65,97},{97,65},{2,34}... | collective-permute-start | bytes 393224 | tf_op jit(solution)/shard_map/ppermute | solution.py:369
  48.0 2.5 %collective-permute-start.3 = (bf16[128,512]{1,0:T(8,128)(2,1)S(1)}, bf16[128,512]{1,0:T(8,128)(2,1)S(1)}, u32[]{:S(2)}, u32[]{:S(2)}) collective-permute-start(bf16[128,512]{1,0:T(8,128)(2,1)S(1)} %get-tuple-element.135.refs_0_), channel_id=1, source_target_pairs={{0,96},{32,64},{64,32},{96,0},{1,97},{33,65},{65,33},{97,1},{2,98}... | collective-permute-start | bytes 393224 | tf_op jit(solution)/shard_map/ppermute | solution.py:369
  50.6 3.5 %process_terms.1 = (bf16[512,1920]{1,0:T(8,128)(2,1)}, bf16[512,256]{1,0:T(8,128)(2,1)S(1)}, bf16[512,512]{1,0:T(8,128)(2,1)S(1)}, s32[1984]{0:T(1024)S(1)}, s32...) custom-call(bf16[512,512]{1,0:T(8,128)(2,1)S(1)} %get-tuple-element., ...), custom_call_target="tpu_custom_call" | custom-call | flops 2000000000 | bytes 1048576 | tf_op jit(solution)/shard_map/process_terms/pallas_call | solution.py:119
  55.3 2.2 %collective-permute-start.4 = (bf16[128,512]{1,0:T(8,128)(2,1)S(1)}, bf16[128,512]{1,0:T(8,128)(2,1)S(1)}, u32[]{:S(2)}, u32[]{:S(2)}) collective-permute-start(bf16[128,512]{1,0:T(8,128)(2,1)S(1)} %band_add_low.2.refs_2_), channel_id=1, source_target_pairs={{0,96},{32,64},{64,32},{96,0},{1,97},{33,65},{65,33},{97,1},{2,98}... | collective-permute-start | bytes 393224 | tf_op jit(solution)/shard_map/ppermute | solution.py:369
  59.6 1.9 %collective-permute-done.4.refs_3_ = bf16[128,512]{1,0:T(8,128)(2,1)S(1)} collective-permute-done((bf16[128,512]{1,0:T(8,128)(2,1)S(1)}, bf16[128,512]{1,0:T(8,128)(2,1)S(1)}, u32[]{:S(2)}, u32[]{:S(2)}) %collective-permute-start.4) | collective-permute-done | bytes 131104 | tf_op jit(solution)/shard_map/ppermute | solution.py:369
  61.5 1.8 %mesh_nodes.1 = (bf16[256,512]{1,0:T(8,128)(2,1)S(1)}, bf16[256,512]{1,0:T(8,128)(2,1)}, bf16[512,256]{1,0:T(8,128)(2,1)S(1)}) custom-call(s32[32,16]{1,0:T(8,128)S(1)} %bitcast.16, bf16[256,512]{1,0:T(8,128)(2,1)S(1)} %get-tuple-element.169.refs_1_, bf16[128,512]{1,0:T(8,128)(2,1)S(1)} %band_add_low.2.refs_2_, ...), custom_call_target="tpu_custom_call" | custom-call | flops 1000000000 | bytes 1048576 | tf_op jit(solution)/shard_map/mesh_nodes/pallas_call | solution.py:119
  63.3 5.1 %collective-permute-start.7 = (bf16[256,512]{1,0:T(8,128)(2,1)S(1)}, bf16[256,512]{1,0:T(8,128)(2,1)S(1)}, u32[]{:S(2)}, u32[]{:S(2)}) collective-permute-start(bf16[256,512]{1,0:T(8,128)(2,1)S(1)} %get-tuple-element.183.refs_2_.refs_0_), channel_id=1, source_target_pairs={{1,0},{2,1},{3,2},{4,3},{5,4},{6,5},{7,6},{8,7},{9,8},{10,9},{11,1... | collective-permute-start | bytes 786440 | tf_op jit(solution)/shard_map/ppermute | solution.py:389
  68.4 3.9 %all-to-all-start.2 = ((bf16[32,8,512]{2,1,0:T(8,128)(2,1)}), bf16[32,8,512]{2,1,0:T(8,128)(2,1)S(1)}, u32[]{:S(2)}, u32[]{:S(2)}) async-start(bf16[32,8,512]{2,1,0:T(8,128)(2,1)} %bitcast.7), calls=%async_computation.2 | async-start | bytes 524288 | tf_op jit(solution)/shard_map/all_to_all | solution.py:393
  72.5 6.2 %process_near.1 = (f32[256,512]{1,0:T(8,128)S(1)}, bf16[512,1920]{1,0:T(8,128)(2,1)}) custom-call(bf16[512,1920]{1,0:T(8,128)(2,1)} %get-tuple-element.182.refs_0_, bf16[512,512]{1,0:T(8,128)(2,1)S(1)} %get-tuple-element.179.refs_1_.refs_3_, bf16[256,512]{1,0:T(8,128)(2,1)S(1)} %get-tuple-element.183.refs_2_.refs_0_, ...), custom_call_target="tpu_custom_call" | custom-call | flops 4000000000 | bytes 1048576 | tf_op jit(solution)/shard_map/process_near/pallas_call | solution.py:119
  78.7 2.5 %all-to-all-done.2 = bf16[32,8,512]{2,1,0:T(8,128)(2,1)S(1)} async-done(((bf16[32,8,512]{2,1,0:T(8,128)(2,1)}), bf16[32,8,512]{2,1,0:T(8,128)(2,1)S(1)}, u32[]{:S(2)}, u32[]{:S(2)}) %all-to-all-start.2) | async-done | bytes 262176 | tf_op jit(solution)/shard_map/all_to_all | solution.py:393
  81.2 1.6 %process_far.1 = (bf16[128,512]{1,0:T(8,128)(2,1)S(1)}, bf16[128,512]{1,0:T(8,128)(2,1)S(1)}, bf16[512,256]{1,0:T(8,128)(2,1)S(1)}, bf16[1984,512]{1,0:T(8,128)(2,1)S(1)}) custom-call(s32[1,256]{1,0:T(1,128)S(1)} %get-tuple-element.168.refs_0_, bf16[512,256]{1,0:T(8,128)(2,1)S(1)} %get-tuple-element.177.refs_6_.refs_1_, ...), custom_call_target="tpu_custom_call" | custom-call | flops 1000000000 | bytes 1048576 | tf_op jit(solution)/shard_map/process_far/pallas_call | solution.py:119
  83.1 2.6 %collective-permute-start.9 = (bf16[128,512]{1,0:T(8,128)(2,1)S(1)}, bf16[128,512]{1,0:T(8,128)(2,1)S(1)}, u32[]{:S(2)}, u32[]{:S(2)}) collective-permute-start(bf16[128,512]{1,0:T(8,128)(2,1)S(1)} %get-tuple-element.192.refs_0_), channel_id=1, source_target_pairs={{0,96},{32,64},{64,32},{96,0},{1,97},{33,65},{65,33},{97,1},{2,98}... | collective-permute-start | bytes 393224 | tf_op jit(solution)/shard_map/ppermute | solution.py:369
  85.8 3.3 %process_rows.1 = (bf16[1984,512]{1,0:T(8,128)(2,1)}, f32[1,512]{1,0:T(1,128)S(1)}, bf16[1024,512]{1,0:T(8,128)(2,1)S(1)}, bf16[512,512]{1,0:T(8,128)(2,1)S(1)},...) custom-call(bf16[512,256]{1,0:T(8,128)(2,1)S(1)} %get-tuple-element., ...), custom_call_target="tpu_custom_call" | custom-call | flops 3000000000 | bytes 1048576 | tf_op jit(solution)/shard_map/process_rows/pallas_call | solution.py:119
  90.4 2.4 %collective-permute-start.10 = (bf16[128,512]{1,0:T(8,128)(2,1)S(1)}, bf16[128,512]{1,0:T(8,128)(2,1)S(1)}, u32[]{:S(2)}, u32[]{:S(2)}) collective-permute-start(bf16[128,512]{1,0:T(8,128)(2,1)S(1)} %band_add_low.3.refs_1_), channel_id=1, source_target_pairs={{0,96},{32,64},{64,32},{96,0},{1,97},{33,65},{65,33},{97,1},{2,98}... | collective-permute-start | bytes 393224 | tf_op jit(solution)/shard_map/ppermute | solution.py:369
  92.9 2.9 %grid_nodes.1 = bf16[1024,512]{1,0:T(8,128)(2,1)} custom-call(bf16[1024,512]{1,0:T(8,128)(2,1)S(1)} %get-tuple-element.216.refs_0_, bf16[512,512]{1,0:T(8,128)(2,1)S(1)} %get-tuple-element.217.refs_1_, bf16[512,512]{1,0:T(8,128)(2,1)S(1)} %get-tuple-element.218.refs_2_, f32[1,512]{1,0:T(1,128)S(1)} %get-tuple-element.219.refs_3_), custom_call_target="tpu_custom_call" | custom-call | flops 3000000000 | bytes 1048576 | tf_op jit(solution)/shard_map/grid_nodes/pallas_call | solution.py:119
  96.6 1.6 %mesh_update.1 = bf16[256,512]{1,0:T(8,128)(2,1)} custom-call(bf16[256,512]{1,0:T(8,128)(2,1)S(1)} %get-tuple-element.183.refs_2_.refs_0_, bf16[128,512]{1,0:T(8,128)(2,1)S(1)} %band_add_low.3.refs_1_, bf16[128,512]{1,0:T(8,128)(2,1)S(1)} %collective-permute-done.10.refs_2_, bf16[128,512]{1,0:T(8,128)(2,1)S(1)} %band_add_high.3.refs_3_, ...), custom_call_target="tpu_custom_call" | custom-call | flops 1000000000 | bytes 1048576 | tf_op jit(solution)/shard_map/mesh_update/pallas_call | solution.py:119
  (28 shorter events, 9.9 us)
Async XLA Ops:
  0.6 27.1 %collective-permute-start = (bf16[1024,512]{1,0:T(8,128)(2,1)}, bf16[1024,512]{1,0:T(8,128)(2,1)}, u32[]{:S(2)}, u32[]{:S(2)}) collective-permute-start(bf16[1024,512]{1,0:T(8,128)(2,1)} %refs_4_.3), channel_id=1, source_target_pairs={{0,1},{1,2},{2,3},{3,4},{4,5},{5,6},{6,7},{7,8},{8,9},{9,10},{10,1... | collective-permute-start | bytes 3145736 | tf_op jit(solution)/shard_map/ppermute | solution.py:389
  0.7 27.1 %collective-permute-start.1 = (bf16[1024,512]{1,0:T(8,128)(2,1)}, bf16[1024,512]{1,0:T(8,128)(2,1)}, u32[]{:S(2)}, u32[]{:S(2)}) collective-permute-start(bf16[1024,512]{1,0:T(8,128)(2,1)} %refs_4_.3), channel_id=1, source_target_pairs={{1,0},{2,1},{3,2},{4,3},{5,4},{6,5},{7,6},{8,7},{9,8},{10,9},{11,1... | collective-permute-start | bytes 3145736 | tf_op jit(solution)/shard_map/ppermute | solution.py:389
  7.5 12.6 %all-to-all-start = ((s32[32,1,16]{2,1,0:T(1,128)}), s32[32,1,16]{2,1,0:T(1,128)S(1)}, u32[]{:S(2)}, u32[]{:S(2)}) async-start(s32[32,1,16]{2,1,0:T(1,128)} %bitcast.1), calls=%async_computation | async-start | bytes 32768 | tf_op jit(solution)/shard_map/all_to_all | solution.py:393
  18.5 9.2 %copy-start = (bf16[256,512]{1,0:T(8,128)(2,1)}, bf16[256,512]{1,0:T(8,128)(2,1)S(1)}, u32[]{:S(2)}) copy-start(bf16[256,512]{1,0:T(8,128)(2,1)S(1)} %encode_begin.1.refs_8_) | copy-start | bytes 786436
  21.5 22.3 %all-to-all-start.1 = ((bf16[32,8,512]{2,1,0:T(8,128)(2,1)}), bf16[32,8,512]{2,1,0:T(8,128)(2,1)S(1)}, u32[]{:S(2)}, u32[]{:S(2)}) async-start(bf16[32,8,512]{2,1,0:T(8,128)(2,1)} %bitcast.3), calls=%async_computation.1 | async-start | bytes 524288 | tf_op jit(solution)/shard_map/all_to_all | solution.py:393
  27.8 1.0 copy-start.1
  46.0 8.2 %collective-permute-start.2 = (bf16[128,512]{1,0:T(8,128)(2,1)S(1)}, bf16[128,512]{1,0:T(8,128)(2,1)S(1)}, u32[]{:S(2)}, u32[]{:S(2)}) collective-permute-start(bf16[128,512]{1,0:T(8,128)(2,1)S(1)} %get-tuple-element.134.refs_0_), channel_id=1, source_target_pairs={{0,32},{32,0},{64,96},{96,64},{1,33},{33,1},{65,97},{97,65},{2,34}... | collective-permute-start | bytes 393224 | tf_op jit(solution)/shard_map/ppermute | solution.py:369
  48.0 6.4 %collective-permute-start.3 = (bf16[128,512]{1,0:T(8,128)(2,1)S(1)}, bf16[128,512]{1,0:T(8,128)(2,1)S(1)}, u32[]{:S(2)}, u32[]{:S(2)}) collective-permute-start(bf16[128,512]{1,0:T(8,128)(2,1)S(1)} %get-tuple-element.135.refs_0_), channel_id=1, source_target_pairs={{0,96},{32,64},{64,32},{96,0},{1,97},{33,65},{65,33},{97,1},{2,98}... | collective-permute-start | bytes 393224 | tf_op jit(solution)/shard_map/ppermute | solution.py:369
  54.5 5.0 %collective-permute-start.5 = (bf16[128,512]{1,0:T(8,128)(2,1)S(1)}, bf16[128,512]{1,0:T(8,128)(2,1)S(1)}, u32[]{:S(2)}, u32[]{:S(2)}) collective-permute-start(bf16[128,512]{1,0:T(8,128)(2,1)S(1)} %band_add_high.2.refs_4_), channel_id=1, source_target_pairs={{0,32},{32,0},{64,96},{96,64},{1,33},{33,1},{65,97},{97,65},{2,34}... | collective-permute-start | bytes 393224 | tf_op jit(solution)/shard_map/ppermute | solution.py:369
  55.3 6.2 %collective-permute-start.4 = (bf16[128,512]{1,0:T(8,128)(2,1)S(1)}, bf16[128,512]{1,0:T(8,128)(2,1)S(1)}, u32[]{:S(2)}, u32[]{:S(2)}) collective-permute-start(bf16[128,512]{1,0:T(8,128)(2,1)S(1)} %band_add_low.2.refs_2_), channel_id=1, source_target_pairs={{0,96},{32,64},{64,32},{96,0},{1,97},{33,65},{65,33},{97,1},{2,98}... | collective-permute-start | bytes 393224 | tf_op jit(solution)/shard_map/ppermute | solution.py:369
  63.3 9.1 %collective-permute-start.6 = (bf16[256,512]{1,0:T(8,128)(2,1)S(1)}, bf16[256,512]{1,0:T(8,128)(2,1)S(1)}, u32[]{:S(2)}, u32[]{:S(2)}) collective-permute-start(bf16[256,512]{1,0:T(8,128)(2,1)S(1)} %get-tuple-element.183.refs_2_.refs_0_), channel_id=1, source_target_pairs={{0,1},{1,2},{2,3},{3,4},{4,5},{5,6},{6,7},{7,8},{8,9},{9,10},{10,1... | collective-permute-start | bytes 786440 | tf_op jit(solution)/shard_map/ppermute | solution.py:389
  63.3 9.1 %collective-permute-start.7 = (bf16[256,512]{1,0:T(8,128)(2,1)S(1)}, bf16[256,512]{1,0:T(8,128)(2,1)S(1)}, u32[]{:S(2)}, u32[]{:S(2)}) collective-permute-start(bf16[256,512]{1,0:T(8,128)(2,1)S(1)} %get-tuple-element.183.refs_2_.refs_0_), channel_id=1, source_target_pairs={{1,0},{2,1},{3,2},{4,3},{5,4},{6,5},{7,6},{8,7},{9,8},{10,9},{11,1... | collective-permute-start | bytes 786440 | tf_op jit(solution)/shard_map/ppermute | solution.py:389
  68.4 12.8 %all-to-all-start.2 = ((bf16[32,8,512]{2,1,0:T(8,128)(2,1)}), bf16[32,8,512]{2,1,0:T(8,128)(2,1)S(1)}, u32[]{:S(2)}, u32[]{:S(2)}) async-start(bf16[32,8,512]{2,1,0:T(8,128)(2,1)} %bitcast.7), calls=%async_computation.2 | async-start | bytes 524288 | tf_op jit(solution)/shard_map/all_to_all | solution.py:393
  82.8 6.3 %collective-permute-start.8 = (bf16[128,512]{1,0:T(8,128)(2,1)S(1)}, bf16[128,512]{1,0:T(8,128)(2,1)S(1)}, u32[]{:S(2)}, u32[]{:S(2)}) collective-permute-start(bf16[128,512]{1,0:T(8,128)(2,1)S(1)} %get-tuple-element.191.refs_0_), channel_id=1, source_target_pairs={{0,32},{32,0},{64,96},{96,64},{1,33},{33,1},{65,97},{97,65},{2,34}... | collective-permute-start | bytes 393224 | tf_op jit(solution)/shard_map/ppermute | solution.py:369
  83.1 6.7 %collective-permute-start.9 = (bf16[128,512]{1,0:T(8,128)(2,1)S(1)}, bf16[128,512]{1,0:T(8,128)(2,1)S(1)}, u32[]{:S(2)}, u32[]{:S(2)}) collective-permute-start(bf16[128,512]{1,0:T(8,128)(2,1)S(1)} %get-tuple-element.192.refs_0_), channel_id=1, source_target_pairs={{0,96},{32,64},{64,32},{96,0},{1,97},{33,65},{65,33},{97,1},{2,98}... | collective-permute-start | bytes 393224 | tf_op jit(solution)/shard_map/ppermute | solution.py:369
  89.9 5.8 %collective-permute-start.11 = (bf16[128,512]{1,0:T(8,128)(2,1)S(1)}, bf16[128,512]{1,0:T(8,128)(2,1)S(1)}, u32[]{:S(2)}, u32[]{:S(2)}) collective-permute-start(bf16[128,512]{1,0:T(8,128)(2,1)S(1)} %band_add_high.3.refs_3_), channel_id=1, source_target_pairs={{0,32},{32,0},{64,96},{96,64},{1,33},{33,1},{65,97},{97,65},{2,34}... | collective-permute-start | bytes 393224 | tf_op jit(solution)/shard_map/ppermute | solution.py:369
  90.4 6.2 %collective-permute-start.10 = (bf16[128,512]{1,0:T(8,128)(2,1)S(1)}, bf16[128,512]{1,0:T(8,128)(2,1)S(1)}, u32[]{:S(2)}, u32[]{:S(2)}) collective-permute-start(bf16[128,512]{1,0:T(8,128)(2,1)S(1)} %band_add_low.3.refs_1_), channel_id=1, source_target_pairs={{0,96},{32,64},{64,32},{96,0},{1,97},{33,65},{65,33},{97,1},{2,98}... | collective-permute-start | bytes 393224 | tf_op jit(solution)/shard_map/ppermute | solution.py:369

commit v5 on v4

--- a/solution.py
+++ b/solution.py
@@ -145,16 +145,12 @@
     return pltpu.VMEM(dims, kind)
 
 
-def encode_block(q, halves, table, rt, gt, wt, sender, receiver, feature):
-    value = None
-    for i in halves:
-        part = slice(q * NEAR_G + i, q * NEAR_G + i + HALF)
-        hot = one_hot(NODES, receiver[:, part])
-        pre = nn(table, one_hot(GRID, sender[part].reshape(1, HALF))) + nn(rt, hot)
-        pre = pre + nn(gt, feature_rows(feature[:, part]))
-        term = nt(hot, messages_t(pre, wt))
-        value = term if value is None else value + term
-    return value
+def encode_part(begin, size, table, rest, wt, sender, receiver, feature):
+    part = slice(begin, begin + size)
+    hot = one_hot(NODES, receiver[:, part])
+    index = sender[part].reshape(1, size)
+    pre = nn(table, one_hot(GRID, index)) + nn(rest[:, :NODES], hot) + nn(rest[:, NODES:], feature_rows(feature[:, part]))
+    return nt(hot, messages_t(pre, wt))
 
 
 def slots_to_rows(row, first):
@@ -173,11 +169,11 @@
 
 
 def weights_kernel(w_send, live, w_recv, mesh, receiver, geo, w_out, *rest):
-    wst, rt, gt, wt, targets = rest[2:]
+    wst, tables, wt, targets = rest[2:]
     eye = identity(D)
     wst[...] = (0.5 * nt(eye, w_send[...])).astype(BF)
     wrt = nt(eye, w_recv[...]).astype(BF)
-    rt[...] = (0.5 * nt(wrt, mesh[...])).astype(BF)
+    tables[:, :NODES] = (0.5 * nt(wrt, mesh[...])).astype(BF)
     lane = lax.broadcasted_iota(jnp.int32, (1, NEAR_G), 1)
     for q in range(3):
         part = slice(q * NEAR_G, (q + 1) * NEAR_G)
@@ -186,29 +182,31 @@
     half = 0.5 * geo[...]
     high = half.astype(BF).astype(F32)
     stacked = jnp.concatenate([high, high, half - high, jnp.zeros((4, D), F32)], axis=0)
-    gt[...] = nt(eye, stacked.astype(BF)).astype(BF)
+    tables[:, NODES:] = nt(eye, stacked.astype(BF)).astype(BF)
     wt[...] = centred_t(w_out[...])
 
 
-def first_edges_kernel(grid, wst, sender, receiver, feature, rt, gt, wt, out):
-    table = nt(wst[...], grid[...]).astype(BF)
-    out[...] = encode_block(1, (0,), table, rt[...], gt[...], wt[...], sender, receiver, feature).astype(BF)
-
-
-def near_edges_kernel(grid, wst, sender, receiver, feature, rt, gt, wt, begun, before, after, out):
-    value = begun[...].astype(F32)
-    for q, rows in ((1, grid), (0, before), (2, after)):
-        table = nt(wst[...], rows[...]).astype(BF)
-        halves = (HALF,) if q == 1 else (0, HALF)
-        value = value + encode_block(q, halves, table, rt[...], gt[...], wt[...], sender, receiver, feature)
-    out[...] = value
-
-
-def far_kernel(receiver, feature, rt, gt, wst, rows, wt, total, *rest):
+def first_edges_kernel(grid, wst, tables, sender, receiver, feature, wt, out, table):
+    table[...] = nt(wst[...], grid[...]).astype(BF)
+    value = encode_part(NEAR_G, HALF, table[...], tables[...], wt[...], sender, receiver, feature)
+    out[...] = value.astype(BF)
+
+
+def near_edges_kernel(table, wst, tables, sender, receiver, feature, wt, before, after, out):
+    rest = (tables[...], wt[...], sender, receiver, feature)
+    out[...] = encode_part(NEAR_G + HALF, HALF, table[...], *rest)
+    for q, rows in ((0, before), (2, after)):
+        side = nt(wst[...], rows[...]).astype(BF)
+        value = encode_part(q * NEAR_G, HALF, side, *rest)
+        out[...] += value + encode_part(q * NEAR_G + HALF, HALF, side, *rest)
+
+
+def far_kernel(tables, receiver, feature, rows, wt, total, begun, low, high):
     part = slice(NG, NG + FAR)
     hot = one_hot(NODES, receiver[:, part])
-    pre = nn(rt[...], hot) + nn(gt[...], feature_rows(feature[:, part])) + nt(wst[...], rows[...])
-    split(total[...] + nt(hot, messages_t(pre, wt[...])), *rest[-2:])
+    pre = nn(tables[:, :NODES], hot) + nn(tables[:, NODES:], feature_rows(feature[:, part])) + nt(identity(D), rows[...])
+    value = total[...] + nt(hot, messages_t(pre, wt[...]))
+    split(value + begun[...].astype(F32), low, high)
 
 
 def split(value, low, high):
@@ -230,8 +228,8 @@
     return (node == index).astype(F32).astype(BF)
 
 
-def send_kernel(asked, grid, out):
-    out[...] = nn(asked_hot(asked[...], 0, GRID), grid[...]).astype(BF)
+def send_kernel(asked, table, out):
+    out[...] = nt(asked_hot(asked[...], 0, GRID), table[...]).astype(BF)
 
 
 def norm(values):
@@ -263,10 +261,12 @@
     return (jnp.concatenate([plus(low, low_in), plus(high, high_in)], axis=0) * edge_gain[...]).astype(BF)
 
 
-def node_kernel(asked, mesh, p0, p1, p2, p3, edge_gain, w_first, w_second, gain, wrt, mid, rows, pt):
+def node_kernel(asked, mesh, p0, p1, p2, p3, edge_gain, w_first, w_second, gain, wst, wrt, mid, rows, sent, pt):
     value = mlp(mesh[...], band_total(p0, p1, p2, p3, edge_gain), w_first, w_second, gain)
+    table = nt(wst[...], value).astype(BF)
+    sent[...] = table
+    rows[...] = nn(asked_hot(asked[...], FAR_G, NODES), value).astype(BF)
     mid[...] = value
-    rows[...] = nn(asked_hot(asked[...], FAR_G, NODES), value).astype(BF)
     pt[...] = nt(wrt[...], value).astype(BF)
 
 
@@ -276,12 +276,11 @@
 
 def grid_kernel(latent, w_first, w_second, gain, out, held, sems):
     copies = []
-    for i in range(4):
-        part = slice(i * NODES, (i + 1) * NODES)
+    for i in range(2):
+        part, where = slice(i * GRID // 2, (i + 1) * GRID // 2), pl.ds(i * GRID // 2, GRID // 2)
         rows = latent[part, :]
         update = norm(nn(silu(nn(rows, w_first[...])), w_second[...])) * gain[...]
         held[part, :] = (rows.astype(F32) + update).astype(BF)
-        where = pl.ds(i * NODES, NODES)
         copies.append(pltpu.make_async_copy(held.at[where, :], out.at[where, :], sems.at[i]))
         copies[-1].start()
     for copy in copies:
@@ -300,14 +299,18 @@
 
 
 def edge_terms_kernel(w_edge, edge, *rest):
-    near, far, held, sem = rest[-4:]
+    near, far, held, sems = rest[-4:]
     wet = (0.5 * nt(identity(D), w_edge[...])).astype(BF)
+    far[...] = nt(wet, edge[NM:, :]).astype(BF)
+    copies = []
     for q in range(3):
-        held[:, q * NM_PAD : (q + 1) * NM_PAD] = nt(wet, edge[q * NEAR_M : q * NEAR_M + NM_PAD, :]).astype(BF)
-    copy = pltpu.make_async_copy(held, near, sem)
-    copy.start()
-    far[...] = nt(wet, edge[NM:, :]).astype(BF)
-    copy.wait()
+        part = slice(q * NM_PAD, (q + 1) * NM_PAD)
+        held[:, part] = nt(wet, edge[q * NEAR_M : q * NEAR_M + NM_PAD, :]).astype(BF)
+        where = pl.ds(q * NM_PAD, NM_PAD)
+        copies.append(pltpu.make_async_copy(held.at[:, where], near.at[:, where], sems.at[q]))
+        copies[-1].start()
+    for copy in copies:
+        copy.wait()
 
 
 def prepare_kernel(w_send, live, sender, receiver, w_recv, w_out, wst, wrt, wt, near, far):
@@ -324,16 +327,15 @@
     far[...] = jnp.where(far_live(live, FAR), receiver[NM:].reshape(1, FAR), -1)
 
 
-def near_kernel(edge_pre, wst, mid, before, after, index, pt, wt, total, sent, held, sem):
-    table = nt(wst[...], jnp.concatenate([before[...], mid[...], after[...]], axis=0)).astype(BF)
+def near_kernel(edge_pre, before, own, after, index, pt, wt, total, sent, held, base, sem):
     target = index[0:1, :]
     hot = one_hot(NODES, target)
     gathered = [
-        nn(table[:, q * NODES : (q + 1) * NODES], one_hot(NODES, index[1:2, q * NM_PAD : (q + 1) * NM_PAD]))
-        for q in range(3)
+        nn(table[...], one_hot(NODES, index[1:2, q * NM_PAD : (q + 1) * NM_PAD]))
+        for q, table in enumerate((before, own, after))
     ]
-    pre = nn(pt[...], hot) + jnp.concatenate(gathered, axis=1) + edge_pre[...].astype(F32)
-    message = messages_t(pre, wt[...], target >= 0)
+    base[...] = nn(pt[...], hot) + jnp.concatenate(gathered, axis=1)
+    message = messages_t(base[...] + edge_pre[...].astype(F32), wt[...], target >= 0)
     held[...] = message
     copy = pltpu.make_async_copy(held, sent, sem)
     copy.start()
@@ -436,52 +438,56 @@
     )
     asked = exchange(asks)
     asks_sent, w_send = lax.optimization_barrier((asks, encode_send))
-    wst, rt, gt, wt, receiver, grid, feature = call(
+    wst, tables, wt, receiver, grid, feature = call(
         weights_kernel,
-        (weight, kept((D, NODES), BF), kept((D, 16), BF), weight, kept((1, NG + FAR), jnp.int32)),
+        (weight, kept((D, NODES + 16), BF), weight, kept((1, NG + FAR), jnp.int32)),
         "HSHHHHHKK",
         (w_send, encode_live, encode_receive, mesh_latent, encode_receiver, encode_geometry, encode_output)
         + (grid_latent, encode_feature),
         flops=3 * 10**9,
         name="encode_weights",
-    )
-    begun = call(
+        grant=56,
+    )
+    begun, table = call(
         first_edges_kernel,
-        [kept((NODES, D), BF)],
-        "VVVVVVVV",
-        (grid, wst, sender, receiver, feature, rt, gt, wt),
+        (kept((NODES, D), BF), kept((D, GRID), BF)),
+        "VVVVVVV",
+        (grid, wst, tables, sender, receiver, feature, wt),
         flops=3 * 10**9,
         name="encode_begin",
-    )
-    asked, wst, begun = lax.optimization_barrier((asked, wst, begun))
-    outgoing = call(send_kernel, [shape((FAR, D), BF)], "VV", (asked, grid), flops=3 * 10**8, name="encode_rows")
+        grant=56,
+    )
+    asked, table = lax.optimization_barrier((asked, table))
+    outgoing = call(send_kernel, [shape((FAR, D), BF)], "VV", (asked, table), flops=3 * 10**8, name="encode_rows")
     far_rows = exchange(outgoing.reshape(N_REG, FAR_G, D)).reshape(FAR, D)
-    outgoing, wst = lax.optimization_barrier((outgoing, wst))
+    outgoing, table = lax.optimization_barrier((outgoing, table))
     total = call(
         near_edges_kernel,
         [kept((NODES, D), F32)],
-        "VVVVVVVVVHH",
-        (grid, wst, sender, receiver, feature, rt, gt, wt, begun, before, after),
+        "VVVVVVVHH",
+        (table, wst, tables, sender, receiver, feature, wt, before, after),
         flops=15 * 10**9,
         name="encode_near",
+        grant=56,
     )
     half = kept((NODES // 2, D), BF)
-    low, high, e_weight, e_rows = call(
+    low, high = call(
         far_kernel,
         (half, half),
-        "VVVVVVVVKK",
-        (receiver, feature, rt, gt, wst, far_rows, wt, total, process_edge, mesh_edge),
+        "VVVVVVH",
+        (tables, receiver, feature, far_rows, wt, total, begun),
         flops=10**9,
         name="encode_far",
+        grant=56,
     )
 
     def edge_terms(args):
         return call(
             edge_terms_kernel,
             (pltpu.HBM((D, 3 * NM_PAD), BF), kept((D, FAR), BF)),
-            "VVKKKKKKKKKK",
+            "HHKKKKKKKKKK",
             args,
-            scratch=[pltpu.VMEM((D, 3 * NM_PAD), BF), pltpu.SemaphoreType.DMA],
+            scratch=[pltpu.VMEM((D, 3 * NM_PAD), BF), pltpu.SemaphoreType.DMA((3,))],
             out_specs=(HBM, VMEM),
             flops=2 * 10**9,
             name="process_terms",
@@ -500,7 +506,7 @@
     (low, low_in, high, high_in), terms, _ = band_stages(
         low,
         high,
-        (e_weight, e_rows, process_send, mesh_sender, mesh_receiver, process_receive, process_output)
+        (process_edge, mesh_edge, process_send, mesh_sender, mesh_receiver, process_receive, process_output)
         + (node_first, node_second, mesh_latent, gains[1], gains[2]),
         edge_terms,
         (),
@@ -510,31 +516,31 @@
     low, high, p_send = lax.optimization_barrier((low, high, p_send))
     p_wst, p_wrt, p_wt, near_index, far_index = prepare((p_send, mesh_live, p_from, p_to, p_recv, p_out))
     parts = (low, low_in, high, high_in)
-    mid, rows, pt = call(
+    mid, rows, own_table, pt = call(
         node_kernel,
-        (kept((NODES, D), BF), shape((FAR, D), BF), kept((D, NODES), BF)),
-        "VVVVVVVVVVV",
-        (asked, n_mesh, *parts, n_eg, n_first, n_second, n_gain, p_wrt),
+        (kept((NODES, D), BF), shape((FAR, D), BF), kept((D, NODES), BF), kept((D, NODES), BF)),
+        "VVVVVVVVVVVV",
+        (asked, n_mesh, *parts, n_eg, n_first, n_second, n_gain, p_wst, p_wrt),
         flops=10**9,
         name="mesh_nodes",
     )
     far_mesh = exchange(rows.reshape(N_REG, FAR_M, D)).reshape(FAR, D)
-    before_mid, after_mid = halo(mid)
+    before_table, after_table = halo(own_table)
     m_total, near_sent = call(
         near_kernel,
         (kept((NODES, D), F32), pltpu.HBM((D, 3 * NM_PAD), BF)),
-        "HVVVVVVV",
-        (near_pre, p_wst, mid, before_mid, after_mid, near_index, pt, p_wt),
-        scratch=[pltpu.VMEM((D, 3 * NM_PAD), BF), pltpu.SemaphoreType.DMA],
+        "HVVVVVV",
+        (near_pre, before_table, own_table, after_table, near_index, pt, p_wt),
+        scratch=[pltpu.VMEM((D, 3 * NM_PAD), kind) for kind in (BF, F32)] + [pltpu.SemaphoreType.DMA],
         out_specs=(VMEM, HBM),
         flops=4 * 10**9,
         name="process_near",
     )
-    low, high, far_sent, r_edge = call(
+    low, high, far_sent = call(
         last_kernel,
         (half, half, kept((D, FAR), BF)),
-        "VVVVVVVK",
-        (far_index, pt, far_pre, p_wst, far_mesh, p_wt, m_total, mesh_edge),
+        "VVVVVVV",
+        (far_index, pt, far_pre, p_wst, far_mesh, p_wt, m_total),
         flops=10**9,
         name="process_far",
     )
@@ -543,7 +549,7 @@
         return call(
             edge_kernel,
             [pltpu.HBM((M2M, D), BF)],
-            "VVHKKKKKKKK",
+            "VHHKKKKKKKK",
             args,
             scratch=[pltpu.VMEM((M2M, D), BF), pltpu.SemaphoreType.DMA((4,))],
             out_specs=[HBM],
@@ -554,7 +560,7 @@
     (low, low_in, high, high_in), from_rows, _ = band_stages(
         low,
         high,
-        (far_sent, r_edge, near_sent, gains[3], grid_latent, grid_first, grid_second, gains[0])
+        (far_sent, mesh_edge, near_sent, gains[3], grid_latent, grid_first, grid_second, gains[0])
         + (update_first, update_second, gains[4]),
         edge_rows,
         (),
@@ -567,7 +573,7 @@
         [pltpu.HBM((GRID, D), BF)],
         "VVVV",
         (g_rows, g_first, g_second, g_gain),
-        scratch=[pltpu.VMEM((GRID, D), BF), pltpu.SemaphoreType.DMA((4,))],
+        scratch=[pltpu.VMEM((GRID, D), BF), pltpu.SemaphoreType.DMA((2,))],
         out_specs=[HBM],
         flops=3 * 10**9,
         name="grid_nodes",

time: 98.8 us -> 96.9 us (0.981)
  starting transfers between devices: 38 us -> 35.9 us
  waiting for transfers between devices: 8.6 us -> 10.7 us
    ppermute x8, starting transfers between devices: 13.6 us -> 11.4 us  [swap(): return lax.ppermute(x, 'band', [(i, i ^ bit) for i in range(4)])]
    ppermute x8, waiting for transfers between devices: 4.39 us -> 6.09 us  [swap(): return lax.ppermute(x, 'band', [(i, i ^ bit) for i in range(4)])]
  transfers between devices with their start and end apart: 15 -> 15, of which waited for: 8 -> 8; matrix products, arithmetic and copies ran while one was open for 0% -> 0% of each run, Pallas kernels for 43% -> 44%
where the time goes in v5:
time: 96.9 us; the launch traced here: 96.5 us
  Pallas kernels  49.1 us (51%)
  starting transfers between devices  35.9 us (37%)
  waiting for transfers between devices  10.7 us (11%)
    pallas_call x18, Pallas kernels, call(): pl.pallas_call(body, out_shape=out_shape, in_specs=[place[spec] for spec...  49.1 us
    all_to_all x3, starting transfers between devices, exchange(): return lax.all_to_all(x, 'region', split_axis=0, concat_axis=0, tiled=True)  14.2 us
    ppermute x8, starting transfers between devices, swap(): return lax.ppermute(x, 'band', [(i, i ^ bit) for i in range(4)])  11.4 us
    ppermute x4, starting transfers between devices, halo(): return (lax.ppermute(x, 'region', up), lax.ppermute(x, 'region', down))  10.2 us
    ppermute x8, waiting for transfers between devices, swap(): return lax.ppermute(x, 'band', [(i, i ^ bit) for i in range(4)])  6.09 us
    all_to_all x3, waiting for transfers between devices, exchange(): return lax.all_to_all(x, 'region', split_axis=0, concat_axis=0, tiled=True)  4.45 us
  transfers between devices with their start and end apart: 15, of which 8 were waited for; matrix products, arithmetic and copies ran while one was open for 0% of the time, Pallas kernels for 44%

profile of v5, /device:TPU:0, one launch (start us, length us, event | category | flops | bytes accessed | tf_op | source)
XLA Modules:
  0.0 96.5 jit_solution(10552073060125573937)
XLA Ops:
  0.7 5.0 %collective-permute-start.1 = (bf16[1024,512]{1,0:T(8,128)(2,1)}, bf16[1024,512]{1,0:T(8,128)(2,1)}, u32[]{:S(2)}, u32[]{:S(2)}) collective-permute-start(bf16[1024,512]{1,0:T(8,128)(2,1)} %refs_4_.3), channel_id=1, source_target_pairs={{1,0},{2,1},{3,2},{4,3},{5,4},{6,5},{7,6},{8,7},{9,8},{10,9},{11,1... | collective-permute-start | bytes 3145736 | tf_op jit(solution)/shard_map/ppermute | solution.py:391
  5.8 1.7 %far_asks.1 = (s32[32,16]{1,0:T(8,128)}, s32[6400]{0:T(1024)S(1)}) custom-call(s32[6400]{0:T(1024)} %refs_0_.1, s32[1984]{0:T(1024)} %refs_3_.2), custom_call_target="tpu_custom_call" | custom-call | bytes 1048576 | tf_op jit(solution)/shard_map/far_asks/pallas_call | solution.py:119
  7.5 4.1 %all-to-all-start = ((s32[32,1,16]{2,1,0:T(1,128)}), s32[32,1,16]{2,1,0:T(1,128)S(1)}, u32[]{:S(2)}, u32[]{:S(2)}) async-start(s32[32,1,16]{2,1,0:T(1,128)} %bitcast.1), calls=%async_computation | async-start | bytes 32768 | tf_op jit(solution)/shard_map/all_to_all | solution.py:395
  11.6 3.6 %encode_weights.1 = (bf16[512,512]{1,0:T(8,128)(2,1)S(1)}, bf16[512,272]{1,0:T(8,128)(2,1)S(1)}, bf16[512,512]{1,0:T(8,128)(2,1)S(1)}, s32[1,6400]{1,0:T(1,128)S...) custom-call(bf16[512,512]{1,0:T(8,128)(2,1)} %refs_0_.2, s32[1,35]{1,0:T(1,128)} %refs_1_.4, ...), custom_call_target="tpu_custom_call" | custom-call | flops 3000000000 | bytes 1048576 | tf_op jit(solution)/shard_map/encode_weights/pallas_call | solution.py:119
  15.2 3.4 %encode_begin.1 = (bf16[256,512]{1,0:T(8,128)(2,1)S(1)}, bf16[512,1024]{1,0:T(8,128)(2,1)S(1)}) custom-call(bf16[1024,512]{1,0:T(8,128)(2,1)S(1)} %get-tuple-element.119.refs_0_, bf16[512,512]{1,0:T(8,128)(2,1)S(1)} %get-tuple-element.120.refs_1_, bf16[512,272]{1,0:T(8,128)(2,1)S(1)} %get-tuple-element.116.refs_2_.refs_0_, ...), custom_call_target="tpu_custom_call" | custom-call | flops 3000000000 | bytes 1048576 | tf_op jit(solution)/shard_map/encode_begin/pallas_call | solution.py:119
  18.6 1.5 %all-to-all-done = s32[32,1,16]{2,1,0:T(1,128)S(1)} async-done(((s32[32,1,16]{2,1,0:T(1,128)}), s32[32,1,16]{2,1,0:T(1,128)S(1)}, u32[]{:S(2)}, u32[]{:S(2)}) %all-to-all-start) | async-done | bytes 2080 | tf_op jit(solution)/shard_map/all_to_all | solution.py:395
  21.5 6.2 %all-to-all-start.1 = ((bf16[32,8,512]{2,1,0:T(8,128)(2,1)}), bf16[32,8,512]{2,1,0:T(8,128)(2,1)S(1)}, u32[]{:S(2)}, u32[]{:S(2)}) async-start(bf16[32,8,512]{2,1,0:T(8,128)(2,1)} %bitcast.3), calls=%async_computation.1 | async-start | bytes 524288 | tf_op jit(solution)/shard_map/all_to_all | solution.py:395
  27.8 14.5 %encode_near.1.refs_5_ = f32[256,512]{1,0:T(8,128)S(1)} custom-call(bf16[512,1024]{1,0:T(8,128)(2,1)S(1)} %get-tuple-element.126.refs_1_.refs_0_, bf16[512,512]{1,0:T(8,128)(2,1)S(1)} %get-tuple-element.120.refs_1_, bf16[512,272]{1,0:T(8,128)(2,1)S(1)} %get-tuple-element.116.refs_2_.refs_0_, s32[6400]{0:T(1024)S(1)} %get-tuple-element.121.refs_3_, ...), custom_call_target="tpu_custom_call" | custom-call | flops 15000000512 | bytes 1048576 | tf_op jit(solution)/shard_map/encode_near/pallas_call | solution.py:119
  43.7 2.1 %collective-permute-start.2 = (bf16[128,512]{1,0:T(8,128)(2,1)S(1)}, bf16[128,512]{1,0:T(8,128)(2,1)S(1)}, u32[]{:S(2)}, u32[]{:S(2)}) collective-permute-start(bf16[128,512]{1,0:T(8,128)(2,1)S(1)} %get-tuple-element.130.refs_0_), channel_id=1, source_target_pairs={{0,32},{32,0},{64,96},{96,64},{1,33},{33,1},{65,97},{97,65},{2,34}... | collective-permute-start | bytes 393224 | tf_op jit(solution)/shard_map/ppermute | solution.py:371
  45.8 2.5 %collective-permute-start.3 = (bf16[128,512]{1,0:T(8,128)(2,1)S(1)}, bf16[128,512]{1,0:T(8,128)(2,1)S(1)}, u32[]{:S(2)}, u32[]{:S(2)}) collective-permute-start(bf16[128,512]{1,0:T(8,128)(2,1)S(1)} %get-tuple-element.131.refs_0_), channel_id=1, source_target_pairs={{0,96},{32,64},{64,32},{96,0},{1,97},{33,65},{65,33},{97,1},{2,98}... | collective-permute-start | bytes 393224 | tf_op jit(solution)/shard_map/ppermute | solution.py:371
  48.3 4.3 %process_terms.1 = (bf16[512,1920]{1,0:T(8,128)(2,1)}, bf16[512,256]{1,0:T(8,128)(2,1)S(1)}, bf16[512,512]{1,0:T(8,128)(2,1)S(1)}, s32[1984]{0:T(1024)S(1)}, s32...) custom-call(bf16[512,512]{1,0:T(8,128)(2,1)} %refs_0_.3, ...), custom_call_target="tpu_custom_call" | custom-call | flops 2000000000 | bytes 1048576 | tf_op jit(solution)/shard_map/process_terms/pallas_call | solution.py:119
  55.3 1.5 %process_prepare.1 = (bf16[512,512]{1,0:T(8,128)(2,1)S(1)}, bf16[512,512]{1,0:T(8,128)(2,1)S(1)}, bf16[512,512]{1,0:T(8,128)(2,1)S(1)}, s32[8,1920]{1,0:T(8,128)S(1)}, s32[1,256]{1,0:T(1,128)S(1)}) custom-call(bf16[512,512]{1,0:T(8,128)(2,1)S(1)} %get-tuple-element.159.refs_0_, s32[1,35]{1,0:T(1,128)} %refs_1_.6, s32[1984]{0:T(1024)S(1)} %get-tuple-element.160.refs_2_, ...), custom_call_target="tpu_custom_call" | custom-call | flops 2000000000 | bytes 1048576 | tf_op jit(solution)/shard_map/process_prepare/pallas_call | solution.py:119
  57.9 2.1 %collective-permute-done.4.refs_3_ = bf16[128,512]{1,0:T(8,128)(2,1)S(1)} collective-permute-done((bf16[128,512]{1,0:T(8,128)(2,1)S(1)}, bf16[128,512]{1,0:T(8,128)(2,1)S(1)}, u32[]{:S(2)}, u32[]{:S(2)}) %collective-permute-start.4) | collective-permute-done | bytes 131104 | tf_op jit(solution)/shard_map/ppermute | solution.py:371
  60.0 1.9 %mesh_nodes.1 = (bf16[256,512]{1,0:T(8,128)(2,1)S(1)}, bf16[256,512]{1,0:T(8,128)(2,1)}, bf16[512,256]{1,0:T(8,128)(2,1)S(1)}, bf16[512,256]{1,0:T(8,128)(2,1)S(1)}) custom-call(s32[32,16]{1,0:T(8,128)S(1)} %bitcast.16, bf16[256,512]{1,0:T(8,128)(2,1)S(1)} %get-tuple-element.165.refs_1_, bf16[128,512]{1,0:T(8,128)(2,1)S(1)} %band_add_low.2.refs_2_, ...), custom_call_target="tpu_custom_call" | custom-call | flops 1000000000 | bytes 1048576 | tf_op jit(solution)/shard_map/mesh_nodes/pallas_call | solution.py:119
  61.9 5.1 %collective-permute-start.7 = (bf16[512,256]{1,0:T(8,128)(2,1)S(1)}, bf16[512,256]{1,0:T(8,128)(2,1)S(1)}, u32[]{:S(2)}, u32[]{:S(2)}) collective-permute-start(bf16[512,256]{1,0:T(8,128)(2,1)S(1)} %get-tuple-element.179.refs_2_), channel_id=1, source_target_pairs={{1,0},{2,1},{3,2},{4,3},{5,4},{6,5},{7,6},{8,7},{9,8},{10,9},{11,1... | collective-permute-start | bytes 786440 | tf_op jit(solution)/shard_map/ppermute | solution.py:391
  66.9 3.9 %all-to-all-start.2 = ((bf16[32,8,512]{2,1,0:T(8,128)(2,1)}), bf16[32,8,512]{2,1,0:T(8,128)(2,1)S(1)}, u32[]{:S(2)}, u32[]{:S(2)}) async-start(bf16[32,8,512]{2,1,0:T(8,128)(2,1)} %bitcast.7), calls=%async_computation.2 | async-start | bytes 524288 | tf_op jit(solution)/shard_map/all_to_all | solution.py:395
  71.0 5.8 %process_near.1 = (f32[256,512]{1,0:T(8,128)S(1)}, bf16[512,1920]{1,0:T(8,128)(2,1)}) custom-call(bf16[512,1920]{1,0:T(8,128)(2,1)} %get-tuple-element.178.refs_0_, bf16[512,256]{1,0:T(8,128)(2,1)S(1)} %collective-permute-done.6.refs_1_, bf16[512,256]{1,0:T(8,128)(2,1)S(1)} %get-tuple-element.179.refs_2_, ...), custom_call_target="tpu_custom_call" | custom-call | flops 4000000000 | bytes 1048576 | tf_op jit(solution)/shard_map/process_near/pallas_call | solution.py:119
  76.8 2.9 %all-to-all-done.2 = bf16[32,8,512]{2,1,0:T(8,128)(2,1)S(1)} async-done(((bf16[32,8,512]{2,1,0:T(8,128)(2,1)}), bf16[32,8,512]{2,1,0:T(8,128)(2,1)S(1)}, u32[]{:S(2)}, u32[]{:S(2)}) %all-to-all-start.2) | async-done | bytes 262176 | tf_op jit(solution)/shard_map/all_to_all | solution.py:395
  81.1 2.1 %collective-permute-start.9 = (bf16[128,512]{1,0:T(8,128)(2,1)S(1)}, bf16[128,512]{1,0:T(8,128)(2,1)S(1)}, u32[]{:S(2)}, u32[]{:S(2)}) collective-permute-start(bf16[128,512]{1,0:T(8,128)(2,1)S(1)} %get-tuple-element.187.refs_0_), channel_id=1, source_target_pairs={{0,96},{32,64},{64,32},{96,0},{1,97},{33,65},{65,33},{97,1},{2,98}... | collective-permute-start | bytes 393224 | tf_op jit(solution)/shard_map/ppermute | solution.py:371
  83.2 3.9 %process_rows.1 = (bf16[1984,512]{1,0:T(8,128)(2,1)}, f32[1,512]{1,0:T(1,128)S(1)}, bf16[1024,512]{1,0:T(8,128)(2,1)S(1)}, bf16[512,512]{1,0:T(8,128)(2,1)S(1)},...) custom-call(bf16[512,256]{1,0:T(8,128)(2,1)S(1)} %get-tuple-element., ...), custom_call_target="tpu_custom_call" | custom-call | flops 3000000000 | bytes 1048576 | tf_op jit(solution)/shard_map/process_rows/pallas_call | solution.py:119
  88.7 1.5 %collective-permute-start.10 = (bf16[128,512]{1,0:T(8,128)(2,1)S(1)}, bf16[128,512]{1,0:T(8,128)(2,1)S(1)}, u32[]{:S(2)}, u32[]{:S(2)}) collective-permute-start(bf16[128,512]{1,0:T(8,128)(2,1)S(1)} %band_add_low.3.refs_1_), channel_id=1, source_target_pairs={{0,96},{32,64},{64,32},{96,0},{1,97},{33,65},{65,33},{97,1},{2,98}... | collective-permute-start | bytes 393224 | tf_op jit(solution)/shard_map/ppermute | solution.py:371
  90.2 2.7 %grid_nodes.1 = bf16[1024,512]{1,0:T(8,128)(2,1)} custom-call(bf16[1024,512]{1,0:T(8,128)(2,1)S(1)} %get-tuple-element.211.refs_0_, bf16[512,512]{1,0:T(8,128)(2,1)S(1)} %get-tuple-element.212.refs_1_, bf16[512,512]{1,0:T(8,128)(2,1)S(1)} %get-tuple-element.213.refs_2_, f32[1,512]{1,0:T(1,128)S(1)} %get-tuple-element.214.refs_3_), custom_call_target="tpu_custom_call" | custom-call | flops 3000000000 | bytes 1048576 | tf_op jit(solution)/shard_map/grid_nodes/pallas_call | solution.py:119
  93.2 1.7 %collective-permute-done.10.refs_2_ = bf16[128,512]{1,0:T(8,128)(2,1)S(1)} collective-permute-done((bf16[128,512]{1,0:T(8,128)(2,1)S(1)}, bf16[128,512]{1,0:T(8,128)(2,1)S(1)}, u32[]{:S(2)}, u32[]{:S(2)}) %collective-permute-start.10) | collective-permute-done | bytes 131104 | tf_op jit(solution)/shard_map/ppermute | solution.py:371
  94.8 1.6 %mesh_update.1 = bf16[256,512]{1,0:T(8,128)(2,1)} custom-call(bf16[256,512]{1,0:T(8,128)(2,1)S(1)} %get-tuple-element.217.refs_0_, bf16[128,512]{1,0:T(8,128)(2,1)S(1)} %band_add_low.3.refs_1_, bf16[128,512]{1,0:T(8,128)(2,1)S(1)} %collective-permute-done.10.refs_2_, bf16[128,512]{1,0:T(8,128)(2,1)S(1)} %band_add_high.3.refs_3_, ...), custom_call_target="tpu_custom_call" | custom-call | flops 1000000000 | bytes 1048576 | tf_op jit(solution)/shard_map/mesh_update/pallas_call | solution.py:119
  (26 shorter events, 9.9 us)
Async XLA Ops:
  0.6 27.1 %collective-permute-start = (bf16[1024,512]{1,0:T(8,128)(2,1)}, bf16[1024,512]{1,0:T(8,128)(2,1)}, u32[]{:S(2)}, u32[]{:S(2)}) collective-permute-start(bf16[1024,512]{1,0:T(8,128)(2,1)} %refs_4_.3), channel_id=1, source_target_pairs={{0,1},{1,2},{2,3},{3,4},{4,5},{5,6},{6,7},{7,8},{8,9},{9,10},{10,1... | collective-permute-start | bytes 3145736 | tf_op jit(solution)/shard_map/ppermute | solution.py:391
  0.7 27.1 %collective-permute-start.1 = (bf16[1024,512]{1,0:T(8,128)(2,1)}, bf16[1024,512]{1,0:T(8,128)(2,1)}, u32[]{:S(2)}, u32[]{:S(2)}) collective-permute-start(bf16[1024,512]{1,0:T(8,128)(2,1)} %refs_4_.3), channel_id=1, source_target_pairs={{1,0},{2,1},{3,2},{4,3},{5,4},{6,5},{7,6},{8,7},{9,8},{10,9},{11,1... | collective-permute-start | bytes 3145736 | tf_op jit(solution)/shard_map/ppermute | solution.py:391
  7.5 12.6 %all-to-all-start = ((s32[32,1,16]{2,1,0:T(1,128)}), s32[32,1,16]{2,1,0:T(1,128)S(1)}, u32[]{:S(2)}, u32[]{:S(2)}) async-start(s32[32,1,16]{2,1,0:T(1,128)} %bitcast.1), calls=%async_computation | async-start | bytes 32768 | tf_op jit(solution)/shard_map/all_to_all | solution.py:395
  18.6 2.9 %copy-start = (bf16[256,512]{1,0:T(8,128)(2,1)}, bf16[256,512]{1,0:T(8,128)(2,1)S(1)}, u32[]{:S(2)}) copy-start(bf16[256,512]{1,0:T(8,128)(2,1)S(1)} %get-tuple-element.127.refs_6_) | copy-start | bytes 786436
  21.5 20.8 %all-to-all-start.1 = ((bf16[32,8,512]{2,1,0:T(8,128)(2,1)}), bf16[32,8,512]{2,1,0:T(8,128)(2,1)S(1)}, u32[]{:S(2)}, u32[]{:S(2)}) async-start(bf16[32,8,512]{2,1,0:T(8,128)(2,1)} %bitcast.3), calls=%async_computation.1 | async-start | bytes 524288 | tf_op jit(solution)/shard_map/all_to_all | solution.py:395
  43.7 8.9 %collective-permute-start.2 = (bf16[128,512]{1,0:T(8,128)(2,1)S(1)}, bf16[128,512]{1,0:T(8,128)(2,1)S(1)}, u32[]{:S(2)}, u32[]{:S(2)}) collective-permute-start(bf16[128,512]{1,0:T(8,128)(2,1)S(1)} %get-tuple-element.130.refs_0_), channel_id=1, source_target_pairs={{0,32},{32,0},{64,96},{96,64},{1,33},{33,1},{65,97},{97,65},{2,34}... | collective-permute-start | bytes 393224 | tf_op jit(solution)/shard_map/ppermute | solution.py:371
  45.8 6.9 %collective-permute-start.3 = (bf16[128,512]{1,0:T(8,128)(2,1)S(1)}, bf16[128,512]{1,0:T(8,128)(2,1)S(1)}, u32[]{:S(2)}, u32[]{:S(2)}) collective-permute-start(bf16[128,512]{1,0:T(8,128)(2,1)S(1)} %get-tuple-element.131.refs_0_), channel_id=1, source_target_pairs={{0,96},{32,64},{64,32},{96,0},{1,97},{33,65},{65,33},{97,1},{2,98}... | collective-permute-start | bytes 393224 | tf_op jit(solution)/shard_map/ppermute | solution.py:371
  52.7 5.2 %collective-permute-start.5 = (bf16[128,512]{1,0:T(8,128)(2,1)S(1)}, bf16[128,512]{1,0:T(8,128)(2,1)S(1)}, u32[]{:S(2)}, u32[]{:S(2)}) collective-permute-start(bf16[128,512]{1,0:T(8,128)(2,1)S(1)} %band_add_high.2.refs_4_), channel_id=1, source_target_pairs={{0,32},{32,0},{64,96},{96,64},{1,33},{33,1},{65,97},{97,65},{2,34}... | collective-permute-start | bytes 393224 | tf_op jit(solution)/shard_map/ppermute | solution.py:371
  53.8 6.2 %collective-permute-start.4 = (bf16[128,512]{1,0:T(8,128)(2,1)S(1)}, bf16[128,512]{1,0:T(8,128)(2,1)S(1)}, u32[]{:S(2)}, u32[]{:S(2)}) collective-permute-start(bf16[128,512]{1,0:T(8,128)(2,1)S(1)} %band_add_low.2.refs_2_), channel_id=1, source_target_pairs={{0,96},{32,64},{64,32},{96,0},{1,97},{33,65},{65,33},{97,1},{2,98}... | collective-permute-start | bytes 393224 | tf_op jit(solution)/shard_map/ppermute | solution.py:371
  61.9 9.1 %collective-permute-start.6 = (bf16[512,256]{1,0:T(8,128)(2,1)S(1)}, bf16[512,256]{1,0:T(8,128)(2,1)S(1)}, u32[]{:S(2)}, u32[]{:S(2)}) collective-permute-start(bf16[512,256]{1,0:T(8,128)(2,1)S(1)} %get-tuple-element.179.refs_2_), channel_id=1, source_target_pairs={{0,1},{1,2},{2,3},{3,4},{4,5},{5,6},{6,7},{7,8},{8,9},{9,10},{10,1... | collective-permute-start | bytes 786440 | tf_op jit(solution)/shard_map/ppermute | solution.py:391
  61.9 9.1 %collective-permute-start.7 = (bf16[512,256]{1,0:T(8,128)(2,1)S(1)}, bf16[512,256]{1,0:T(8,128)(2,1)S(1)}, u32[]{:S(2)}, u32[]{:S(2)}) collective-permute-start(bf16[512,256]{1,0:T(8,128)(2,1)S(1)} %get-tuple-element.179.refs_2_), channel_id=1, source_target_pairs={{1,0},{2,1},{3,2},{4,3},{5,4},{6,5},{7,6},{8,7},{9,8},{10,9},{11,1... | collective-permute-start | bytes 786440 | tf_op jit(solution)/shard_map/ppermute | solution.py:391
  66.9 12.8 %all-to-all-start.2 = ((bf16[32,8,512]{2,1,0:T(8,128)(2,1)}), bf16[32,8,512]{2,1,0:T(8,128)(2,1)S(1)}, u32[]{:S(2)}, u32[]{:S(2)}) async-start(bf16[32,8,512]{2,1,0:T(8,128)(2,1)} %bitcast.7), calls=%async_computation.2 | async-start | bytes 524288 | tf_op jit(solution)/shard_map/all_to_all | solution.py:395
  81.0 6.1 %collective-permute-start.8 = (bf16[128,512]{1,0:T(8,128)(2,1)S(1)}, bf16[128,512]{1,0:T(8,128)(2,1)S(1)}, u32[]{:S(2)}, u32[]{:S(2)}) collective-permute-start(bf16[128,512]{1,0:T(8,128)(2,1)S(1)} %get-tuple-element.186.refs_0_), channel_id=1, source_target_pairs={{0,32},{32,0},{64,96},{96,64},{1,33},{33,1},{65,97},{97,65},{2,34}... | collective-permute-start | bytes 393224 | tf_op jit(solution)/shard_map/ppermute | solution.py:371
  81.1 7.0 %collective-permute-start.9 = (bf16[128,512]{1,0:T(8,128)(2,1)S(1)}, bf16[128,512]{1,0:T(8,128)(2,1)S(1)}, u32[]{:S(2)}, u32[]{:S(2)}) collective-permute-start(bf16[128,512]{1,0:T(8,128)(2,1)S(1)} %get-tuple-element.187.refs_0_), channel_id=1, source_target_pairs={{0,96},{32,64},{64,32},{96,0},{1,97},{33,65},{65,33},{97,1},{2,98}... | collective-permute-start | bytes 393224 | tf_op jit(solution)/shard_map/ppermute | solution.py:371
  88.1 5.0 %collective-permute-start.11 = (bf16[128,512]{1,0:T(8,128)(2,1)S(1)}, bf16[128,512]{1,0:T(8,128)(2,1)S(1)}, u32[]{:S(2)}, u32[]{:S(2)}) collective-permute-start(bf16[128,512]{1,0:T(8,128)(2,1)S(1)} %band_add_high.3.refs_3_), channel_id=1, source_target_pairs={{0,32},{32,0},{64,96},{96,64},{1,33},{33,1},{65,97},{97,65},{2,34}... | collective-permute-start | bytes 393224 | tf_op jit(solution)/shard_map/ppermute | solution.py:371
  88.7 6.2 %collective-permute-start.10 = (bf16[128,512]{1,0:T(8,128)(2,1)S(1)}, bf16[128,512]{1,0:T(8,128)(2,1)S(1)}, u32[]{:S(2)}, u32[]{:S(2)}) collective-permute-start(bf16[128,512]{1,0:T(8,128)(2,1)S(1)} %band_add_low.3.refs_1_), channel_id=1, source_target_pairs={{0,96},{32,64},{64,32},{96,0},{1,97},{33,65},{65,33},{97,1},{2,98}... | collective-permute-start | bytes 393224 | tf_op jit(solution)/shard_map/ppermute | solution.py:371

commit v6 on v5

--- a/solution.py
+++ b/solution.py
@@ -201,18 +201,12 @@
         out[...] += value + encode_part(q * NEAR_G + HALF, HALF, side, *rest)
 
 
-def far_kernel(tables, receiver, feature, rows, wt, total, begun, low, high):
+def far_kernel(tables, receiver, feature, rows, wt, total, begun, out):
     part = slice(NG, NG + FAR)
     hot = one_hot(NODES, receiver[:, part])
     pre = nn(tables[:, :NODES], hot) + nn(tables[:, NODES:], feature_rows(feature[:, part])) + nt(identity(D), rows[...])
     value = total[...] + nt(hot, messages_t(pre, wt[...]))
-    split(value + begun[...].astype(F32), low, high)
-
-
-def split(value, low, high):
-    value = value.astype(BF)
-    low[...] = value[: NODES // 2, :]
-    high[...] = value[NODES // 2 :, :]
+    out[...] = (value + begun[...].astype(F32)).astype(BF)
 
 
 def asked_hot(asked, first, nodes):
@@ -257,12 +251,12 @@
     out[...] = plus(a, b).astype(BF)
 
 
-def band_total(low, low_in, high, high_in, edge_gain):
-    return (jnp.concatenate([plus(low, low_in), plus(high, high_in)], axis=0) * edge_gain[...]).astype(BF)
-
-
-def node_kernel(asked, mesh, p0, p1, p2, p3, edge_gain, w_first, w_second, gain, wst, wrt, mid, rows, sent, pt):
-    value = mlp(mesh[...], band_total(p0, p1, p2, p3, edge_gain), w_first, w_second, gain)
+def band_total(a, b, edge_gain):
+    return (plus(a, b) * edge_gain[...]).astype(BF)
+
+
+def node_kernel(asked, mesh, p0, p1, edge_gain, w_first, w_second, gain, wst, wrt, mid, rows, sent, pt):
+    value = mlp(mesh[...], band_total(p0, p1, edge_gain), w_first, w_second, gain)
     table = nt(wst[...], value).astype(BF)
     sent[...] = table
     rows[...] = nn(asked_hot(asked[...], FAR_G, NODES), value).astype(BF)
@@ -270,8 +264,8 @@
     pt[...] = nt(wrt[...], value).astype(BF)
 
 
-def update_kernel(mid, p0, p1, p2, p3, edge_gain, w_first, w_second, gain, out):
-    out[...] = mlp(mid[...], band_total(p0, p1, p2, p3, edge_gain), w_first, w_second, gain)
+def update_kernel(mid, p0, p1, edge_gain, w_first, w_second, gain, out):
+    out[...] = mlp(mid[...], band_total(p0, p1, edge_gain), w_first, w_second, gain)
 
 
 def grid_kernel(latent, w_first, w_second, gain, out, held, sems):
@@ -344,12 +338,12 @@
 
 
 def last_kernel(target, pt, edge_pre, wst, rows, wt, total, *rest):
-    low, high, sent = rest[-3:]
+    out, sent = rest[-2:]
     hot = one_hot(NODES, target[...])
     pre = edge_pre[...].astype(F32) + nn(pt[...], hot) + nt(wst[...], rows[...])
     message = messages_t(pre, wt[...], target[...] >= 0)
     sent[...] = message
-    split(total[...] + nt(hot, message), low, high)
+    out[...] = (total[...] + nt(hot, message)).astype(BF)
 
 
 def edge_kernel(far, edge, near, gain, *rest):
@@ -367,21 +361,23 @@
         copy.wait()
 
 
-def swap(x, bit):
-    return lax.ppermute(x, "band", [(i, i ^ bit) for i in range(4)])
-
-
-def band_stages(low, high, first_args, first, second_args, second):
-    low, high, first_args = lax.optimization_barrier((low, high, first_args))
-    low_in, high_in = swap(low, 1), swap(high, 3)
+def swap(x, even, odd):
+    regions = lax.axis_size("region")
+    pairs = [
+        (band * regions + region, (band ^ (odd if region % 2 else even)) * regions + region)
+        for band in range(lax.axis_size("band"))
+        for region in range(regions)
+    ]
+    return lax.ppermute(x, ("band", "region"), pairs)
+
+
+def band_stages(part, first_args, first):
+    part, first_args = lax.optimization_barrier((part, first_args))
+    part_in = swap(part, 1, 3)
     first_out = first(first_args)
-    low_in, high_in, first_out = lax.optimization_barrier((low_in, high_in, first_out))
-    half = kept((NODES // 2, D), BF)
-    low = call(add_kernel, [half], "VV", (low, low_in), name="band_add_low")
-    low_in = swap(low, 3)
-    high = call(add_kernel, [half], "VV", (high, high_in), name="band_add_high")
-    high_in = swap(high, 1)
-    return (low, low_in, high, high_in), first_out, second(second_args)
+    part_in, first_out = lax.optimization_barrier((part_in, first_out))
+    part = call(add_kernel, [kept((NODES, D), BF)], "VV", (part, part_in), name="band_add")
+    return part, swap(part, 3, 1), first_out
 
 
 def halo(x):
@@ -470,10 +466,9 @@
         name="encode_near",
         grant=56,
     )
-    half = kept((NODES // 2, D), BF)
-    low, high = call(
+    part = call(
         far_kernel,
-        (half, half),
+        [kept((NODES, D), BF)],
         "VVVVVVH",
         (tables, receiver, feature, far_rows, wt, total, begun),
         flops=10**9,
@@ -503,24 +498,20 @@
             name="process_prepare",
         )
 
-    (low, low_in, high, high_in), terms, _ = band_stages(
-        low,
-        high,
+    part, part_in, terms = band_stages(
+        part,
         (process_edge, mesh_edge, process_send, mesh_sender, mesh_receiver, process_receive, process_output)
         + (node_first, node_second, mesh_latent, gains[1], gains[2]),
         edge_terms,
-        (),
-        lambda args: (),
     )
     near_pre, far_pre, p_send, p_from, p_to, p_recv, p_out, n_first, n_second, n_mesh, n_eg, n_gain = terms
-    low, high, p_send = lax.optimization_barrier((low, high, p_send))
+    part, p_send = lax.optimization_barrier((part, p_send))
     p_wst, p_wrt, p_wt, near_index, far_index = prepare((p_send, mesh_live, p_from, p_to, p_recv, p_out))
-    parts = (low, low_in, high, high_in)
     mid, rows, own_table, pt = call(
         node_kernel,
         (kept((NODES, D), BF), shape((FAR, D), BF), kept((D, NODES), BF), kept((D, NODES), BF)),
-        "VVVVVVVVVVVV",
-        (asked, n_mesh, *parts, n_eg, n_first, n_second, n_gain, p_wst, p_wrt),
+        "VVVVVVVVVV",
+        (asked, n_mesh, part, part_in, n_eg, n_first, n_second, n_gain, p_wst, p_wrt),
         flops=10**9,
         name="mesh_nodes",
     )
@@ -536,9 +527,9 @@
         flops=4 * 10**9,
         name="process_near",
     )
-    low, high, far_sent = call(
+    part, far_sent = call(
         last_kernel,
-        (half, half, kept((D, FAR), BF)),
+        (kept((NODES, D), BF), kept((D, FAR), BF)),
         "VVVVVVV",
         (far_index, pt, far_pre, p_wst, far_mesh, p_wt, m_total),
         flops=10**9,
@@ -557,17 +548,14 @@
             name="process_rows",
         )
 
-    (low, low_in, high, high_in), from_rows, _ = band_stages(
-        low,
-        high,
+    part, part_in, from_rows = band_stages(
+        part,
         (far_sent, mesh_edge, near_sent, gains[3], grid_latent, grid_first, grid_second, gains[0])
         + (update_first, update_second, gains[4]),
         edge_rows,
-        (),
-        lambda args: (),
     )
     edge_out, m_gain, g_rows, g_first, g_second, g_gain, u_first, u_second, u_gain = from_rows
-    low, high, g_rows = lax.optimization_barrier((low, high, g_rows))
+    part, g_rows = lax.optimization_barrier((part, g_rows))
     grid_out = call(
         grid_kernel,
         [pltpu.HBM((GRID, D), BF)],
@@ -579,12 +567,11 @@
         name="grid_nodes",
     )
     grid_out, u_gain = lax.optimization_barrier((grid_out, u_gain))
-    parts = (low, low_in, high, high_in)
     mesh_out = call(
         update_kernel,
         [shape((NODES, D), BF)],
-        "VVVVVVVVV",
-        (mid, *parts, m_gain, u_first, u_second, u_gain),
+        "VVVVVVV",
+        (mid, part, part_in, m_gain, u_first, u_second, u_gain),
         flops=10**9,
         name="mesh_update",
     )

time: 96.9 us -> 96.3 us (level)
  starting transfers between devices: 35.9 us -> 34.3 us
    ppermute x8 -> x4, starting transfers between devices: 11.4 us -> 9.87 us  [swap(): return lax.ppermute(x, ('band', 'region'), pairs)]
    ppermute x8 -> x4, waiting for transfers between devices: 6.09 us -> 7.01 us  [swap(): return lax.ppermute(x, ('band', 'region'), pairs)]
    pallas_call x18 -> x16, Pallas kernels: 49.1 us -> 49.1 us  [call(): pl.pallas_call(body, out_shape=out_shape, in_specs=[place[spec] for spec...]
  transfers between devices with their start and end apart: 15 -> 11, of which waited for: 8 -> 7; matrix products, arithmetic and copies ran while one was open for 0% -> 0% of each run, Pallas kernels for 44% -> 45%
where the time goes in v6:
time: 96.3 us; the launch traced here: 95.8 us
  Pallas kernels  49.1 us (51%)
  starting transfers between devices  34.3 us (36%)
  waiting for transfers between devices  11.6 us (12%)
    pallas_call x16, Pallas kernels, call(): pl.pallas_call(body, out_shape=out_shape, in_specs=[place[spec] for spec...  49.1 us
    all_to_all x3, starting transfers between devices, exchange(): return lax.all_to_all(x, 'region', split_axis=0, concat_axis=0, tiled=True)  14.2 us
    ppermute x4, starting transfers between devices, halo(): return (lax.ppermute(x, 'region', up), lax.ppermute(x, 'region', down))  10.2 us
    ppermute x4, starting transfers between devices, swap(): return lax.ppermute(x, ('band', 'region'), pairs)  9.87 us
    ppermute x4, waiting for transfers between devices, swap(): return lax.ppermute(x, ('band', 'region'), pairs)  7.01 us
    all_to_all x3, waiting for transfers between devices, exchange(): return lax.all_to_all(x, 'region', split_axis=0, concat_axis=0, tiled=True)  4.45 us
  transfers between devices with their start and end apart: 11, of which 7 were waited for; matrix products, arithmetic and copies ran while one was open for 0% of the time, Pallas kernels for 45%

profile of v6, /device:TPU:0, one launch (start us, length us, event | category | flops | bytes accessed | tf_op | source)
XLA Modules:
  0.0 95.8 jit_solution(9487208382046258441)
XLA Ops:
  0.7 5.0 %collective-permute-start.1 = (bf16[1024,512]{1,0:T(8,128)(2,1)}, bf16[1024,512]{1,0:T(8,128)(2,1)}, u32[]{:S(2)}, u32[]{:S(2)}) collective-permute-start(bf16[1024,512]{1,0:T(8,128)(2,1)} %refs_4_.3), channel_id=1, source_target_pairs={{1,0},{2,1},{3,2},{4,3},{5,4},{6,5},{7,6},{8,7},{9,8},{10,9},{11,1... | collective-permute-start | bytes 3145736 | tf_op jit(solution)/shard_map/ppermute | solution.py:387
  5.8 1.7 %far_asks.1 = (s32[32,16]{1,0:T(8,128)}, s32[6400]{0:T(1024)S(1)}) custom-call(s32[6400]{0:T(1024)} %refs_0_.1, s32[1984]{0:T(1024)} %refs_3_.2), custom_call_target="tpu_custom_call" | custom-call | bytes 1048576 | tf_op jit(solution)/shard_map/far_asks/pallas_call | solution.py:119
  7.5 4.1 %all-to-all-start = ((s32[32,1,16]{2,1,0:T(1,128)}), s32[32,1,16]{2,1,0:T(1,128)S(1)}, u32[]{:S(2)}, u32[]{:S(2)}) async-start(s32[32,1,16]{2,1,0:T(1,128)} %bitcast.1), calls=%async_computation | async-start | bytes 32768 | tf_op jit(solution)/shard_map/all_to_all | solution.py:391
  11.6 3.6 %encode_weights.1 = (bf16[512,512]{1,0:T(8,128)(2,1)S(1)}, bf16[512,272]{1,0:T(8,128)(2,1)S(1)}, bf16[512,512]{1,0:T(8,128)(2,1)S(1)}, s32[1,6400]{1,0:T(1,128)S...) custom-call(bf16[512,512]{1,0:T(8,128)(2,1)} %refs_0_.2, s32[1,35]{1,0:T(1,128)} %refs_1_.4, ...), custom_call_target="tpu_custom_call" | custom-call | flops 3000000000 | bytes 1048576 | tf_op jit(solution)/shard_map/encode_weights/pallas_call | solution.py:119
  15.2 3.4 %encode_begin.1 = (bf16[256,512]{1,0:T(8,128)(2,1)S(1)}, bf16[512,1024]{1,0:T(8,128)(2,1)S(1)}) custom-call(bf16[1024,512]{1,0:T(8,128)(2,1)S(1)} %get-tuple-element.110.refs_0_, bf16[512,512]{1,0:T(8,128)(2,1)S(1)} %get-tuple-element.111.refs_1_, bf16[512,272]{1,0:T(8,128)(2,1)S(1)} %get-tuple-element.107.refs_2_.refs_0_, ...), custom_call_target="tpu_custom_call" | custom-call | flops 3000000000 | bytes 1048576 | tf_op jit(solution)/shard_map/encode_begin/pallas_call | solution.py:119
  18.6 1.5 %all-to-all-done = s32[32,1,16]{2,1,0:T(1,128)S(1)} async-done(((s32[32,1,16]{2,1,0:T(1,128)}), s32[32,1,16]{2,1,0:T(1,128)S(1)}, u32[]{:S(2)}, u32[]{:S(2)}) %all-to-all-start) | async-done | bytes 2080 | tf_op jit(solution)/shard_map/all_to_all | solution.py:391
  21.5 6.2 %all-to-all-start.1 = ((bf16[32,8,512]{2,1,0:T(8,128)(2,1)}), bf16[32,8,512]{2,1,0:T(8,128)(2,1)S(1)}, u32[]{:S(2)}, u32[]{:S(2)}) async-start(bf16[32,8,512]{2,1,0:T(8,128)(2,1)} %bitcast.3), calls=%async_computation.1 | async-start | bytes 524288 | tf_op jit(solution)/shard_map/all_to_all | solution.py:391
  27.8 14.5 %encode_near.1.refs_5_ = f32[256,512]{1,0:T(8,128)S(1)} custom-call(bf16[512,1024]{1,0:T(8,128)(2,1)S(1)} %get-tuple-element.117.refs_1_.refs_0_, bf16[512,512]{1,0:T(8,128)(2,1)S(1)} %get-tuple-element.111.refs_1_, bf16[512,272]{1,0:T(8,128)(2,1)S(1)} %get-tuple-element.107.refs_2_.refs_0_, s32[6400]{0:T(1024)S(1)} %get-tuple-element.112.refs_3_, ...), custom_call_target="tpu_custom_call" | custom-call | flops 15000000512 | bytes 1048576 | tf_op jit(solution)/shard_map/encode_near/pallas_call | solution.py:119
  43.7 2.3 %collective-permute-start.2 = (bf16[256,512]{1,0:T(8,128)(2,1)S(1)}, bf16[256,512]{1,0:T(8,128)(2,1)S(1)}, u32[]{:S(2)}, u32[]{:S(2)}) collective-permute-start(bf16[256,512]{1,0:T(8,128)(2,1)S(1)} %encode_far.1.refs_0_), channel_id=1, source_target_pairs={{0,32},{1,97},{2,34},{3,99},{4,36},{5,101},{6,38},{7,103},{8,40},{... | collective-permute-start | bytes 786440 | tf_op jit(solution)/shard_map/ppermute | solution.py:371
  46.0 4.3 %process_terms.1 = (bf16[512,1920]{1,0:T(8,128)(2,1)}, bf16[512,256]{1,0:T(8,128)(2,1)S(1)}, bf16[512,512]{1,0:T(8,128)(2,1)S(1)}, s32[1984]{0:T(1024)S(1)}, s32...) custom-call(bf16[512,512]{1,0:T(8,128)(2,1)} %refs_0_.3, ...), custom_call_target="tpu_custom_call" | custom-call | flops 2000000000 | bytes 1048576 | tf_op jit(solution)/shard_map/process_terms/pallas_call | solution.py:119
  50.4 4.2 %collective-permute-start.3 = (bf16[256,512]{1,0:T(8,128)(2,1)S(1)}, bf16[256,512]{1,0:T(8,128)(2,1)S(1)}, u32[]{:S(2)}, u32[]{:S(2)}) collective-permute-start(bf16[256,512]{1,0:T(8,128)(2,1)S(1)} %band_add.2.refs_2_), channel_id=1, source_target_pairs={{0,96},{1,33},{2,98},{3,35},{4,100},{5,37},{6,102},{7,39},{8,104},... | collective-permute-start | bytes 786440 | tf_op jit(solution)/shard_map/ppermute | solution.py:371
  54.6 1.5 %process_prepare.1 = (bf16[512,512]{1,0:T(8,128)(2,1)S(1)}, bf16[512,512]{1,0:T(8,128)(2,1)S(1)}, bf16[512,512]{1,0:T(8,128)(2,1)S(1)}, s32[8,1920]{1,0:T(8,128)S(1)}, s32[1,256]{1,0:T(1,128)S(1)}) custom-call(bf16[512,512]{1,0:T(8,128)(2,1)S(1)} %get-tuple-element.146.refs_0_, s32[1,35]{1,0:T(1,128)} %refs_1_.6, s32[1984]{0:T(1024)S(1)} %get-tuple-element.147.refs_2_, ...), custom_call_target="tpu_custom_call" | custom-call | flops 2000000000 | bytes 1048576 | tf_op jit(solution)/shard_map/process_prepare/pallas_call | solution.py:119
  56.1 2.8 %collective-permute-done.3.refs_3_ = bf16[256,512]{1,0:T(8,128)(2,1)S(1)} collective-permute-done((bf16[256,512]{1,0:T(8,128)(2,1)S(1)}, bf16[256,512]{1,0:T(8,128)(2,1)S(1)}, u32[]{:S(2)}, u32[]{:S(2)}) %collective-permute-start.3) | collective-permute-done | bytes 262176 | tf_op jit(solution)/shard_map/ppermute | solution.py:371
  59.0 1.9 %mesh_nodes.1 = (bf16[256,512]{1,0:T(8,128)(2,1)S(1)}, bf16[256,512]{1,0:T(8,128)(2,1)}, bf16[512,256]{1,0:T(8,128)(2,1)S(1)}, bf16[512,256]{1,0:T(8,128)(2,1)S(1)}) custom-call(s32[32,16]{1,0:T(8,128)S(1)} %bitcast.16, bf16[256,512]{1,0:T(8,128)(2,1)S(1)} %get-tuple-element.152.refs_1_, bf16[256,512]{1,0:T(8,128)(2,1)S(1)} %band_add.2.refs_2_, ...), custom_call_target="tpu_custom_call" | custom-call | flops 1000000000 | bytes 1048576 | tf_op jit(solution)/shard_map/mesh_nodes/pallas_call | solution.py:119
  60.9 5.1 %collective-permute-start.5 = (bf16[512,256]{1,0:T(8,128)(2,1)S(1)}, bf16[512,256]{1,0:T(8,128)(2,1)S(1)}, u32[]{:S(2)}, u32[]{:S(2)}) collective-permute-start(bf16[512,256]{1,0:T(8,128)(2,1)S(1)} %get-tuple-element.165.refs_2_), channel_id=1, source_target_pairs={{1,0},{2,1},{3,2},{4,3},{5,4},{6,5},{7,6},{8,7},{9,8},{10,9},{11,1... | collective-permute-start | bytes 786440 | tf_op jit(solution)/shard_map/ppermute | solution.py:387
  65.9 3.9 %all-to-all-start.2 = ((bf16[32,8,512]{2,1,0:T(8,128)(2,1)}), bf16[32,8,512]{2,1,0:T(8,128)(2,1)S(1)}, u32[]{:S(2)}, u32[]{:S(2)}) async-start(bf16[32,8,512]{2,1,0:T(8,128)(2,1)} %bitcast.7), calls=%async_computation.2 | async-start | bytes 524288 | tf_op jit(solution)/shard_map/all_to_all | solution.py:391
  70.0 5.8 %process_near.1 = (f32[256,512]{1,0:T(8,128)S(1)}, bf16[512,1920]{1,0:T(8,128)(2,1)}) custom-call(bf16[512,1920]{1,0:T(8,128)(2,1)} %get-tuple-element.164.refs_0_, bf16[512,256]{1,0:T(8,128)(2,1)S(1)} %collective-permute-done.4.refs_1_, bf16[512,256]{1,0:T(8,128)(2,1)S(1)} %get-tuple-element.165.refs_2_, ...), custom_call_target="tpu_custom_call" | custom-call | flops 4000000000 | bytes 1048576 | tf_op jit(solution)/shard_map/process_near/pallas_call | solution.py:119
  75.8 2.9 %all-to-all-done.2 = bf16[32,8,512]{2,1,0:T(8,128)(2,1)S(1)} async-done(((bf16[32,8,512]{2,1,0:T(8,128)(2,1)}), bf16[32,8,512]{2,1,0:T(8,128)(2,1)S(1)}, u32[]{:S(2)}, u32[]{:S(2)}) %all-to-all-start.2) | async-done | bytes 262176 | tf_op jit(solution)/shard_map/all_to_all | solution.py:391
  80.1 3.9 %process_rows.1 = (bf16[1984,512]{1,0:T(8,128)(2,1)}, f32[1,512]{1,0:T(1,128)S(1)}, bf16[1024,512]{1,0:T(8,128)(2,1)S(1)}, bf16[512,512]{1,0:T(8,128)(2,1)S(1)},...) custom-call(bf16[512,256]{1,0:T(8,128)(2,1)S(1)} %get-tuple-element., ...), custom_call_target="tpu_custom_call" | custom-call | flops 3000000000 | bytes 1048576 | tf_op jit(solution)/shard_map/process_rows/pallas_call | solution.py:119
  84.0 2.4 %collective-permute-done.6.refs_1_ = bf16[256,512]{1,0:T(8,128)(2,1)S(1)} collective-permute-done((bf16[256,512]{1,0:T(8,128)(2,1)S(1)}, bf16[256,512]{1,0:T(8,128)(2,1)S(1)}, u32[]{:S(2)}, u32[]{:S(2)}) %collective-permute-start.6) | collective-permute-done | bytes 262176 | tf_op jit(solution)/shard_map/ppermute | solution.py:371
  86.5 3.3 %collective-permute-start.7 = (bf16[256,512]{1,0:T(8,128)(2,1)S(1)}, bf16[256,512]{1,0:T(8,128)(2,1)S(1)}, u32[]{:S(2)}, u32[]{:S(2)}) collective-permute-start(bf16[256,512]{1,0:T(8,128)(2,1)S(1)} %band_add.3.refs_1_), channel_id=1, source_target_pairs={{0,96},{1,33},{2,98},{3,35},{4,100},{5,37},{6,102},{7,39},{8,104},... | collective-permute-start | bytes 786440 | tf_op jit(solution)/shard_map/ppermute | solution.py:371
  89.8 2.6 %grid_nodes.1 = bf16[1024,512]{1,0:T(8,128)(2,1)} custom-call(bf16[1024,512]{1,0:T(8,128)(2,1)S(1)} %get-tuple-element.194.refs_0_, bf16[512,512]{1,0:T(8,128)(2,1)S(1)} %get-tuple-element.195.refs_1_, bf16[512,512]{1,0:T(8,128)(2,1)S(1)} %get-tuple-element.196.refs_2_, f32[1,512]{1,0:T(1,128)S(1)} %get-tuple-element.197.refs_3_), custom_call_target="tpu_custom_call" | custom-call | flops 3000000000 | bytes 1048576 | tf_op jit(solution)/shard_map/grid_nodes/pallas_call | solution.py:119
  92.5 1.7 %collective-permute-done.7.refs_2_ = bf16[256,512]{1,0:T(8,128)(2,1)S(1)} collective-permute-done((bf16[256,512]{1,0:T(8,128)(2,1)S(1)}, bf16[256,512]{1,0:T(8,128)(2,1)S(1)}, u32[]{:S(2)}, u32[]{:S(2)}) %collective-permute-start.7) | collective-permute-done | bytes 262176 | tf_op jit(solution)/shard_map/ppermute | solution.py:371
  94.2 1.6 %mesh_update.1 = bf16[256,512]{1,0:T(8,128)(2,1)} custom-call(bf16[256,512]{1,0:T(8,128)(2,1)S(1)} %get-tuple-element.200.refs_0_, bf16[256,512]{1,0:T(8,128)(2,1)S(1)} %band_add.3.refs_1_, bf16[256,512]{1,0:T(8,128)(2,1)S(1)} %collective-permute-done.7.refs_2_, f32[1,512]{1,0:T(1,128)S(1)} %get-tuple-element.202.refs_3_, ...), custom_call_target="tpu_custom_call" | custom-call | flops 1000000000 | bytes 1048576 | tf_op jit(solution)/shard_map/mesh_update/pallas_call | solution.py:119
  (16 shorter events, 4.5 us)
Async XLA Ops:
  0.6 27.1 %collective-permute-start = (bf16[1024,512]{1,0:T(8,128)(2,1)}, bf16[1024,512]{1,0:T(8,128)(2,1)}, u32[]{:S(2)}, u32[]{:S(2)}) collective-permute-start(bf16[1024,512]{1,0:T(8,128)(2,1)} %refs_4_.3), channel_id=1, source_target_pairs={{0,1},{1,2},{2,3},{3,4},{4,5},{5,6},{6,7},{7,8},{8,9},{9,10},{10,1... | collective-permute-start | bytes 3145736 | tf_op jit(solution)/shard_map/ppermute | solution.py:387
  0.7 27.1 %collective-permute-start.1 = (bf16[1024,512]{1,0:T(8,128)(2,1)}, bf16[1024,512]{1,0:T(8,128)(2,1)}, u32[]{:S(2)}, u32[]{:S(2)}) collective-permute-start(bf16[1024,512]{1,0:T(8,128)(2,1)} %refs_4_.3), channel_id=1, source_target_pairs={{1,0},{2,1},{3,2},{4,3},{5,4},{6,5},{7,6},{8,7},{9,8},{10,9},{11,1... | collective-permute-start | bytes 3145736 | tf_op jit(solution)/shard_map/ppermute | solution.py:387
  7.5 12.6 %all-to-all-start = ((s32[32,1,16]{2,1,0:T(1,128)}), s32[32,1,16]{2,1,0:T(1,128)S(1)}, u32[]{:S(2)}, u32[]{:S(2)}) async-start(s32[32,1,16]{2,1,0:T(1,128)} %bitcast.1), calls=%async_computation | async-start | bytes 32768 | tf_op jit(solution)/shard_map/all_to_all | solution.py:391
  18.6 2.9 %copy-start = (bf16[256,512]{1,0:T(8,128)(2,1)}, bf16[256,512]{1,0:T(8,128)(2,1)S(1)}, u32[]{:S(2)}) copy-start(bf16[256,512]{1,0:T(8,128)(2,1)S(1)} %get-tuple-element.118.refs_6_) | copy-start | bytes 786436
  21.5 20.8 %all-to-all-start.1 = ((bf16[32,8,512]{2,1,0:T(8,128)(2,1)}), bf16[32,8,512]{2,1,0:T(8,128)(2,1)S(1)}, u32[]{:S(2)}, u32[]{:S(2)}) async-start(bf16[32,8,512]{2,1,0:T(8,128)(2,1)} %bitcast.3), calls=%async_computation.1 | async-start | bytes 524288 | tf_op jit(solution)/shard_map/all_to_all | solution.py:391
  43.7 6.7 %collective-permute-start.2 = (bf16[256,512]{1,0:T(8,128)(2,1)S(1)}, bf16[256,512]{1,0:T(8,128)(2,1)S(1)}, u32[]{:S(2)}, u32[]{:S(2)}) collective-permute-start(bf16[256,512]{1,0:T(8,128)(2,1)S(1)} %encode_far.1.refs_0_), channel_id=1, source_target_pairs={{0,32},{1,97},{2,34},{3,99},{4,36},{5,101},{6,38},{7,103},{8,40},{... | collective-permute-start | bytes 786440 | tf_op jit(solution)/shard_map/ppermute | solution.py:371
  50.4 8.5 %collective-permute-start.3 = (bf16[256,512]{1,0:T(8,128)(2,1)S(1)}, bf16[256,512]{1,0:T(8,128)(2,1)S(1)}, u32[]{:S(2)}, u32[]{:S(2)}) collective-permute-start(bf16[256,512]{1,0:T(8,128)(2,1)S(1)} %band_add.2.refs_2_), channel_id=1, source_target_pairs={{0,96},{1,33},{2,98},{3,35},{4,100},{5,37},{6,102},{7,39},{8,104},... | collective-permute-start | bytes 786440 | tf_op jit(solution)/shard_map/ppermute | solution.py:371
  60.9 9.1 %collective-permute-start.4 = (bf16[512,256]{1,0:T(8,128)(2,1)S(1)}, bf16[512,256]{1,0:T(8,128)(2,1)S(1)}, u32[]{:S(2)}, u32[]{:S(2)}) collective-permute-start(bf16[512,256]{1,0:T(8,128)(2,1)S(1)} %get-tuple-element.165.refs_2_), channel_id=1, source_target_pairs={{0,1},{1,2},{2,3},{3,4},{4,5},{5,6},{6,7},{7,8},{8,9},{9,10},{10,1... | collective-permute-start | bytes 786440 | tf_op jit(solution)/shard_map/ppermute | solution.py:387
  60.9 9.1 %collective-permute-start.5 = (bf16[512,256]{1,0:T(8,128)(2,1)S(1)}, bf16[512,256]{1,0:T(8,128)(2,1)S(1)}, u32[]{:S(2)}, u32[]{:S(2)}) collective-permute-start(bf16[512,256]{1,0:T(8,128)(2,1)S(1)} %get-tuple-element.165.refs_2_), channel_id=1, source_target_pairs={{1,0},{2,1},{3,2},{4,3},{5,4},{6,5},{7,6},{8,7},{9,8},{10,9},{11,1... | collective-permute-start | bytes 786440 | tf_op jit(solution)/shard_map/ppermute | solution.py:387
  65.9 12.8 %all-to-all-start.2 = ((bf16[32,8,512]{2,1,0:T(8,128)(2,1)}), bf16[32,8,512]{2,1,0:T(8,128)(2,1)S(1)}, u32[]{:S(2)}, u32[]{:S(2)}) async-start(bf16[32,8,512]{2,1,0:T(8,128)(2,1)} %bitcast.7), calls=%async_computation.2 | async-start | bytes 524288 | tf_op jit(solution)/shard_map/all_to_all | solution.py:391
  80.0 6.5 %collective-permute-start.6 = (bf16[256,512]{1,0:T(8,128)(2,1)S(1)}, bf16[256,512]{1,0:T(8,128)(2,1)S(1)}, u32[]{:S(2)}, u32[]{:S(2)}) collective-permute-start(bf16[256,512]{1,0:T(8,128)(2,1)S(1)} %get-tuple-element.171.refs_0_), channel_id=1, source_target_pairs={{0,32},{1,97},{2,34},{3,99},{4,36},{5,101},{6,38},{7,103},{8,40},{... | collective-permute-start | bytes 786440 | tf_op jit(solution)/shard_map/ppermute | solution.py:371
  86.5 7.7 %collective-permute-start.7 = (bf16[256,512]{1,0:T(8,128)(2,1)S(1)}, bf16[256,512]{1,0:T(8,128)(2,1)S(1)}, u32[]{:S(2)}, u32[]{:S(2)}) collective-permute-start(bf16[256,512]{1,0:T(8,128)(2,1)S(1)} %band_add.3.refs_1_), channel_id=1, source_target_pairs={{0,96},{1,33},{2,98},{3,35},{4,100},{5,37},{6,102},{7,39},{8,104},... | collective-permute-start | bytes 786440 | tf_op jit(solution)/shard_map/ppermute | solution.py:371

commit v7 on v6

--- a/solution.py
+++ b/solution.py
@@ -237,8 +237,8 @@
     return (half * jnp.tanh(half) + half).astype(BF)
 
 
-def mlp(latent, summed, w_first, w_second, gain):
-    merged = nn(latent, w_first[:D, :]) + nn(summed, w_first[D:, :])
+def mlp(latent, base, summed, w_first, w_second, gain):
+    merged = base[...] + nn(summed, w_first[D:, :])
     update = norm(nn(silu(merged), w_second[...])) * gain[...]
     return (latent.astype(F32) + update).astype(BF)
 
@@ -255,20 +255,21 @@
     return (plus(a, b) * edge_gain[...]).astype(BF)
 
 
-def node_kernel(asked, mesh, p0, p1, edge_gain, w_first, w_second, gain, wst, wrt, mid, rows, sent, pt):
-    value = mlp(mesh[...], band_total(p0, p1, edge_gain), w_first, w_second, gain)
+def node_kernel(hot, base, mesh, p0, p1, edge_gain, w_first, w_second, gain, wst, wrt, mid, rows, sent, pt):
+    value = mlp(mesh[...], base, band_total(p0, p1, edge_gain), w_first, w_second, gain)
     table = nt(wst[...], value).astype(BF)
     sent[...] = table
-    rows[...] = nn(asked_hot(asked[...], FAR_G, NODES), value).astype(BF)
+    rows[...] = nn(hot[...], value).astype(BF)
     mid[...] = value
     pt[...] = nt(wrt[...], value).astype(BF)
 
 
-def update_kernel(mid, p0, p1, edge_gain, w_first, w_second, gain, out):
-    out[...] = mlp(mid[...], band_total(p0, p1, edge_gain), w_first, w_second, gain)
-
-
-def grid_kernel(latent, w_first, w_second, gain, out, held, sems):
+def update_kernel(mid, base, p0, p1, edge_gain, w_first, w_second, gain, out):
+    out[...] = mlp(mid[...], base, band_total(p0, p1, edge_gain), w_first, w_second, gain)
+
+
+def grid_kernel(latent, w_first, w_second, gain, mid, u_first, out, base, held, sems):
+    base[...] = nn(mid[...], u_first[:D, :])
     copies = []
     for i in range(2):
         part, where = slice(i * GRID // 2, (i + 1) * GRID // 2), pl.ds(i * GRID // 2, GRID // 2)
@@ -307,7 +308,11 @@
         copy.wait()
 
 
-def prepare_kernel(w_send, live, sender, receiver, w_recv, w_out, wst, wrt, wt, near, far):
+def prepare_kernel(
+    w_send, live, sender, receiver, w_recv, w_out, asked, mesh, n_first, wst, wrt, wt, near, far, hot, base
+):
+    hot[...] = asked_hot(asked[...], FAR_G, NODES)
+    base[...] = nn(mesh[...], n_first[:D, :])
     eye = identity(D)
     wst[...] = (0.5 * nt(eye, w_send[...])).astype(BF)
     wrt[...] = (0.5 * nt(eye, w_recv[...])).astype(BF)
@@ -491,8 +496,9 @@
     def prepare(args):
         return call(
             prepare_kernel,
-            (weight, weight, weight, kept((8, 3 * NM_PAD), jnp.int32), kept((1, FAR), jnp.int32)),
-            "VSVVVV",
+            (weight, weight, weight, kept((8, 3 * NM_PAD), jnp.int32), kept((1, FAR), jnp.int32))
+            + (kept((FAR, NODES), BF), kept((NODES, D), F32)),
+            "VSVVVVVVV",
             args,
             flops=2 * 10**9,
             name="process_prepare",
@@ -506,12 +512,14 @@
     )
     near_pre, far_pre, p_send, p_from, p_to, p_recv, p_out, n_first, n_second, n_mesh, n_eg, n_gain = terms
     part, p_send = lax.optimization_barrier((part, p_send))
-    p_wst, p_wrt, p_wt, near_index, far_index = prepare((p_send, mesh_live, p_from, p_to, p_recv, p_out))
+    p_wst, p_wrt, p_wt, near_index, far_index, n_hot, n_base = prepare(
+        (p_send, mesh_live, p_from, p_to, p_recv, p_out, asked, n_mesh, n_first)
+    )
     mid, rows, own_table, pt = call(
         node_kernel,
         (kept((NODES, D), BF), shape((FAR, D), BF), kept((D, NODES), BF), kept((D, NODES), BF)),
-        "VVVVVVVVVV",
-        (asked, n_mesh, part, part_in, n_eg, n_first, n_second, n_gain, p_wst, p_wrt),
+        "VVVVVVVVVVV",
+        (n_hot, n_base, n_mesh, part, part_in, n_eg, n_first, n_second, n_gain, p_wst, p_wrt),
         flops=10**9,
         name="mesh_nodes",
     )
@@ -556,13 +564,13 @@
     )
     edge_out, m_gain, g_rows, g_first, g_second, g_gain, u_first, u_second, u_gain = from_rows
     part, g_rows = lax.optimization_barrier((part, g_rows))
-    grid_out = call(
+    grid_out, u_base = call(
         grid_kernel,
-        [pltpu.HBM((GRID, D), BF)],
-        "VVVV",
-        (g_rows, g_first, g_second, g_gain),
+        [pltpu.HBM((GRID, D), BF), kept((NODES, D), F32)],
+        "VVVVVV",
+        (g_rows, g_first, g_second, g_gain, mid, u_first),
         scratch=[pltpu.VMEM((GRID, D), BF), pltpu.SemaphoreType.DMA((2,))],
-        out_specs=[HBM],
+        out_specs=[HBM, VMEM],
         flops=3 * 10**9,
         name="grid_nodes",
     )
@@ -570,8 +578,8 @@
     mesh_out = call(
         update_kernel,
         [shape((NODES, D), BF)],
-        "VVVVVVV",
-        (mid, part, part_in, m_gain, u_first, u_second, u_gain),
+        "VVVVVVVV",
+        (mid, u_base, part, part_in, m_gain, u_first, u_second, u_gain),
         flops=10**9,
         name="mesh_update",
     )

time: 96.3 us -> 95.8 us (level)
  no operation moved by 1% of the time
where the time goes in v7:
time: 95.8 us; the launch traced here: 95.4 us
  Pallas kernels  48.9 us (51%)
  starting transfers between devices  34.3 us (36%)
  waiting for transfers between devices  11.4 us (12%)
    pallas_call x16, Pallas kernels, call(): pl.pallas_call(body, out_shape=out_shape, in_specs=[place[spec] for spec...  48.9 us
    all_to_all x3, starting transfers between devices, exchange(): return lax.all_to_all(x, 'region', split_axis=0, concat_axis=0, tiled=True)  14.2 us
    ppermute x4, starting transfers between devices, halo(): return (lax.ppermute(x, 'region', up), lax.ppermute(x, 'region', down))  10.2 us
    ppermute x4, starting transfers between devices, swap(): return lax.ppermute(x, ('band', 'region'), pairs)  9.87 us
    ppermute x4, waiting for transfers between devices, swap(): return lax.ppermute(x, ('band', 'region'), pairs)  6.75 us
    all_to_all x3, waiting for transfers between devices, exchange(): return lax.all_to_all(x, 'region', split_axis=0, concat_axis=0, tiled=True)  4.46 us
  transfers between devices with their start and end apart: 11, of which 7 were waited for; matrix products, arithmetic and copies ran while one was open for 0% of the time, Pallas kernels for 45%

profile of v7, /device:TPU:0, one launch (start us, length us, event | category | flops | bytes accessed | tf_op | source)
XLA Modules:
  0.0 95.4 jit_solution(728575431210577107)
XLA Ops:
  0.7 5.0 %collective-permute-start.1 = (bf16[1024,512]{1,0:T(8,128)(2,1)}, bf16[1024,512]{1,0:T(8,128)(2,1)}, u32[]{:S(2)}, u32[]{:S(2)}) collective-permute-start(bf16[1024,512]{1,0:T(8,128)(2,1)} %refs_4_.3), channel_id=1, source_target_pairs={{1,0},{2,1},{3,2},{4,3},{5,4},{6,5},{7,6},{8,7},{9,8},{10,9},{11,1... | collective-permute-start | bytes 3145736 | tf_op jit(solution)/shard_map/ppermute | solution.py:392
  5.8 1.7 %far_asks.1 = (s32[32,16]{1,0:T(8,128)}, s32[6400]{0:T(1024)S(1)}) custom-call(s32[6400]{0:T(1024)} %refs_0_.1, s32[1984]{0:T(1024)} %refs_3_.2), custom_call_target="tpu_custom_call" | custom-call | bytes 1048576 | tf_op jit(solution)/shard_map/far_asks/pallas_call | solution.py:119
  7.5 4.1 %all-to-all-start = ((s32[32,1,16]{2,1,0:T(1,128)}), s32[32,1,16]{2,1,0:T(1,128)S(1)}, u32[]{:S(2)}, u32[]{:S(2)}) async-start(s32[32,1,16]{2,1,0:T(1,128)} %bitcast.1), calls=%async_computation | async-start | bytes 32768 | tf_op jit(solution)/shard_map/all_to_all | solution.py:396
  11.6 3.6 %encode_weights.1 = (bf16[512,512]{1,0:T(8,128)(2,1)S(1)}, bf16[512,272]{1,0:T(8,128)(2,1)S(1)}, bf16[512,512]{1,0:T(8,128)(2,1)S(1)}, s32[1,6400]{1,0:T(1,128)S...) custom-call(bf16[512,512]{1,0:T(8,128)(2,1)} %refs_0_.2, s32[1,35]{1,0:T(1,128)} %refs_1_.4, ...), custom_call_target="tpu_custom_call" | custom-call | flops 3000000000 | bytes 1048576 | tf_op jit(solution)/shard_map/encode_weights/pallas_call | solution.py:119
  15.2 3.4 %encode_begin.1 = (bf16[256,512]{1,0:T(8,128)(2,1)S(1)}, bf16[512,1024]{1,0:T(8,128)(2,1)S(1)}) custom-call(bf16[1024,512]{1,0:T(8,128)(2,1)S(1)} %get-tuple-element.114.refs_0_, bf16[512,512]{1,0:T(8,128)(2,1)S(1)} %get-tuple-element.115.refs_1_, bf16[512,272]{1,0:T(8,128)(2,1)S(1)} %get-tuple-element.111.refs_2_.refs_0_, ...), custom_call_target="tpu_custom_call" | custom-call | flops 3000000000 | bytes 1048576 | tf_op jit(solution)/shard_map/encode_begin/pallas_call | solution.py:119
  18.6 1.5 %all-to-all-done = s32[32,1,16]{2,1,0:T(1,128)S(1)} async-done(((s32[32,1,16]{2,1,0:T(1,128)}), s32[32,1,16]{2,1,0:T(1,128)S(1)}, u32[]{:S(2)}, u32[]{:S(2)}) %all-to-all-start) | async-done | bytes 2080 | tf_op jit(solution)/shard_map/all_to_all | solution.py:396
  21.5 6.2 %all-to-all-start.1 = ((bf16[32,8,512]{2,1,0:T(8,128)(2,1)}), bf16[32,8,512]{2,1,0:T(8,128)(2,1)S(1)}, u32[]{:S(2)}, u32[]{:S(2)}) async-start(bf16[32,8,512]{2,1,0:T(8,128)(2,1)} %bitcast.3), calls=%async_computation.1 | async-start | bytes 524288 | tf_op jit(solution)/shard_map/all_to_all | solution.py:396
  27.8 14.5 %encode_near.1.refs_5_ = f32[256,512]{1,0:T(8,128)S(1)} custom-call(bf16[512,1024]{1,0:T(8,128)(2,1)S(1)} %get-tuple-element.121.refs_1_.refs_0_, bf16[512,512]{1,0:T(8,128)(2,1)S(1)} %get-tuple-element.115.refs_1_, bf16[512,272]{1,0:T(8,128)(2,1)S(1)} %get-tuple-element.111.refs_2_.refs_0_, s32[6400]{0:T(1024)S(1)} %get-tuple-element.116.refs_3_, ...), custom_call_target="tpu_custom_call" | custom-call | flops 15000000512 | bytes 1048576 | tf_op jit(solution)/shard_map/encode_near/pallas_call | solution.py:119
  43.7 2.3 %collective-permute-start.2 = (bf16[256,512]{1,0:T(8,128)(2,1)S(1)}, bf16[256,512]{1,0:T(8,128)(2,1)S(1)}, u32[]{:S(2)}, u32[]{:S(2)}) collective-permute-start(bf16[256,512]{1,0:T(8,128)(2,1)S(1)} %encode_far.1.refs_0_), channel_id=1, source_target_pairs={{0,32},{1,97},{2,34},{3,99},{4,36},{5,101},{6,38},{7,103},{8,40},{... | collective-permute-start | bytes 786440 | tf_op jit(solution)/shard_map/ppermute | solution.py:376
  46.0 4.3 %process_terms.1 = (bf16[512,1920]{1,0:T(8,128)(2,1)}, bf16[512,256]{1,0:T(8,128)(2,1)S(1)}, bf16[512,512]{1,0:T(8,128)(2,1)S(1)}, s32[1984]{0:T(1024)S(1)}, s32...) custom-call(bf16[512,512]{1,0:T(8,128)(2,1)} %refs_0_.3, ...), custom_call_target="tpu_custom_call" | custom-call | flops 2000000000 | bytes 1048576 | tf_op jit(solution)/shard_map/process_terms/pallas_call | solution.py:119
  50.4 4.2 %collective-permute-start.3 = (bf16[256,512]{1,0:T(8,128)(2,1)S(1)}, bf16[256,512]{1,0:T(8,128)(2,1)S(1)}, u32[]{:S(2)}, u32[]{:S(2)}) collective-permute-start(bf16[256,512]{1,0:T(8,128)(2,1)S(1)} %band_add.2.refs_3_), channel_id=1, source_target_pairs={{0,96},{1,33},{2,98},{3,35},{4,100},{5,37},{6,102},{7,39},{8,104},... | collective-permute-start | bytes 786440 | tf_op jit(solution)/shard_map/ppermute | solution.py:376
  54.6 1.6 %process_prepare.1 = (bf16[512,512]{1,0:T(8,128)(2,1)S(1)}, bf16[512,512]{1,0:T(8,128)(2,1)S(1)}, bf16[512,512]{1,0:T(8,128)(2,1)S(1)}, s32[8,1920]{1,0:T(8,128)...) custom-call(bf16[512,512]{1,0:T(8,128)(2,1)S(1)} %get-tuple-element.150.refs_0_, ...), custom_call_target="tpu_custom_call" | custom-call | flops 2000000000 | bytes 1048576 | tf_op jit(solution)/shard_map/process_prepare/pallas_call | solution.py:119
  56.2 2.7 %collective-permute-done.3.refs_4_ = bf16[256,512]{1,0:T(8,128)(2,1)S(1)} collective-permute-done((bf16[256,512]{1,0:T(8,128)(2,1)S(1)}, bf16[256,512]{1,0:T(8,128)(2,1)S(1)}, u32[]{:S(2)}, u32[]{:S(2)}) %collective-permute-start.3) | collective-permute-done | bytes 262176 | tf_op jit(solution)/shard_map/ppermute | solution.py:376
  59.0 1.7 %mesh_nodes.1 = (bf16[256,512]{1,0:T(8,128)(2,1)S(1)}, bf16[256,512]{1,0:T(8,128)(2,1)}, bf16[512,256]{1,0:T(8,128)(2,1)S(1)}, bf16[512,256]{1,0:T(8,128)(2,1)S(1)}) custom-call(bf16[256,256]{1,0:T(8,128)(2,1)S(1)} %get-tuple-element.158.refs_0_, f32[256,512]{1,0:T(8,128)S(1)} %get-tuple-element.159.refs_1_, ...), custom_call_target="tpu_custom_call" | custom-call | flops 1000000000 | bytes 1048576 | tf_op jit(solution)/shard_map/mesh_nodes/pallas_call | solution.py:119
  60.6 5.1 %collective-permute-start.5 = (bf16[512,256]{1,0:T(8,128)(2,1)S(1)}, bf16[512,256]{1,0:T(8,128)(2,1)S(1)}, u32[]{:S(2)}, u32[]{:S(2)}) collective-permute-start(bf16[512,256]{1,0:T(8,128)(2,1)S(1)} %get-tuple-element.171.refs_2_), channel_id=1, source_target_pairs={{1,0},{2,1},{3,2},{4,3},{5,4},{6,5},{7,6},{8,7},{9,8},{10,9},{11,1... | collective-permute-start | bytes 786440 | tf_op jit(solution)/shard_map/ppermute | solution.py:392
  65.7 3.9 %all-to-all-start.2 = ((bf16[32,8,512]{2,1,0:T(8,128)(2,1)}), bf16[32,8,512]{2,1,0:T(8,128)(2,1)S(1)}, u32[]{:S(2)}, u32[]{:S(2)}) async-start(bf16[32,8,512]{2,1,0:T(8,128)(2,1)} %bitcast.7), calls=%async_computation.2 | async-start | bytes 524288 | tf_op jit(solution)/shard_map/all_to_all | solution.py:396
  69.7 5.8 %process_near.1 = (f32[256,512]{1,0:T(8,128)S(1)}, bf16[512,1920]{1,0:T(8,128)(2,1)}) custom-call(bf16[512,1920]{1,0:T(8,128)(2,1)} %get-tuple-element.170.refs_0_, bf16[512,256]{1,0:T(8,128)(2,1)S(1)} %collective-permute-done.4.refs_1_, bf16[512,256]{1,0:T(8,128)(2,1)S(1)} %get-tuple-element.171.refs_2_, ...), custom_call_target="tpu_custom_call" | custom-call | flops 4000000000 | bytes 1048576 | tf_op jit(solution)/shard_map/process_near/pallas_call | solution.py:119
  75.6 2.9 %all-to-all-done.2 = bf16[32,8,512]{2,1,0:T(8,128)(2,1)S(1)} async-done(((bf16[32,8,512]{2,1,0:T(8,128)(2,1)}), bf16[32,8,512]{2,1,0:T(8,128)(2,1)S(1)}, u32[]{:S(2)}, u32[]{:S(2)}) %all-to-all-start.2) | async-done | bytes 262176 | tf_op jit(solution)/shard_map/all_to_all | solution.py:396
  79.9 3.9 %process_rows.1 = (bf16[1984,512]{1,0:T(8,128)(2,1)}, f32[1,512]{1,0:T(1,128)S(1)}, bf16[1024,512]{1,0:T(8,128)(2,1)S(1)}, bf16[512,512]{1,0:T(8,128)(2,1)S(1)},...) custom-call(bf16[512,256]{1,0:T(8,128)(2,1)S(1)} %get-tuple-element., ...), custom_call_target="tpu_custom_call" | custom-call | flops 3000000000 | bytes 1048576 | tf_op jit(solution)/shard_map/process_rows/pallas_call | solution.py:119
  83.8 2.4 %collective-permute-done.6.refs_1_ = bf16[256,512]{1,0:T(8,128)(2,1)S(1)} collective-permute-done((bf16[256,512]{1,0:T(8,128)(2,1)S(1)}, bf16[256,512]{1,0:T(8,128)(2,1)S(1)}, u32[]{:S(2)}, u32[]{:S(2)}) %collective-permute-start.6) | collective-permute-done | bytes 262176 | tf_op jit(solution)/shard_map/ppermute | solution.py:376
  86.3 3.3 %collective-permute-start.7 = (bf16[256,512]{1,0:T(8,128)(2,1)S(1)}, bf16[256,512]{1,0:T(8,128)(2,1)S(1)}, u32[]{:S(2)}, u32[]{:S(2)}) collective-permute-start(bf16[256,512]{1,0:T(8,128)(2,1)S(1)} %band_add.3.refs_2_), channel_id=1, source_target_pairs={{0,96},{1,33},{2,98},{3,35},{4,100},{5,37},{6,102},{7,39},{8,104},... | collective-permute-start | bytes 786440 | tf_op jit(solution)/shard_map/ppermute | solution.py:376
  89.6 2.8 %grid_nodes.1 = (bf16[1024,512]{1,0:T(8,128)(2,1)}, f32[256,512]{1,0:T(8,128)S(1)}) custom-call(bf16[1024,512]{1,0:T(8,128)(2,1)S(1)} %get-tuple-element.200.refs_0_, bf16[512,512]{1,0:T(8,128)(2,1)S(1)} %get-tuple-element.201.refs_1_, bf16[512,512]{1,0:T(8,128)(2,1)S(1)} %get-tuple-element.202.refs_2_, f32[1,512]{1,0:T(1,128)S(1)} %get-tuple-element.203.refs_3_, ...), custom_call_target="tpu_custom_call" | custom-call | flops 3000000000 | bytes 1048576 | tf_op jit(solution)/shard_map/grid_nodes/pallas_call | solution.py:119
  92.4 1.6 %collective-permute-done.7.refs_3_ = bf16[256,512]{1,0:T(8,128)(2,1)S(1)} collective-permute-done((bf16[256,512]{1,0:T(8,128)(2,1)S(1)}, bf16[256,512]{1,0:T(8,128)(2,1)S(1)}, u32[]{:S(2)}, u32[]{:S(2)}) %collective-permute-start.7) | collective-permute-done | bytes 262176 | tf_op jit(solution)/shard_map/ppermute | solution.py:376
  93.9 1.5 %mesh_update.1 = bf16[256,512]{1,0:T(8,128)(2,1)} custom-call(bf16[256,512]{1,0:T(8,128)(2,1)S(1)} %get-tuple-element.204.refs_4_.refs_0_, f32[256,512]{1,0:T(8,128)S(1)} %get-tuple-element.209.refs_1_, bf16[256,512]{1,0:T(8,128)(2,1)S(1)} %band_add.3.refs_2_, bf16[256,512]{1,0:T(8,128)(2,1)S(1)} %collective-permute-done.7.refs_3_, ...), custom_call_target="tpu_custom_call" | custom-call | flops 1000000000 | bytes 1048576 | tf_op jit(solution)/shard_map/mesh_update/pallas_call | solution.py:119
  (16 shorter events, 4.5 us)
Async XLA Ops:
  0.6 27.1 %collective-permute-start = (bf16[1024,512]{1,0:T(8,128)(2,1)}, bf16[1024,512]{1,0:T(8,128)(2,1)}, u32[]{:S(2)}, u32[]{:S(2)}) collective-permute-start(bf16[1024,512]{1,0:T(8,128)(2,1)} %refs_4_.3), channel_id=1, source_target_pairs={{0,1},{1,2},{2,3},{3,4},{4,5},{5,6},{6,7},{7,8},{8,9},{9,10},{10,1... | collective-permute-start | bytes 3145736 | tf_op jit(solution)/shard_map/ppermute | solution.py:392
  0.7 27.1 %collective-permute-start.1 = (bf16[1024,512]{1,0:T(8,128)(2,1)}, bf16[1024,512]{1,0:T(8,128)(2,1)}, u32[]{:S(2)}, u32[]{:S(2)}) collective-permute-start(bf16[1024,512]{1,0:T(8,128)(2,1)} %refs_4_.3), channel_id=1, source_target_pairs={{1,0},{2,1},{3,2},{4,3},{5,4},{6,5},{7,6},{8,7},{9,8},{10,9},{11,1... | collective-permute-start | bytes 3145736 | tf_op jit(solution)/shard_map/ppermute | solution.py:392
  7.5 12.6 %all-to-all-start = ((s32[32,1,16]{2,1,0:T(1,128)}), s32[32,1,16]{2,1,0:T(1,128)S(1)}, u32[]{:S(2)}, u32[]{:S(2)}) async-start(s32[32,1,16]{2,1,0:T(1,128)} %bitcast.1), calls=%async_computation | async-start | bytes 32768 | tf_op jit(solution)/shard_map/all_to_all | solution.py:396
  18.6 2.9 %copy-start = (bf16[256,512]{1,0:T(8,128)(2,1)}, bf16[256,512]{1,0:T(8,128)(2,1)S(1)}, u32[]{:S(2)}) copy-start(bf16[256,512]{1,0:T(8,128)(2,1)S(1)} %get-tuple-element.122.refs_6_) | copy-start | bytes 786436
  21.5 20.8 %all-to-all-start.1 = ((bf16[32,8,512]{2,1,0:T(8,128)(2,1)}), bf16[32,8,512]{2,1,0:T(8,128)(2,1)S(1)}, u32[]{:S(2)}, u32[]{:S(2)}) async-start(bf16[32,8,512]{2,1,0:T(8,128)(2,1)} %bitcast.3), calls=%async_computation.1 | async-start | bytes 524288 | tf_op jit(solution)/shard_map/all_to_all | solution.py:396
  43.7 6.7 %collective-permute-start.2 = (bf16[256,512]{1,0:T(8,128)(2,1)S(1)}, bf16[256,512]{1,0:T(8,128)(2,1)S(1)}, u32[]{:S(2)}, u32[]{:S(2)}) collective-permute-start(bf16[256,512]{1,0:T(8,128)(2,1)S(1)} %encode_far.1.refs_0_), channel_id=1, source_target_pairs={{0,32},{1,97},{2,34},{3,99},{4,36},{5,101},{6,38},{7,103},{8,40},{... | collective-permute-start | bytes 786440 | tf_op jit(solution)/shard_map/ppermute | solution.py:376
  50.4 8.5 %collective-permute-start.3 = (bf16[256,512]{1,0:T(8,128)(2,1)S(1)}, bf16[256,512]{1,0:T(8,128)(2,1)S(1)}, u32[]{:S(2)}, u32[]{:S(2)}) collective-permute-start(bf16[256,512]{1,0:T(8,128)(2,1)S(1)} %band_add.2.refs_3_), channel_id=1, source_target_pairs={{0,96},{1,33},{2,98},{3,35},{4,100},{5,37},{6,102},{7,39},{8,104},... | collective-permute-start | bytes 786440 | tf_op jit(solution)/shard_map/ppermute | solution.py:376
  60.6 9.1 %collective-permute-start.4 = (bf16[512,256]{1,0:T(8,128)(2,1)S(1)}, bf16[512,256]{1,0:T(8,128)(2,1)S(1)}, u32[]{:S(2)}, u32[]{:S(2)}) collective-permute-start(bf16[512,256]{1,0:T(8,128)(2,1)S(1)} %get-tuple-element.171.refs_2_), channel_id=1, source_target_pairs={{0,1},{1,2},{2,3},{3,4},{4,5},{5,6},{6,7},{7,8},{8,9},{9,10},{10,1... | collective-permute-start | bytes 786440 | tf_op jit(solution)/shard_map/ppermute | solution.py:392
  60.6 9.1 %collective-permute-start.5 = (bf16[512,256]{1,0:T(8,128)(2,1)S(1)}, bf16[512,256]{1,0:T(8,128)(2,1)S(1)}, u32[]{:S(2)}, u32[]{:S(2)}) collective-permute-start(bf16[512,256]{1,0:T(8,128)(2,1)S(1)} %get-tuple-element.171.refs_2_), channel_id=1, source_target_pairs={{1,0},{2,1},{3,2},{4,3},{5,4},{6,5},{7,6},{8,7},{9,8},{10,9},{11,1... | collective-permute-start | bytes 786440 | tf_op jit(solution)/shard_map/ppermute | solution.py:392
  65.7 12.8 %all-to-all-start.2 = ((bf16[32,8,512]{2,1,0:T(8,128)(2,1)}), bf16[32,8,512]{2,1,0:T(8,128)(2,1)S(1)}, u32[]{:S(2)}, u32[]{:S(2)}) async-start(bf16[32,8,512]{2,1,0:T(8,128)(2,1)} %bitcast.7), calls=%async_computation.2 | async-start | bytes 524288 | tf_op jit(solution)/shard_map/all_to_all | solution.py:396
  79.8 6.5 %collective-permute-start.6 = (bf16[256,512]{1,0:T(8,128)(2,1)S(1)}, bf16[256,512]{1,0:T(8,128)(2,1)S(1)}, u32[]{:S(2)}, u32[]{:S(2)}) collective-permute-start(bf16[256,512]{1,0:T(8,128)(2,1)S(1)} %get-tuple-element.177.refs_0_), channel_id=1, source_target_pairs={{0,32},{1,97},{2,34},{3,99},{4,36},{5,101},{6,38},{7,103},{8,40},{... | collective-permute-start | bytes 786440 | tf_op jit(solution)/shard_map/ppermute | solution.py:376
  86.3 7.7 %collective-permute-start.7 = (bf16[256,512]{1,0:T(8,128)(2,1)S(1)}, bf16[256,512]{1,0:T(8,128)(2,1)S(1)}, u32[]{:S(2)}, u32[]{:S(2)}) collective-permute-start(bf16[256,512]{1,0:T(8,128)(2,1)S(1)} %band_add.3.refs_2_), channel_id=1, source_target_pairs={{0,96},{1,33},{2,98},{3,35},{4,100},{5,37},{6,102},{7,39},{8,104},... | collective-permute-start | bytes 786440 | tf_op jit(solution)/shard_map/ppermute | solution.py:376
